TPU v7x, 128 devices: a whole 4x4x4 slice. The times are simulated.
128 devices in a mesh: fsdp: 16 (over z, x), head: 8 (over y, core).
Axes of the slice: x: 4, y: 4, z: 4, core: 2. Of those that a mesh axis runs over, the one named last changes fastest.
Arguments:
- grad_parts: bfloat16 [8, 2048, 8192], P('head', 'fsdp'), may hold values from -6 to 6
- params: float32 [2048, 8192], P('fsdp', 'head'), may hold values from -1 to 1
- moment_one: float32 [2048, 8192], P('fsdp', 'head'), may hold values from -3 to 3
- moment_two: float32 [2048, 8192], P('fsdp', 'head'), may hold values from 0.0001 to 0.01
- query_latent: bfloat16 [8, 128, 1536], P(None, 'fsdp'), may hold values from -6 to 6
- rope_weight: bfloat16 [1536, 4096], P(None, 'head'), may hold values from -0.15625 to 0.15625
- value_weight: bfloat16 [512, 8192], P(None, 'head'), may hold values from -0.25 to 0.25
- out_weight: bfloat16 [8192, 7168], P('head', 'fsdp'), may hold values from -0.0625 to 0.0625
- latent_cache: bfloat16 [128, 8192, 512], P('fsdp'), may hold values from -6 to 6
- rope_cache: bfloat16 [128, 64, 8192], P('fsdp'), may hold values from -6 to 6
- new_latent: bfloat16 [8, 128, 512], P(None, 'fsdp'), may hold values from -6 to 6
- new_rope: bfloat16 [8, 128, 64], P(None, 'fsdp'), may hold values from -6 to 6
- lengths: int32 [128], P('fsdp'), may hold values from 1 to 8192, as said below
Outputs:
- new_params: float32 [2048, 8192], P('fsdp', 'head')
- new_one: float32 [2048, 8192], P('fsdp', 'head')
- new_two: float32 [2048, 8192], P('fsdp', 'head')
- decoded: bfloat16 [8, 128, 7168], P(None, 'fsdp')
Inputs may be any that keep to these rules, and one draw needn't show every extreme that they name: `lengths`: some sequence has exactly 8192 filled slots.
All inputs are finite; a program needn't handle non-finite values.
Results may differ from a plain program's by a relative error of at most 0.02.
Values may be sent and summed in bfloat16 or wider, within the bound.
No kernel may reach another device: no remote copies, remote signals or barrier semaphores. Data moves between devices by JAX's collectives and lax.ppermute only.
A program may use at most 256 MiB of HBM per device.

v0:
```python
import math

import jax
import jax.numpy as jnp
from jax import lax
from jax.sharding import PartitionSpec as P

HDIM = 128
ROPE = 64


first_fix = 1.0 - math.exp(100.0 * math.log(0.9))
second_fix = 1.0 - math.exp(100.0 * math.log(0.999))


def rotate(vector, position):
    half = vector.shape[-1] // 2
    index_f = jnp.arange(half, dtype=jnp.float32)
    frequency = jnp.exp(-math.log(10000.0) * 2.0 * index_f / vector.shape[-1])
    angle = position[..., None] * frequency
    first = vector[..., :half]
    second = vector[..., half:]
    cosine = jnp.cos(angle)
    sine = jnp.sin(angle)
    return jnp.concatenate(
        [first * cosine - second * sine, first * sine + second * cosine], axis=-1
    )


def adam_update(weights, first, second, grad):
    first = 0.9 * first + 0.1 * grad
    second = 0.999 * second + 0.001 * grad * grad
    step_size = 0.003 / first_fix
    denom = jnp.sqrt(second / second_fix) + 1e-08
    return (weights - step_size * first / denom, first, second)


def attend(items):
    query_lat, query_rope, latent, rotary, new_lat, new_rot, length = items
    steps_n = query_lat.shape[0]
    scale = 1.0 / math.sqrt(HDIM + ROPE)
    score_cache = (
        jnp.einsum("thk,jk->thj", query_lat, latent, preferred_element_type=jnp.float32)
        + jnp.einsum("thr,rj->thj", query_rope, rotary, preferred_element_type=jnp.float32)
    ) * scale
    score_new = (
        jnp.einsum("thk,uk->thu", query_lat, new_lat, preferred_element_type=jnp.float32)
        + jnp.einsum("thr,ur->thu", query_rope, new_rot, preferred_element_type=jnp.float32)
    ) * scale
    mask_cache = (jnp.arange(latent.shape[0], dtype=jnp.int32) < length)[None, None, :]
    mask_new = (
        jnp.arange(steps_n, dtype=jnp.int32)[None, :]
        <= jnp.arange(steps_n, dtype=jnp.int32)[:, None]
    )[:, None, :]
    top = jnp.maximum(
        jnp.max(jnp.where(mask_cache, score_cache, -1e30), axis=-1),
        jnp.max(jnp.where(mask_new, score_new, -1e30), axis=-1),
    )
    expo_cache = jnp.where(mask_cache, jnp.exp(score_cache - top[..., None]), 0.0)
    expo_new = jnp.where(mask_new, jnp.exp(score_new - top[..., None]), 0.0)
    total = jnp.sum(expo_cache, axis=-1) + jnp.sum(expo_new, axis=-1)
    prob_cache = (expo_cache / total[..., None]).astype(jnp.bfloat16)
    prob_new = (expo_new / total[..., None]).astype(jnp.bfloat16)
    mixed = jnp.einsum(
        "thj,jk->thk", prob_cache, latent, preferred_element_type=jnp.float32
    ) + jnp.einsum("thu,uk->thk", prob_new, new_lat, preferred_element_type=jnp.float32)
    return mixed.astype(jnp.bfloat16)


def body(
    grad_parts,
    params,
    moment_one,
    moment_two,
    query_latent,
    rope_weight,
    value_weight,
    out_weight,
    latent_cache,
    rope_cache,
    new_latent,
    new_rope,
    lengths,
):
    blocks = lax.all_to_all(grad_parts, "head", split_axis=2, concat_axis=0, tiled=True)
    summed = jnp.sum(blocks.astype(jnp.float32), axis=0)
    new_params, new_one, new_two = adam_update(params, moment_one, moment_two, summed)
    owned = new_params.astype(jnp.bfloat16)
    stacked = lax.all_gather(owned, "fsdp", axis=0, tiled=True)
    q_rank = query_latent.shape[2]
    lat_rank = latent_cache.shape[2]
    steps_n = query_latent.shape[0]
    seq_local = query_latent.shape[1]
    heads_local = stacked.shape[1] // HDIM
    up_query = stacked[:q_rank]
    up_key = stacked[q_rank:].reshape(lat_rank, heads_local, HDIM)
    flat_latent = query_latent.reshape(steps_n * seq_local, q_rank)
    query_nope = jnp.dot(flat_latent, up_query, preferred_element_type=jnp.float32).astype(
        jnp.bfloat16
    )
    query_nope = query_nope.reshape(steps_n * seq_local, heads_local, HDIM)
    query_lat = jnp.einsum(
        "xhd,khd->xhk", query_nope, up_key, preferred_element_type=jnp.float32
    ).astype(jnp.bfloat16)
    query_lat = query_lat.reshape(steps_n, seq_local, heads_local, lat_rank)
    query_rope = jnp.dot(flat_latent, rope_weight, preferred_element_type=jnp.float32).reshape(
        steps_n, seq_local, heads_local, ROPE
    )
    position = (lengths[None, :] + jnp.arange(steps_n, dtype=jnp.int32)[:, None]).astype(
        jnp.float32
    )[:, :, None]
    query_rope = rotate(query_rope, position).astype(jnp.bfloat16)
    attended = lax.map(
        attend,
        (
            jnp.transpose(query_lat, (1, 0, 2, 3)),
            jnp.transpose(query_rope, (1, 0, 2, 3)),
            latent_cache,
            rope_cache,
            jnp.transpose(new_latent, (1, 0, 2)),
            jnp.transpose(new_rope, (1, 0, 2)),
            lengths,
        ),
    )
    attended = jnp.transpose(attended, (1, 0, 2, 3)).reshape(
        steps_n * seq_local, heads_local, lat_rank
    )
    values = jnp.einsum(
        "xhk,khd->xhd",
        attended,
        value_weight.reshape(lat_rank, heads_local, HDIM),
        preferred_element_type=jnp.float32,
    ).astype(jnp.bfloat16)
    values = values.reshape(steps_n * seq_local, heads_local * HDIM)
    partial_value = jnp.dot(
        values,
        lax.all_gather(out_weight, "fsdp", axis=1, tiled=True),
        preferred_element_type=jnp.float32,
    ).reshape(steps_n, seq_local, -1)
    total = lax.psum(partial_value, "head")
    return (new_params, new_one, new_two, total.astype(jnp.bfloat16))


def solution(mesh):
    return jax.shard_map(
        body,
        mesh=mesh,
        in_specs=(
            P("head", "fsdp", None),
            P("fsdp", "head"),
            P("fsdp", "head"),
            P("fsdp", "head"),
            P(None, "fsdp", None),
            P(None, "head"),
            P(None, "head"),
            P("head", "fsdp"),
            P("fsdp", None, None),
            P("fsdp", None, None),
            P(None, "fsdp", None),
            P(None, "fsdp", None),
            P("fsdp"),
        ),
        out_specs=(P("fsdp", "head"), P("fsdp", "head"), P("fsdp", "head"), P(None, "fsdp", None)),
        check_vma=False,
    )
```

profile of v0, /device:TPU:1, one launch (start us, length us, event | category | flops | bytes accessed | tf_op | source)
XLA Modules:
  0.0 375.7 jit_solution(18295202030117908744)
XLA Ops:
  7.2 9.6 %copy.44 = bf16[1,128,8192]{1,0,2:T(2,128)(2,1)} copy(bf16[1,128,8192]{2,1,0:T(8,128)(2,1)} %param.15) | data formatting | bytes 4194304 | tf_op args[0]
  17.3 45.2 %reduce.3 = bf16[8192,128]{1,0:T(8,128)(2,1)S(1)} reduce(bf16[8192,1,128]{2,1,0:T(2,128)(2,1)} %bitcast.126, bf16[]{:T(256)} %broadcast.52), dimensions={1}, to_apply=%bitcast.82.reduce_sub_computation | reduce | bytes 4194306
  65.7 32.4 %all_to_all.4 = bf16[8,2,65536]{2,1,0:T(2,128)(2,1)S(1)} all-to-all(bf16[8,2,65536]{2,1,0:T(2,128)(2,1)} %reshape.111), channel_id=1, replica_groups=mesh['fsdp'=16,'head'=8] {'head'}, dimensions={0} | all-to-all | bytes 4194304 | tf_op jit(solution)/shard_map/all_to_all | solution.py:85
  102.5 8.4 %bitcast_convert_fusion = f32[1,128,8192]{1,0,2:T(1,128)} fusion(bf16[8192,1,128]{2,1,0:T(2,128)(2,1)} %reshape.112), kind=kLoop, calls=%fused_computation.90 | loop fusion | flops 1048576 | bytes 6291456 | tf_op jit(solution)/shard_map/convert_element_type | solution.py:86
  120.2 48.5 %all-gather.3.cloned.1.call-done = bf16[2048,1024]{1,0:T(8,128)(2,1)} async-done(((bf16[128,1024]{1,0:T(8,128)(2,1)}), bf16[2048,1024]{1,0:T(8,128)(2,1)}) %all-gather.3.cloned.1.call-update) | async-done | bytes 4194320 | tf_op jit(solution)/shard_map/all_gather | solution.py:89
  173.7 132.6 %while.10 = (s32[]{:T(128)}, bf16[8,8,8,512]{3,2,0,1:T(8,128)(2,1)}, s32[8]{0:T(128)S(1)}, bf16[8,8,8,512]{3,2,1,0:T(8,128)(2,1)S(1)}, bf16[8,8192,512]{2,1,0:T(...) while((s32[]{:T(128)}, ...), condition=%wide.region_6.7_spmd, body=%wide.region_1.6_spmd.sunk | while | flops 1147811328 | bytes 28945152 | solution.py:113
  174.9 6.0 %fusion.91 = f32[8,8,8192]{2,1,0:T(8,128)S(1)} fusion(bf16[8,8192,512]{2,1,0:T(8,128)(2,1)} %get-tuple-element.200, s32[]{:T(128)S(6)} %copy.85, bf16[8,8,8,512]{3,2,1,0:T(8,128)(2,1)S(1)} %get-tuple-element.199), kind=kOutput, calls=%fused_computation.4.clone.1 | convolution fusion | flops 536870912 | bytes 10552320 | tf_op jit(solution)/shard_map/while/body/eval_jaxpr/thk,jk->thj/dot_general | solution.py:43
  184.1 5.1 %fusion.95 = f32[8,8,512]{2,1,0:T(8,128)S(1)} fusion(bf16[8,8192,512]{2,1,0:T(8,128)(2,1)} %get-tuple-element.200, s32[]{:T(128)S(6)} %copy.85, f32[8,8,8192]{2,1,0:T(8,128)S(1)} %get-tuple-element.172, f32[8,8]{1,0:T(8,128)S(1)} %add.92, f32[8,8]{1,0:T(8,128)S(1)} %max.8, pred[8192]{0:T(1024)(128)(4,1)S(1)} %iota_compare_fusion.4), kind=kOutput, calls=%fused_computation.2.clone.1 | convolution fusion | flops 538968064 | bytes 10625540 | tf_op jit(solution)/shard_map/while/body/eval_jaxpr/thj,jk->thk/dot_general | solution.py:64
  191.3 6.2 %fusion.91 = f32[8,8,8192]{2,1,0:T(8,128)S(1)} fusion(bf16[8,8192,512]{2,1,0:T(8,128)(2,1)} %get-tuple-element.200, s32[]{:T(128)S(6)} %copy.85, bf16[8,8,8,512]{3,2,1,0:T(8,128)(2,1)S(1)} %get-tuple-element.199), kind=kOutput, calls=%fused_computation.4.clone.1 | convolution fusion | flops 536870912 | bytes 10552320 | tf_op jit(solution)/shard_map/while/body/eval_jaxpr/thk,jk->thj/dot_general | solution.py:43
  200.5 5.0 %fusion.95 = f32[8,8,512]{2,1,0:T(8,128)S(1)} fusion(bf16[8,8192,512]{2,1,0:T(8,128)(2,1)} %get-tuple-element.200, s32[]{:T(128)S(6)} %copy.85, f32[8,8,8192]{2,1,0:T(8,128)S(1)} %get-tuple-element.172, f32[8,8]{1,0:T(8,128)S(1)} %add.92, f32[8,8]{1,0:T(8,128)S(1)} %max.8, pred[8192]{0:T(1024)(128)(4,1)S(1)} %iota_compare_fusion.4), kind=kOutput, calls=%fused_computation.2.clone.1 | convolution fusion | flops 538968064 | bytes 10625540 | tf_op jit(solution)/shard_map/while/body/eval_jaxpr/thj,jk->thk/dot_general | solution.py:64
  207.7 7.2 %fusion.91 = f32[8,8,8192]{2,1,0:T(8,128)S(1)} fusion(bf16[8,8192,512]{2,1,0:T(8,128)(2,1)} %get-tuple-element.200, s32[]{:T(128)S(6)} %copy.85, bf16[8,8,8,512]{3,2,1,0:T(8,128)(2,1)S(1)} %get-tuple-element.199), kind=kOutput, calls=%fused_computation.4.clone.1 | convolution fusion | flops 536870912 | bytes 10552320 | tf_op jit(solution)/shard_map/while/body/eval_jaxpr/thk,jk->thj/dot_general | solution.py:43
  218.0 5.2 %fusion.95 = f32[8,8,512]{2,1,0:T(8,128)S(1)} fusion(bf16[8,8192,512]{2,1,0:T(8,128)(2,1)} %get-tuple-element.200, s32[]{:T(128)S(6)} %copy.85, f32[8,8,8192]{2,1,0:T(8,128)S(1)} %get-tuple-element.172, f32[8,8]{1,0:T(8,128)S(1)} %add.92, f32[8,8]{1,0:T(8,128)S(1)} %max.8, pred[8192]{0:T(1024)(128)(4,1)S(1)} %iota_compare_fusion.4), kind=kOutput, calls=%fused_computation.2.clone.1 | convolution fusion | flops 538968064 | bytes 10625540 | tf_op jit(solution)/shard_map/while/body/eval_jaxpr/thj,jk->thk/dot_general | solution.py:64
  225.4 6.1 %fusion.91 = f32[8,8,8192]{2,1,0:T(8,128)S(1)} fusion(bf16[8,8192,512]{2,1,0:T(8,128)(2,1)} %get-tuple-element.200, s32[]{:T(128)S(6)} %copy.85, bf16[8,8,8,512]{3,2,1,0:T(8,128)(2,1)S(1)} %get-tuple-element.199), kind=kOutput, calls=%fused_computation.4.clone.1 | convolution fusion | flops 536870912 | bytes 10552320 | tf_op jit(solution)/shard_map/while/body/eval_jaxpr/thk,jk->thj/dot_general | solution.py:43
  234.6 5.1 %fusion.95 = f32[8,8,512]{2,1,0:T(8,128)S(1)} fusion(bf16[8,8192,512]{2,1,0:T(8,128)(2,1)} %get-tuple-element.200, s32[]{:T(128)S(6)} %copy.85, f32[8,8,8192]{2,1,0:T(8,128)S(1)} %get-tuple-element.172, f32[8,8]{1,0:T(8,128)S(1)} %add.92, f32[8,8]{1,0:T(8,128)S(1)} %max.8, pred[8192]{0:T(1024)(128)(4,1)S(1)} %iota_compare_fusion.4), kind=kOutput, calls=%fused_computation.2.clone.1 | convolution fusion | flops 538968064 | bytes 10625540 | tf_op jit(solution)/shard_map/while/body/eval_jaxpr/thj,jk->thk/dot_general | solution.py:64
  241.8 6.3 %fusion.91 = f32[8,8,8192]{2,1,0:T(8,128)S(1)} fusion(bf16[8,8192,512]{2,1,0:T(8,128)(2,1)} %get-tuple-element.200, s32[]{:T(128)S(6)} %copy.85, bf16[8,8,8,512]{3,2,1,0:T(8,128)(2,1)S(1)} %get-tuple-element.199), kind=kOutput, calls=%fused_computation.4.clone.1 | convolution fusion | flops 536870912 | bytes 10552320 | tf_op jit(solution)/shard_map/while/body/eval_jaxpr/thk,jk->thj/dot_general | solution.py:43
  251.2 5.3 %fusion.95 = f32[8,8,512]{2,1,0:T(8,128)S(1)} fusion(bf16[8,8192,512]{2,1,0:T(8,128)(2,1)} %get-tuple-element.200, s32[]{:T(128)S(6)} %copy.85, f32[8,8,8192]{2,1,0:T(8,128)S(1)} %get-tuple-element.172, f32[8,8]{1,0:T(8,128)S(1)} %add.92, f32[8,8]{1,0:T(8,128)S(1)} %max.8, pred[8192]{0:T(1024)(128)(4,1)S(1)} %iota_compare_fusion.4), kind=kOutput, calls=%fused_computation.2.clone.1 | convolution fusion | flops 538968064 | bytes 10625540 | tf_op jit(solution)/shard_map/while/body/eval_jaxpr/thj,jk->thk/dot_general | solution.py:64
  258.7 6.0 %fusion.91 = f32[8,8,8192]{2,1,0:T(8,128)S(1)} fusion(bf16[8,8192,512]{2,1,0:T(8,128)(2,1)} %get-tuple-element.200, s32[]{:T(128)S(6)} %copy.85, bf16[8,8,8,512]{3,2,1,0:T(8,128)(2,1)S(1)} %get-tuple-element.199), kind=kOutput, calls=%fused_computation.4.clone.1 | convolution fusion | flops 536870912 | bytes 10552320 | tf_op jit(solution)/shard_map/while/body/eval_jaxpr/thk,jk->thj/dot_general | solution.py:43
  267.8 5.0 %fusion.95 = f32[8,8,512]{2,1,0:T(8,128)S(1)} fusion(bf16[8,8192,512]{2,1,0:T(8,128)(2,1)} %get-tuple-element.200, s32[]{:T(128)S(6)} %copy.85, f32[8,8,8192]{2,1,0:T(8,128)S(1)} %get-tuple-element.172, f32[8,8]{1,0:T(8,128)S(1)} %add.92, f32[8,8]{1,0:T(8,128)S(1)} %max.8, pred[8192]{0:T(1024)(128)(4,1)S(1)} %iota_compare_fusion.4), kind=kOutput, calls=%fused_computation.2.clone.1 | convolution fusion | flops 538968064 | bytes 10625540 | tf_op jit(solution)/shard_map/while/body/eval_jaxpr/thj,jk->thk/dot_general | solution.py:64
  275.0 6.0 %fusion.91 = f32[8,8,8192]{2,1,0:T(8,128)S(1)} fusion(bf16[8,8192,512]{2,1,0:T(8,128)(2,1)} %get-tuple-element.200, s32[]{:T(128)S(6)} %copy.85, bf16[8,8,8,512]{3,2,1,0:T(8,128)(2,1)S(1)} %get-tuple-element.199), kind=kOutput, calls=%fused_computation.4.clone.1 | convolution fusion | flops 536870912 | bytes 10552320 | tf_op jit(solution)/shard_map/while/body/eval_jaxpr/thk,jk->thj/dot_general | solution.py:43
  284.0 5.0 %fusion.95 = f32[8,8,512]{2,1,0:T(8,128)S(1)} fusion(bf16[8,8192,512]{2,1,0:T(8,128)(2,1)} %get-tuple-element.200, s32[]{:T(128)S(6)} %copy.85, f32[8,8,8192]{2,1,0:T(8,128)S(1)} %get-tuple-element.172, f32[8,8]{1,0:T(8,128)S(1)} %add.92, f32[8,8]{1,0:T(8,128)S(1)} %max.8, pred[8192]{0:T(1024)(128)(4,1)S(1)} %iota_compare_fusion.4), kind=kOutput, calls=%fused_computation.2.clone.1 | convolution fusion | flops 538968064 | bytes 10625540 | tf_op jit(solution)/shard_map/while/body/eval_jaxpr/thj,jk->thk/dot_general | solution.py:64
  291.2 6.0 %fusion.91 = f32[8,8,8192]{2,1,0:T(8,128)S(1)} fusion(bf16[8,8192,512]{2,1,0:T(8,128)(2,1)} %get-tuple-element.200, s32[]{:T(128)S(6)} %copy.85, bf16[8,8,8,512]{3,2,1,0:T(8,128)(2,1)S(1)} %get-tuple-element.199), kind=kOutput, calls=%fused_computation.4.clone.1 | convolution fusion | flops 536870912 | bytes 10552320 | tf_op jit(solution)/shard_map/while/body/eval_jaxpr/thk,jk->thj/dot_general | solution.py:43
  300.3 5.0 %fusion.95 = f32[8,8,512]{2,1,0:T(8,128)S(1)} fusion(bf16[8,8192,512]{2,1,0:T(8,128)(2,1)} %get-tuple-element.200, s32[]{:T(128)S(6)} %copy.85, f32[8,8,8192]{2,1,0:T(8,128)S(1)} %get-tuple-element.172, f32[8,8]{1,0:T(8,128)S(1)} %add.92, f32[8,8]{1,0:T(8,128)S(1)} %max.8, pred[8192]{0:T(1024)(128)(4,1)S(1)} %iota_compare_fusion.4), kind=kOutput, calls=%fused_computation.2.clone.1 | convolution fusion | flops 538968064 | bytes 10625540 | tf_op jit(solution)/shard_map/while/body/eval_jaxpr/thj,jk->thk/dot_general | solution.py:64
  308.0 9.7 %fusion.46 = f32[8,8,7168]{2,1,0:T(8,128)S(1)} fusion(bf16[8,8,1024]{2,1,0:T(8,128)(2,1)S(1)} %dot_general.45, bf16[1024,7168]{0,1:T(8,128)(2,1)} %all-gather.5.cloned.1.call-done), kind=kOutput, calls=%fused_computation.57 | convolution fusion | flops 939524096 | bytes 16646144 | tf_op jit(solution)/shard_map/dot_general | solution.py:135
  317.7 51.2 %all-reduce.1 = bf16[8,8,7168]{2,1,0:T(8,128)(2,1)} all-reduce(f32[8,8,7168]{2,1,0:T(8,128)S(1)} %fusion.46), channel_id=1, replica_groups=mesh['fsdp'=16,'head'=8] {'head'}, use_global_device_ids=true, to_apply=%region_7.8 | all-reduce | flops 458752 | bytes 2752512 | tf_op jit(solution)/shard_map/psum | solution.py:140
  (135 shorter events, 65.1 us)
Async XLA Ops:
  7.2 299.1 %copy-start = (bf16[512,1024]{1,0:T(8,128)(2,1)S(1)}, bf16[512,1024]{1,0:T(8,128)(2,1)}, u32[]{:S(2)}) copy-start(bf16[512,1024]{1,0:T(8,128)(2,1)} %param.21) | copy-start | bytes 3145732
  7.2 161.5 %all-gather.3.cloned.1.call-start = ((), (), s32[]{:S(2)}) async-start(), calls=%async_computation.1 | async-start | bytes 4456448 | tf_op jit(solution)/shard_map/all_gather | solution.py:89
  110.9 2.7 copy-start.1
  110.9 2.7 copy-start.2
  116.2 2.5 copy-start.6
  116.2 2.8 copy-start.3
  116.2 191.7 %all-gather.5.cloned.1.call-start = ((), (), s32[]{:S(2)}) async-start(), calls=%async_computation.2 | async-start | bytes 15597568 | tf_op jit(solution)/shard_map/all_gather | solution.py:137
  118.7 1.4 copy-start.4
  118.7 1.5 copy-start.5
  168.7 1.2 slice-start
  173.0 0.7 copy-start.7
Sparse Core Ops, SparseCore 0:
  116.3 52.3 all-gather.2
  170.8 100.2 all-gather.4
where the time goes:
time: 380 us; the launch traced here: 376 us
  matrix products  132 us (35%)
  blocking collectives  83.6 us (22%)
  other arithmetic  69.7 us (18%)
  waiting for transfers between devices  49 us (13%)
  local copies, waits for them, and re-layouts  26.6 us (7%)
  between operations  14.3 us (4%)
    psum x1, blocking collectives, body(): total = lax.psum(partial_value, 'head')  51.2 us
    dot_general x8, matrix products, attend(): jnp.einsum('thk,jk->thj', query_lat, latent, preferred_element_type=jnp.f...  49.9 us
    all_gather x1, waiting for transfers between devices, body(): stacked = lax.all_gather(owned, 'fsdp', axis=0, tiled=True)  48.5 us
    unnamed x1, other arithmetic  45.2 us
    dot_general x8, matrix products, attend(): jnp.einsum('thj,jk->thk', prob_cache, latent, preferred_element_type=jnp....  40.9 us
    all_to_all x1, blocking collectives, body(): lax.all_to_all(grad_parts, 'head', split_axis=2, concat_axis=0, tiled=True)  32.4 us
    unnamed x24, local copies, waits for them, and re-layouts  19.6 us
    dot_general x8, matrix products, attend(): jnp.einsum('thr,rj->thj', query_rope, rotary, preferred_element_type=jnp....  14.9 us
  transfers between devices with their start and end apart: 2, of which 1 were waited for; matrix products, arithmetic and copies ran while one was open for 37% of the time, Pallas kernels for 0%

commit v1 on v0

v1 whole, which is shorter than its diff:
```python
import functools
import itertools
import math

import jax
import jax.numpy as jnp
import numpy as np
from jax import lax
from jax.experimental import pallas as pl
from jax.experimental.pallas import tpu as pltpu
from jax.sharding import PartitionSpec as P

HDIM = 128
ROPE = 64
SIDE = 4
BLOCK = 1024
SLOTS = 12
MIB = 1024 * 1024

first_fix = 1.0 - math.exp(100.0 * math.log(0.9))
second_fix = 1.0 - math.exp(100.0 * math.log(0.999))
NEG = -1e30
LOG2E = math.log2(math.e)

NT = (((1,), (1,)), ((), ()))
NN = (((1,), (0,)), ((), ()))


def dot(a, b, dims):
    return lax.dot_general(a, b, dims, preferred_element_type=jnp.float32)


def moves(axis, direction):
    perm = []
    for z in range(SIDE):
        for x in range(SIDE):
            for y in range(SIDE):
                for c in range(2):
                    d = direction * (1 - 2 * c)
                    to = {"x": x, "y": y, "z": z}
                    to[axis] = (to[axis] + d) % SIDE
                    perm.append(
                        (
                            (z * SIDE + x) * 2 * SIDE + y * 2 + c,
                            (to["z"] * SIDE + to["x"]) * 2 * SIDE + to["y"] * 2 + c,
                        )
                    )
    return perm


def forth(v, axis):
    return lax.ppermute(v, ("fsdp", "head"), moves(axis, 1))


def back(v, axis):
    return lax.ppermute(v, ("fsdp", "head"), moves(axis, -1))


def other_core(v):
    return lax.ppermute(v, "head", [(i, i ^ 1) for i in range(2 * SIDE)])


def ring(own, axis):
    one = forth(own, axis)
    two = back(own, axis)
    return own, one, two, forth(one, axis)


def ring_sum(blocks, axis):
    near, far = blocks[1], forth(blocks[3], axis)
    two = back(blocks[2], axis)
    one = forth((near.astype(jnp.float32) + far.astype(jnp.float32)).astype(near.dtype), axis)
    return blocks[0], one, two


VMEM = pl.BlockSpec(memory_space=pltpu.VMEM)
SMEM = pl.BlockSpec(memory_space=pltpu.SMEM)
HBM = pl.BlockSpec(memory_space=pl.ANY)
F32 = jnp.float32
BF16 = jnp.bfloat16


def pack_body(idx_ref, g_ref, o_ref, buf, in_sem, out_sem):
    cols = buf.shape[2]

    def come(j):
        at = pl.multiple_of(idx_ref[j] * cols, 128)
        return pltpu.make_async_copy(g_ref.at[:, pl.ds(at, cols)], buf.at[j], in_sem.at[j])

    def go(j):
        return pltpu.make_async_copy(buf.at[j], o_ref.at[j], out_sem.at[j])

    for j in range(SIDE):
        come(j).start()
    for j in range(SIDE):
        come(j).wait()
        go(j).start()
    for j in range(SIDE):
        go(j).wait()


def pack(idx, g):
    shape = (SIDE, g.shape[0], g.shape[1] // (2 * SIDE))
    return pl.pallas_call(
        pack_body,
        in_specs=[SMEM, HBM],
        out_specs=HBM,
        out_shape=jax.ShapeDtypeStruct(shape, g.dtype),
        scratch_shapes=[
            pltpu.VMEM(shape, g.dtype),
            pltpu.SemaphoreType.DMA((SIDE,)),
            pltpu.SemaphoreType.DMA((SIDE,)),
        ],
        name="pack_columns",
    )(idx, g)


def add_body(idx_ref, g_ref, got, o0, o1, o2, o3, buf, sem):
    cols = buf.shape[2]

    def come(j):
        at = pl.multiple_of(idx_ref[j] * cols, 128)
        return pltpu.make_async_copy(g_ref.at[:, pl.ds(at, cols)], buf.at[j], sem.at[j])

    outs = (o0, o1, o2, o3)
    for j in (3, 2, 1, 0):
        come(j).start()
    for j in (3, 2, 1, 0):
        come(j).wait()
        outs[j][...] = (buf[j].astype(F32) + got[j].astype(F32)).astype(outs[j].dtype)


def add_pairs(idx, g, got):
    shape = got.shape
    return pl.pallas_call(
        add_body,
        in_specs=[SMEM, HBM, VMEM],
        out_specs=[VMEM] * SIDE,
        out_shape=[jax.ShapeDtypeStruct(shape[1:], F32)]
        + [jax.ShapeDtypeStruct(shape[1:], BF16)] * 3,
        scratch_shapes=[pltpu.VMEM(shape, g.dtype), pltpu.SemaphoreType.DMA((SIDE,))],
        name="add_pairs",
    )(idx, g, got)


def adam_body(r0, r1, r2, p, one, two, new_p, new_one, new_two, wa, wb):
    grad = r0[...]
    for r in (r1, r2):
        grad += r[...].astype(F32)
    first = 0.9 * one[...] + 0.1 * grad
    second = 0.999 * two[...] + 0.001 * grad * grad
    step_size = 0.003 / first_fix
    denom = jnp.sqrt(second / second_fix) + 1e-08
    params = p[...] - step_size * first / denom
    new_p[...] = params
    new_one[...] = first
    new_two[...] = second
    rounded = params.astype(BF16)

    @pl.when(pl.program_id(0) == 0)
    def _():
        wa[...] = rounded

    @pl.when(pl.program_id(0) == 1)
    def _():
        wb[...] = rounded


def adam(parts, p, one, two):
    rows, cols = p.shape
    step = rows // 2
    tile = pl.BlockSpec((step, cols), lambda i: (i, 0))
    whole = pl.BlockSpec((step, cols), lambda i: (0, 0))
    full = jax.ShapeDtypeStruct((rows, cols), F32)
    half = jax.ShapeDtypeStruct((step, cols), BF16)
    return pl.pallas_call(
        adam_body,
        grid=(2,),
        in_specs=[tile] * 6,
        out_specs=[tile] * 3 + [whole] * 2,
        out_shape=[full] * 3 + [half] * 2,
        name="adam",
    )(*parts, p, one, two)


def stack_body(*refs):
    out = refs[-1]
    rows = refs[0].shape[0]
    for k, ref in enumerate(refs[:-1]):
        out[k * rows : (k + 1) * rows, :] = ref[...]


def stack_rows(blocks):
    rows, cols = blocks[0].shape
    return pl.pallas_call(
        stack_body,
        in_specs=[VMEM] * len(blocks),
        out_specs=VMEM,
        out_shape=jax.ShapeDtypeStruct((len(blocks) * rows, cols), blocks[0].dtype),
        name="stack_rows",
    )(*blocks)


def query_body(place_ref, ql_ref, *refs, seqs, steps, heads, q_rank):
    units = refs[:8]
    keep_ref, send_ref, w_buf, lat_buf, sem = refs[8:]
    z, x, sign = place_ref[0], place_ref[1], place_ref[2]
    offsets = (0, SIDE - sign, SIDE + sign, 2)
    shard = w_buf.shape[0] // (SIDE * SIDE)
    half = shard // 2
    copies = []
    for part in range(2):
        for major in range(SIDE):
            for minor in range(SIDE):
                zo, xo = (major, minor) if part == 0 else (minor, major)
                f = lax.rem(z + offsets[zo], SIDE) * SIDE + lax.rem(x + offsets[xo], SIDE)
                at = pl.multiple_of(f * shard + part * half, 64)
                copies.append(
                    pltpu.make_async_copy(
                        units[part * SIDE + major].at[pl.ds(minor * half, half), :],
                        w_buf.at[pl.ds(at, half), :],
                        sem.at[len(copies)],
                    )
                )
    for copy in copies:
        copy.start()
    for copy in copies:
        copy.wait()
    nope = dot(ql_ref[...], w_buf[:q_rank, :], NN).astype(BF16)
    for h in range(heads):
        cols = slice(h * HDIM, (h + 1) * HDIM)
        lat = dot(nope[:, cols], w_buf[q_rank:, cols], NT)
        lat_buf[:, h * steps : (h + 1) * steps, :] = lat.reshape(seqs, steps, -1)
    keep_ref[...] = lat_buf[: seqs // 2].astype(BF16)
    send_ref[...] = lat_buf[seqs // 2 :].astype(BF16)


def queries(place, ql, units, w_rows, seqs, q_rank):
    cols = units[0].shape[1]
    heads = cols // HDIM
    steps = ql.shape[0] // seqs
    lat_rank = w_rows - q_rank
    out = jax.ShapeDtypeStruct((seqs // 2, heads * steps, lat_rank), BF16)
    return pl.pallas_call(
        functools.partial(query_body, seqs=seqs, steps=steps, heads=heads, q_rank=q_rank),
        in_specs=[SMEM, VMEM] + [HBM] * 8,
        out_specs=[VMEM] * 2,
        out_shape=[out] * 2,
        scratch_shapes=[
            pltpu.VMEM((w_rows, cols), BF16),
            pltpu.VMEM((seqs, heads * steps, lat_rank), F32),
            pltpu.SemaphoreType.DMA((32,)),
        ],
        compiler_params=pltpu.CompilerParams(vmem_limit_bytes=24 * MIB),
        name="queries",
    )(place, ql, *units)


def attention_body(
    order_ref,
    len_ref,
    q_own,
    q_got,
    r_own,
    r_got,
    nl_ref,
    nr_ref,
    lat_hbm,
    rope_hbm,
    keep_ref,
    send_ref,
    lat_buf,
    rope_buf,
    q_buf,
    qr_buf,
    acc,
    m_ref,
    l_ref,
    p0,
    p1,
    a0,
    a1,
    seq_of,
    blk_of,
    lat_sem,
    rope_sem,
    *,
    steps,
):
    seqs, rows, _ = q_buf.shape
    part = rows // 2
    factor = LOG2E / math.sqrt(HDIM + ROPE)

    def listing(s, at):
        blocks = lax.div(len_ref[s] + (BLOCK - 1), BLOCK)

        def put(j, at):
            seq_of[at] = s
            blk_of[at] = j
            return at + 1

        return lax.fori_loop(0, blocks, put, at)

    count = lax.fori_loop(0, seqs, listing, 0)

    def lat_copy(i):
        slot = lax.rem(i, SLOTS)
        start = pl.multiple_of(blk_of[i] * BLOCK, BLOCK)
        return pltpu.make_async_copy(
            lat_hbm.at[order_ref[seq_of[i]], pl.ds(start, BLOCK), :],
            lat_buf.at[slot],
            lat_sem.at[slot],
        )

    def rope_copy(i):
        slot = lax.rem(i, SLOTS)
        start = pl.multiple_of(blk_of[i] * BLOCK, BLOCK)
        return pltpu.make_async_copy(
            rope_hbm.at[order_ref[seq_of[i]], :, pl.ds(start, BLOCK)],
            rope_buf.at[slot],
            rope_sem.at[slot],
        )

    def fetch(i):
        @pl.when(i < count)
        def _():
            lat_copy(i).start()
            rope_copy(i).start()

    for i in range(SLOTS - 1):
        fetch(i)

    q_buf[:, :part, :] = q_own[...]
    q_buf[:, part:, :] = q_got[...]
    qr_buf[:, :part, :] = r_own[...]
    qr_buf[:, part:, :] = r_got[...]

    width = nl_ref.shape[1]
    token = lax.broadcasted_iota(jnp.int32, (rows, width), 1)
    step = lax.rem(lax.broadcasted_iota(jnp.int32, (rows, width), 0), steps)
    seen = token <= step
    for s in range(seqs):
        score = dot(q_buf[s], nl_ref[s], NT) + dot(qr_buf[s], nr_ref[s], NT)
        score = jnp.where(seen, score, NEG)
        top = jnp.max(score, axis=1, keepdims=True)
        prob = jnp.exp2((score - top) * factor)
        m_ref[s] = jnp.broadcast_to(top, (rows, 128))
        l_ref[s] = prob
        acc[s] = dot(prob.astype(BF16), nl_ref[s], NN)

    lane = lax.broadcasted_iota(jnp.int32, (rows, BLOCK), 1)

    def scores(i, p_ref, a_ref):
        slot = lax.rem(i, SLOTS)
        s = seq_of[i]
        lat_copy(i).wait()
        rope_copy(i).wait()
        score = dot(q_buf[s], lat_buf[slot], NT) + dot(qr_buf[s], rope_buf[slot], NN)
        score = jnp.where(lane < len_ref[s] - blk_of[i] * BLOCK, score, NEG)
        before = m_ref[s]
        top = jnp.maximum(before, jnp.max(score, axis=1, keepdims=True))
        prob = jnp.exp2((score - top[:, :1]) * factor)
        alpha = jnp.exp2((before - top) * factor)
        total = l_ref[s] * alpha
        for k in range(BLOCK // 128):
            total += prob[:, k * 128 : (k + 1) * 128]
        m_ref[s] = top
        l_ref[s] = total
        a_ref[...] = alpha
        p_ref[...] = prob.astype(BF16)

    def gather(i, p_ref, a_ref):
        slot = lax.rem(i, SLOTS)
        s = seq_of[i]
        acc[s] = acc[s] * a_ref[:, :1] + dot(p_ref[...], lat_buf[slot], NN)

    scores(0, p0, a0)

    def pair(k, carry):
        i = 2 * k
        fetch(i + SLOTS - 1)
        gather(i, p0, a0)
        scores(i + 1, p1, a1)
        fetch(i + SLOTS)
        gather(i + 1, p1, a1)
        scores(i + 2, p0, a0)
        return carry

    pairs = lax.div(count - 1, 2)
    lax.fori_loop(0, pairs, pair, 0)

    @pl.when(2 * pairs + 1 < count)
    def _():
        fetch(2 * pairs + SLOTS - 1)
        gather(2 * pairs, p0, a0)
        scores(2 * pairs + 1, p1, a1)
        gather(2 * pairs + 1, p1, a1)

    @pl.when(2 * pairs + 1 >= count)
    def _():
        gather(2 * pairs, p0, a0)

    for s in range(seqs):
        mixed = (acc[s] / jnp.sum(l_ref[s], axis=1, keepdims=True)).astype(BF16)
        keep_ref[s] = mixed[:part]
        send_ref[s] = mixed[part:]


def attention(order, lengths, q_own, q_got, r_own, r_got, nl, nr, lat, rope, steps):
    seqs, part, lat_rank = q_own.shape
    rows = 2 * part
    most = seqs * (lat.shape[1] // BLOCK) + 1
    out = jax.ShapeDtypeStruct(q_own.shape, BF16)
    return pl.pallas_call(
        functools.partial(attention_body, steps=steps),
        in_specs=[SMEM, SMEM] + [VMEM] * 6 + [HBM] * 2,
        out_specs=[VMEM] * 2,
        out_shape=[out] * 2,
        scratch_shapes=[
            pltpu.VMEM((SLOTS, BLOCK, lat_rank), BF16),
            pltpu.VMEM((SLOTS, ROPE, BLOCK), BF16),
            pltpu.VMEM((seqs, rows, lat_rank), BF16),
            pltpu.VMEM((seqs, rows, ROPE), BF16),
            pltpu.VMEM((seqs, rows, lat_rank), F32),
            pltpu.VMEM((seqs, rows, 128), F32),
            pltpu.VMEM((seqs, rows, 128), F32),
            pltpu.VMEM((rows, BLOCK), BF16),
            pltpu.VMEM((rows, BLOCK), BF16),
            pltpu.VMEM((rows, 128), F32),
            pltpu.VMEM((rows, 128), F32),
            pltpu.SMEM((most,), jnp.int32),
            pltpu.SMEM((most,), jnp.int32),
            pltpu.SemaphoreType.DMA((SLOTS,)),
            pltpu.SemaphoreType.DMA((SLOTS,)),
        ],
        compiler_params=pltpu.CompilerParams(vmem_limit_bytes=40 * MIB),
        name="attention",
    )(order, lengths, q_own, q_got, r_own, r_got, nl, nr, lat, rope)


def values_body(order_ref, step_ref, own, got, vw_ref, out_ref, mixed, flat):
    half, rows, lat_rank = own.shape
    seqs = 2 * half
    heads = vw_ref.shape[1] // HDIM
    steps = rows // heads
    mixed[:half] = own[...].astype(F32)
    mixed[half:] = got[...].astype(F32)
    for h in range(heads):
        cols = slice(h * HDIM, (h + 1) * HDIM)
        part = mixed[:, h * steps : (h + 1) * steps, :].reshape(seqs * steps, lat_rank)
        flat[:, cols] = dot(part.astype(BF16), vw_ref[:, cols], NN).astype(BF16)
    count = seqs * steps
    row = lax.broadcasted_iota(jnp.int32, (count, count), 0)
    col = lax.broadcasted_iota(jnp.int32, (count, count), 1)
    want_step = jnp.zeros((count, count), jnp.int32)
    want_seq = jnp.zeros((count, count), jnp.int32)
    for k in range(steps):
        want_step = jnp.where(lax.div(row, seqs) == k, step_ref[k], want_step)
    for k in range(seqs):
        want_seq = jnp.where(lax.div(col, steps) == k, order_ref[k], want_seq)
    same = (want_step == lax.rem(col, steps)) & (want_seq == lax.rem(row, seqs))
    pick = jnp.where(same, 1.0, 0.0).astype(BF16)
    out_ref[...] = dot(pick, flat[...], NN).astype(BF16)


def project_values(order, step_order, own, got, vw):
    half, rows, lat_rank = own.shape
    cols = vw.shape[1]
    count = 2 * half * rows * HDIM // cols
    return pl.pallas_call(
        values_body,
        in_specs=[SMEM, SMEM] + [VMEM] * 3,
        out_specs=VMEM,
        out_shape=jax.ShapeDtypeStruct((count, cols), BF16),
        scratch_shapes=[
            pltpu.VMEM((2 * half, rows, lat_rank), F32),
            pltpu.VMEM((count, cols), BF16),
        ],
        compiler_params=pltpu.CompilerParams(vmem_limit_bytes=24 * MIB),
        name="project_values",
    )(order, step_order, own, got, vw)


def output_body(place_ref, *refs, seqs):
    tokens, weights = refs[:4], refs[4:8]
    send_ref, keep_ref, v_buf, w_buf, v_sem, w_sem = refs[8:]
    x, sign = place_ref[1], place_ref[2]
    offsets = (0, SIDE - sign, SIDE + sign, 2)
    depth = v_buf.shape[2]
    part = weights[0].shape[0]
    copies = []
    for k in range(SIDE):
        to = lax.rem(offsets[k], SIDE) if k else 0
        copies.append(pltpu.make_async_copy(tokens[k], v_buf.at[to], v_sem.at[k]))
    for k in range(SIDE):
        at = pl.multiple_of(lax.rem(x + offsets[k], SIDE) * part, 64)
        copies.append(
            pltpu.make_async_copy(weights[k], w_buf.at[pl.ds(at, part), :], w_sem.at[k])
        )
    for copy in copies:
        copy.start()
    for copy in copies:
        copy.wait()
    tokens_all = v_buf[...].reshape(-1, depth)
    width = 256
    for n in range(w_buf.shape[0] // width):
        cols = slice(n * width, (n + 1) * width)
        res = dot(tokens_all, w_buf[cols, :], NT).reshape(SIDE, 2 * SIDE, seqs, width)
        for b in range(SIDE):
            for z in range(SIDE):
                send_ref[b, z, :, cols] = res[z, b].astype(BF16)
                keep_ref[b, z, :, cols] = res[z, SIDE + b].astype(BF16)


def output_blocks(place, tokens, weights, seqs):
    count, depth = tokens[0].shape
    cols = SIDE * weights[0].shape[0]
    out = jax.ShapeDtypeStruct((SIDE, SIDE, seqs, cols), BF16)
    return pl.pallas_call(
        functools.partial(output_body, seqs=seqs),
        in_specs=[SMEM] + [HBM] * 8,
        out_specs=[VMEM] * 2,
        out_shape=[out] * 2,
        scratch_shapes=[
            pltpu.VMEM((SIDE, count, depth), BF16),
            pltpu.VMEM((cols, depth), BF16),
            pltpu.SemaphoreType.DMA((SIDE,)),
            pltpu.SemaphoreType.DMA((SIDE,)),
        ],
        compiler_params=pltpu.CompilerParams(vmem_limit_bytes=24 * MIB),
        name="output_blocks",
    )(place, *tokens, *weights)


def join_body(a, b, o0, o1, o2, o3):
    for j, o in enumerate((o0, o1, o2, o3)):
        o[...] = (a[j].astype(F32) + b[j].astype(F32)).astype(o.dtype)


def join_pairs(a, b):
    out = jax.ShapeDtypeStruct(a.shape[1:], BF16)
    return pl.pallas_call(
        join_body,
        in_specs=[VMEM] * 2,
        out_specs=[VMEM] * SIDE,
        out_shape=[out] * SIDE,
        name="join_pairs",
    )(a, b)


def total_body(a, b, c, o0, o1, o2, o3):
    for j, o in enumerate((o0, o1, o2, o3)):
        o[...] = (a[j].astype(F32) + b[j].astype(F32) + c[j].astype(F32)).astype(o.dtype)


def total_blocks(parts):
    out = jax.ShapeDtypeStruct(parts[0].shape[1:], BF16)
    return pl.pallas_call(
        total_body,
        in_specs=[VMEM] * 3,
        out_specs=[VMEM] * SIDE,
        out_shape=[out] * SIDE,
        name="total_blocks",
    )(*parts)


def columns_body(at_ref, *refs):
    out = refs[-1]
    width = refs[0].shape[1]
    for k, ref in enumerate(refs[:-1]):
        out[:, pl.ds(pl.multiple_of(at_ref[k] * width, 128), width)] = ref[...]


def join_columns(at, blocks):
    rows, width = blocks[0].shape
    return pl.pallas_call(
        columns_body,
        in_specs=[SMEM] + [VMEM] * SIDE,
        out_specs=VMEM,
        out_shape=jax.ShapeDtypeStruct((rows, SIDE * width), BF16),
        name="join_columns",
    )(at, *blocks)


def settle_body(idx_ref, *refs):
    out = refs[-1]
    for k, ref in enumerate(refs[:-1]):
        out[idx_ref[k]] = ref[...]


def settle(idx, blocks):
    return pl.pallas_call(
        settle_body,
        in_specs=[SMEM] + [VMEM] * 8,
        out_specs=VMEM,
        out_shape=jax.ShapeDtypeStruct((8,) + blocks[0].shape, BF16),
        name="settle",
    )(idx, *blocks)


def splits(seqs):
    table = []
    for rest in itertools.combinations(range(1, seqs), seqs // 2 - 1):
        mine = (0,) + rest
        table.append(mine + tuple(s for s in range(seqs) if s not in mine))
    return np.array(table, np.int32)


def balanced_order(lengths):
    seqs = lengths.shape[0]
    table = splits(seqs)
    member = np.zeros((table.shape[0], seqs), np.int32)
    for i, row in enumerate(table):
        member[i, row[: seqs // 2]] = 1
    blocks = lax.div(lengths + (BLOCK - 1), BLOCK)
    first = jnp.sum(member * blocks[None, :], axis=1)
    larger = jnp.maximum(first, jnp.sum(blocks) - first)
    index = np.arange(table.shape[0], dtype=np.int32)
    score = larger * table.shape[0] + index
    chosen = (score == jnp.min(score)).astype(jnp.int32)
    return jnp.sum(chosen[:, None] * table, axis=0)


def rotate(vector, position):
    half = vector.shape[-1] // 2
    index_f = jnp.arange(half, dtype=jnp.float32)
    frequency = jnp.exp(-math.log(10000.0) * 2.0 * index_f / vector.shape[-1])
    angle = position[..., None] * frequency
    first = vector[..., :half]
    second = vector[..., half:]
    cosine = jnp.cos(angle)
    sine = jnp.sin(angle)
    return jnp.concatenate(
        [first * cosine - second * sine, first * sine + second * cosine], axis=-1
    )


def body(
    grad_parts,
    params,
    moment_one,
    moment_two,
    query_latent,
    rope_weight,
    value_weight,
    out_weight,
    latent_cache,
    rope_cache,
    new_latent,
    new_rope,
    lengths,
):
    head = lax.axis_index("head")
    y, core = lax.div(head, 2), lax.rem(head, 2)
    fsdp = lax.axis_index("fsdp")
    z, x = lax.div(fsdp, SIDE), lax.rem(fsdp, SIDE)
    sign = 1 - 2 * core
    place = jnp.stack([z, x, sign])

    def turned(base, s):
        return lax.rem(jnp.stack([base, base + SIDE + s, base + SIDE - s, base + 2]), SIDE)

    send_idx = 2 * turned(y, -sign) + (1 - core)
    keep_idx = 2 * turned(y, sign) + core

    grad = grad_parts[0]
    got = other_core(pack(send_idx, grad))
    parts = ring_sum(add_pairs(keep_idx, grad, got), "y")
    new_params, new_one, new_two, w_a, w_b = adam(parts, params, moment_one, moment_two)

    w_t = out_weight.T
    w_one, w_two = forth(w_t, "x"), back(w_t, "x")
    w_one, w_a, w_b = lax.optimization_barrier((w_one, w_a, w_b))

    units = []
    for piece, first, then in ((w_a, "x", "z"), (w_b, "z", "x")):
        units += list(ring(stack_rows(ring(piece, first)), then))
    out_weights = (w_t, w_one, w_two, forth(w_one, "x"))

    steps_n, seq_local, q_rank = query_latent.shape
    heads_local = value_weight.shape[1] // HDIM
    half = seq_local // 2
    order = balanced_order(lengths)
    order = jnp.where(core == 0, order, jnp.concatenate([order[half:], order[:half]]))
    chosen = order[:, None] == jnp.arange(seq_local, dtype=jnp.int32)[None, :]
    lengths_in = jnp.sum(jnp.where(chosen, lengths[None, :], 0), axis=1)
    chosen = chosen.astype(BF16)

    def arrange(which, arrays):
        return jnp.einsum("ps,tsq->ptq", which, arrays, preferred_element_type=F32).astype(BF16)

    by_seq = arrange(chosen, query_latent).reshape(seq_local * steps_n, q_rank)
    query_rope = jnp.dot(by_seq, rope_weight, preferred_element_type=F32).reshape(
        seq_local, steps_n, heads_local, ROPE
    )
    position = (lengths_in[:, None] + jnp.arange(steps_n, dtype=jnp.int32)[None, :]).astype(F32)[
        :, :, None
    ]
    query_rope = rotate(query_rope, position).astype(BF16)
    query_rope = jnp.transpose(query_rope, (0, 2, 1, 3)).reshape(
        seq_local, heads_local * steps_n, ROPE
    )
    r_own, r_got = query_rope[:half], other_core(query_rope[half:])
    pad = ((0, 0), (0, 128 - steps_n), (0, 0))
    nl = jnp.pad(arrange(chosen[:half], new_latent), pad)
    nr = jnp.pad(arrange(chosen[:half], new_rope), pad)

    w_rows = SIDE * SIDE * params.shape[0]
    q_own, q_send = queries(place, by_seq, units, w_rows, seq_local, q_rank)
    mixed, mixed_send = attention(
        order,
        lengths_in[:half],
        q_own,
        other_core(q_send),
        r_own,
        r_got,
        nl,
        nr,
        latent_cache,
        rope_cache,
        steps_n,
    )
    step_order = jnp.concatenate([send_idx, keep_idx])
    values = project_values(order, step_order, mixed, other_core(mixed_send), value_weight)

    send, keep = output_blocks(place, ring(values, "z"), out_weights, seq_local)
    parts = ring_sum(join_pairs(keep, other_core(send)), "y")
    blocks = total_blocks(parts)

    arrived = [blocks[0]]
    for d in range(1, SIDE):
        perm = [
            (zz * SIDE + xx, ((zz + d) % SIDE) * SIDE + xx)
            for zz in range(SIDE)
            for xx in range(SIDE)
        ]
        arrived.append(lax.ppermute(blocks[d], "fsdp", perm))
    back_z = lax.rem(z + SIDE - jnp.arange(SIDE, dtype=jnp.int32), SIDE)
    mine = join_columns(back_z, arrived)

    column = list(ring(mine, "y"))
    column += [other_core(b) for b in column]
    from_own = 2 * turned(y, -sign) + core
    from_other = 2 * turned(y, sign) + (1 - core)
    decoded = settle(jnp.concatenate([from_own, from_other]), column)
    return (new_params, new_one, new_two, decoded)


def solution(mesh):
    return jax.shard_map(
        body,
        mesh=mesh,
        in_specs=(
            P("head", "fsdp", None),
            P("fsdp", "head"),
            P("fsdp", "head"),
            P("fsdp", "head"),
            P(None, "fsdp", None),
            P(None, "head"),
            P(None, "head"),
            P("head", "fsdp"),
            P("fsdp", None, None),
            P("fsdp", None, None),
            P(None, "fsdp", None),
            P(None, "fsdp", None),
            P("fsdp"),
        ),
        out_specs=(P("fsdp", "head"), P("fsdp", "head"), P("fsdp", "head"), P(None, "fsdp", None)),
        check_vma=False,
    )
```

time: 380 us -> 190 us (0.50)
  matrix products: 132 us -> 3.49 us
  blocking collectives: 83.6 us -> 0 us
  starting transfers between devices: 0.26 us -> 75 us
  other arithmetic: 69.7 us -> 11.6 us
  Pallas kernels: 0 us -> 54.3 us
  waiting for transfers between devices: 49 us -> 31.1 us
  local copies, waits for them, and re-layouts: 26.6 us -> 11.4 us
  between operations: 14.3 us -> 1.04 us
    dot_general x53 -> x4, matrix products: 132 us -> 3.49 us  [the longest x1 2.98 us: body(): jnp.dot(by_seq, rope_weight, preferred_element_type=F32)]
    ppermute x0 -> x39, starting transfers between devices: none -> 75 us  [the longest x18 42.5 us: forth(): return lax.ppermute(v, ('fsdp', 'head'), moves(axis, 1))]
    pallas_call x0 -> x13, Pallas kernels: none -> 54.3 us  [the longest x1 21.9 us: attention(): pl.pallas_call(functools.partial(attention_body, steps=steps), in_specs=[...]
    psum x1 -> x0, blocking collectives: 51.2 us -> none  [body(): total = lax.psum(partial_value, 'head')]
    all_gather x2 -> x0, waiting for transfers between devices: 48.5 us -> none  [the longest x1 48.5 us: body(): stacked = lax.all_gather(owned, 'fsdp', axis=0, tiled=True)]
    unnamed x1 -> x0, other arithmetic: 45.2 us -> none
    all_to_all x1 -> x0, blocking collectives: 32.4 us -> none  [body(): lax.all_to_all(grad_parts, 'head', split_axis=2, concat_axis=0, tiled=True)]
    ppermute x0 -> x39, waiting for transfers between devices: none -> 31.1 us  [the longest x18 23 us: forth(): return lax.ppermute(v, ('fsdp', 'head'), moves(axis, 1))]
  transfers between devices with their start and end apart: 2 -> 39, of which waited for: 1 -> 19; matrix products, arithmetic and copies ran while one was open for 37% -> 9% of each run, Pallas kernels for 0% -> 22%
where the time goes in v1:
time: 190 us; the launch traced here: 188 us
  starting transfers between devices  75 us (39%)
  Pallas kernels  54.3 us (29%)
  waiting for transfers between devices  31.1 us (16%)
  other arithmetic  11.6 us (6%)
  local copies, waits for them, and re-layouts  11.4 us (6%)
  matrix products  3.49 us (2%)
    ppermute x18, starting transfers between devices, forth(): return lax.ppermute(v, ('fsdp', 'head'), moves(axis, 1))  42.5 us
    ppermute x9, starting transfers between devices, other_core(): return lax.ppermute(v, 'head', [(i, i ^ 1) for i in range(2 * SIDE)])  23.1 us
    ppermute x18, waiting for transfers between devices, forth(): return lax.ppermute(v, ('fsdp', 'head'), moves(axis, 1))  23 us
    pallas_call x1, Pallas kernels, attention(): pl.pallas_call(functools.partial(attention_body, steps=steps), in_specs=[...  21.9 us
    unnamed x69, local copies, waits for them, and re-layouts  10.5 us
    pallas_call x1, Pallas kernels, queries(): pl.pallas_call(functools.partial(query_body, seqs=seqs, steps=steps, head...  7.55 us
    ppermute x9, starting transfers between devices, back(): return lax.ppermute(v, ('fsdp', 'head'), moves(axis, -1))  5.95 us
    pallas_call x2, Pallas kernels, stack_rows(): pl.pallas_call(stack_body, in_specs=[VMEM] * len(blocks), out_specs=VMEM,...  3.84 us
  transfers between devices with their start and end apart: 39, of which 19 were waited for; matrix products, arithmetic and copies ran while one was open for 9% of the time, Pallas kernels for 22%

profile of v1, /device:TPU:1, one launch (start us, length us, event | category | flops | bytes accessed | tf_op | source)
XLA Modules:
  0.0 187.9 jit_solution(4747854106425668719)
XLA Ops:
  1.8 2.8 %pack_columns.1 = bf16[4,128,1024]{2,1,0:T(8,128)(2,1)} custom-call(s32[4]{0:T(128)} %broadcast_add_fusion.1.idx_ref, bf16[128,8192]{1,0:T(8,128)(2,1)} %bitcast.44), custom_call_target="tpu_custom_call" | custom-call | tf_op jit(solution)/shard_map/pack_columns/pallas_call | solution.py:104
  13.2 3.5 %add_pairs.1 = (f32[128,1024]{1,0:T(8,128)}, bf16[128,1024]{1,0:T(8,128)(2,1)}, bf16[128,1024]{1,0:T(8,128)(2,1)}, bf16[128,1024]{1,0:T(8,128)(2,1)}) custom-call(s32[4]{0:T(128)} %broadcast_add_fusion.3.idx_ref, bf16[128,8192]{1,0:T(8,128)(2,1)} %bitcast.45, bf16[4,128,1024]{2,1,0:T(8,128)(2,1)} %collective-permute-done.got), custom_call_target="tpu_custom_call" | custom-call | tf_op jit(solution)/shard_map/add_pairs/pallas_call | solution.py:135
  16.7 2.8 %collective-permute-start.1 = (bf16[128,1024]{1,0:T(8,128)(2,1)}, bf16[128,1024]{1,0:T(8,128)(2,1)}, u32[]{:S(2)}, u32[]{:S(2)}) collective-permute-start(bf16[128,1024]{1,0:T(8,128)(2,1)} %get-tuple-element.32), channel_id=1, source_target_pairs={{0,2},{1,7},{2,4},{3,1},{4,6},{5,3},{6,0},{7,5},{8,10},{9,15},{10,... | collective-permute-start | bytes 786440 | tf_op jit(solution)/shard_map/ppermute | solution.py:52
  19.7 4.5 %collective-permute-done.1 = bf16[128,1024]{1,0:T(8,128)(2,1)} collective-permute-done((bf16[128,1024]{1,0:T(8,128)(2,1)}, bf16[128,1024]{1,0:T(8,128)(2,1)}, u32[]{:S(2)}, u32[]{:S(2)}) %collective-permute-start.1) | collective-permute-done | bytes 262176 | tf_op jit(solution)/shard_map/ppermute | solution.py:52
  26.0 3.3 %collective-permute-start.2 = (bf16[128,1024]{1,0:T(8,128)(2,1)}, bf16[128,1024]{1,0:T(8,128)(2,1)}, u32[]{:S(2)}, u32[]{:S(2)}) collective-permute-start(bf16[128,1024]{1,0:T(8,128)(2,1)} %add_convert_fusion), channel_id=1, source_target_pairs={{0,2},{1,7},{2,4},{3,1},{4,6},{5,3},{6,0},{7,5},{8,10},{9,15},{10,... | collective-permute-start | bytes 786440 | tf_op jit(solution)/shard_map/ppermute | solution.py:52
  33.0 3.0 %adam.1 = (f32[128,1024]{1,0:T(8,128)}, f32[128,1024]{1,0:T(8,128)}, f32[128,1024]{1,0:T(8,128)}, bf16[64,1024]{1,0:T(8,128)(2,1)}, bf16[64,1024]{1,0:T(8,128)(2,1)}) custom-call(f32[128,1024]{1,0:T(8,128)} %get-tuple-element.30.r0, bf16[128,1024]{1,0:T(8,128)(2,1)} %collective-permute-done.2.r1, bf16[128,1024]{1,0:T(8,128)(2,1)} %copy-done.9, ...), custom_call_target="tpu_custom_call" | custom-call | tf_op jit(solution)/shard_map/adam/pallas_call | solution.py:176
  36.0 4.1 %collective-permute-start.5 = (bf16[64,1024]{1,0:T(8,128)(2,1)}, bf16[64,1024]{1,0:T(8,128)(2,1)S(1)}, u32[]{:S(2)}, u32[]{:S(2)}) collective-permute-start(bf16[64,1024]{1,0:T(8,128)(2,1)} %get-tuple-element.39.refs_0_), channel_id=1, source_target_pairs={{0,8},{1,25},{2,10},{3,27},{4,12},{5,29},{6,14},{7,31},{8,16},{9,1... | collective-permute-start | bytes 393224 | tf_op jit(solution)/shard_map/ppermute | solution.py:52
  40.1 3.8 %collective-permute-start.11 = (bf16[64,1024]{1,0:T(8,128)(2,1)}, bf16[64,1024]{1,0:T(8,128)(2,1)}, u32[]{:S(2)}, u32[]{:S(2)}) collective-permute-start(bf16[64,1024]{1,0:T(8,128)(2,1)} %get-tuple-element.40.refs_0_), channel_id=1, source_target_pairs={{0,32},{1,97},{2,34},{3,99},{4,36},{5,101},{6,38},{7,103},{8,40},{... | collective-permute-start | bytes 393224 | tf_op jit(solution)/shard_map/ppermute | solution.py:52
  43.8 3.0 %fusion = f32[8,8,8,64]{3,1,2,0:T(8,128)} fusion(bf16[8,64,1536,1]{2,1,0,3:T(8,128)(2,1)} %bitcast.46, bf16[8,8,1536,1]{2,0,1,3:T(8,128)(2,1)S(1)} %bitcast.47), kind=kOutput, calls=%fused_computation.5 | convolution fusion | flops 100663296 | bytes 1900544 | tf_op jit(solution)/shard_map/dot_general | solution.py:693
  47.2 2.6 %collective-permute-start.7 = (bf16[64,1024]{1,0:T(8,128)(2,1)S(1)}, bf16[64,1024]{1,0:T(8,128)(2,1)}, u32[]{:S(2)}, u32[]{:S(2)}) collective-permute-start(bf16[64,1024]{1,0:T(8,128)(2,1)S(1)} %collective-permute-done.5.refs_1_), channel_id=1, source_target_pairs={{0,8},{1,25},{2,10},{3,27},{4,12},{5,29},{6,14},{7,31},{8,16},{9,1... | collective-permute-start | bytes 393224 | tf_op jit(solution)/shard_map/ppermute | solution.py:52
  58.2 3.2 %collective-permute-start.14 = (bf16[256,1024]{1,0:T(8,128)(2,1)}, bf16[256,1024]{1,0:T(8,128)(2,1)S(1)}, u32[]{:S(2)}, u32[]{:S(2)}) collective-permute-start(bf16[256,1024]{1,0:T(8,128)(2,1)} %stack_rows.3.refs_4_), channel_id=1, source_target_pairs={{0,8},{1,25},{2,10},{3,27},{4,12},{5,29},{6,14},{7,31},{8,16},{9,1... | collective-permute-start | bytes 1572872 | tf_op jit(solution)/shard_map/ppermute | solution.py:52
  67.9 3.0 %collective-permute-start.16 = (bf16[256,1024]{1,0:T(8,128)(2,1)S(1)}, bf16[256,1024]{1,0:T(8,128)(2,1)S(1)}, u32[]{:S(2)}, u32[]{:S(2)}) collective-permute-start(bf16[256,1024]{1,0:T(8,128)(2,1)S(1)} %collective-permute-done.14.refs_5_), channel_id=1, source_target_pairs={{0,8},{1,25},{2,10},{3,27},{4,12},{5,29},{6,14},{7,31},{8,16},{9,1... | collective-permute-start | bytes 1572872 | tf_op jit(solution)/shard_map/ppermute | solution.py:52
  80.2 7.5 %queries.1 = (bf16[4,64,512]{2,1,0:T(8,128)(2,1)S(1)}, bf16[4,64,512]{2,1,0:T(8,128)(2,1)S(1)}) custom-call(s32[3]{0:T(128)S(1)} %pad_add_fusion.1.place_ref, bf16[64,1536]{1,0:T(8,128)(2,1)S(1)} %bitcast.42, bf16[256,1024]{1,0:T(8,128)(2,1)S(1)} %copy-done.2, bf16[256,1024]{1,0:T(8,128)(2,1)} %collective-permute-done.8.refs_1_, ...), custom_call_target="tpu_custom_call" | custom-call | tf_op jit(solution)/shard_map/queries/pallas_call | solution.py:244
  87.8 4.0 %collective-permute-start.17 = (bf16[4,64,512]{2,1,0:T(8,128)(2,1)S(1)}, bf16[4,64,512]{2,1,0:T(8,128)(2,1)S(1)}, u32[]{:S(2)}, u32[]{:S(2)}) collective-permute-start(bf16[4,64,512]{2,1,0:T(8,128)(2,1)S(1)} %get-tuple-element.42), channel_id=1, source_target_pairs={{0,1},{1,0},{2,3},{3,2},{4,5},{5,4},{6,7},{7,6},{8,9},{9,8},{10,11... | collective-permute-start | bytes 786440 | tf_op jit(solution)/shard_map/ppermute | solution.py:60
  92.9 3.4 %copy-done.1 = bf16[8,64,8192]{2,1,0:T(8,128)(2,1)S(1)} copy-done((bf16[8,64,8192]{2,1,0:T(8,128)(2,1)S(1)}, bf16[8,64,8192]{2,1,0:T(8,128)(2,1)}, u32[]{:S(2)}) %copy-start.1) | copy-done | bytes 8388632
  96.3 21.9 %attention.1 = (bf16[4,64,512]{2,1,0:T(8,128)(2,1)S(1)}, bf16[4,64,512]{2,1,0:T(8,128)(2,1)S(1)}) custom-call(s32[8]{0:T(128)S(1)} %broadcast_select_fusion.order_ref, s32[4]{0:T(128)S(1)} %bitcast.43, bf16[4,64,512]{2,1,0:T(8,128)(2,1)S(1)} %get-tuple-element.41.q_own, bf16[4,64,512]{2,1,0:T(8,128)(2,1)S(1)} %collective-permute-done.17.q_got, ...), custom_call_target="tpu_custom_call" | custom-call | tf_op jit(solution)/shard_map/attention/pallas_call | solution.py:414
  123.1 4.6 %collective-permute-start.21 = (bf16[64,1024]{1,0:T(8,128)(2,1)S(1)}, bf16[64,1024]{1,0:T(8,128)(2,1)S(1)}, u32[]{:S(2)}, u32[]{:S(2)}) collective-permute-start(bf16[64,1024]{1,0:T(8,128)(2,1)S(1)} %project_values.1.refs_0_), channel_id=1, source_target_pairs={{0,96},{1,33},{2,98},{3,35},{4,100},{5,37},{6,102},{7,39},{8,104},... | collective-permute-start | bytes 393224 | tf_op jit(solution)/shard_map/ppermute | solution.py:56
  130.2 4.3 %collective-permute-done.22.refs_3_ = bf16[64,1024]{1,0:T(8,128)(2,1)S(1)} collective-permute-done((bf16[64,1024]{1,0:T(8,128)(2,1)S(1)}, bf16[64,1024]{1,0:T(8,128)(2,1)S(1)}, u32[]{:S(2)}, u32[]{:S(2)}) %collective-permute-start.22) | collective-permute-done | bytes 131104 | tf_op jit(solution)/shard_map/ppermute | solution.py:52
  134.5 3.4 %output_blocks.1 = (bf16[4,4,8,1792]{3,2,1,0:T(8,128)(2,1)S(1)}, bf16[4,4,8,1792]{3,2,1,0:T(8,128)(2,1)S(1)}) custom-call(s32[3]{0:T(128)S(1)} %pad_add_fusion.1.place_ref, bf16[64,1024]{1,0:T(8,128)(2,1)S(1)} %project_values.1.refs_0_, bf16[64,1024]{1,0:T(8,128)(2,1)S(1)} %collective-permute-done.20.refs_1_, ...), custom_call_target="tpu_custom_call" | custom-call | tf_op jit(solution)/shard_map/output_blocks/pallas_call | solution.py:519
  138.7 3.0 %collective-permute-start.25 = (bf16[4,4,8,1792]{3,2,1,0:T(8,128)(2,1)S(1)}, bf16[4,4,8,1792]{3,2,1,0:T(8,128)(2,1)S(1)}, u32[]{:S(2)}, u32[]{:S(2)}) collective-permute-start(bf16[4,4,8,1792]{3,2,1,0:T(8,128)(2,1)S(1)} %get-tuple-element.47), channel_id=1, source_target_pairs={{0,1},{1,0},{2,3},{3,2},{4,5},{5,4},{6,7},{7,6},{8,9},{9,8},{10,11... | collective-permute-start | bytes 1376264 | tf_op jit(solution)/shard_map/ppermute | solution.py:60
  164.2 2.8 %collective-permute-start.32 = (bf16[8,7168]{1,0:T(8,128)(2,1)}, bf16[8,7168]{1,0:T(8,128)(2,1)S(1)}, u32[]{:S(2)}, u32[]{:S(2)}) collective-permute-start(bf16[8,7168]{1,0:T(8,128)(2,1)} %join_columns.1.refs_0_), channel_id=1, source_target_pairs={{0,2},{1,7},{2,4},{3,1},{4,6},{5,3},{6,0},{7,5},{8,10},{9,15},{10,... | collective-permute-start | bytes 344072 | tf_op jit(solution)/shard_map/ppermute | solution.py:52
  169.1 3.0 %collective-permute-start.34 = (bf16[8,7168]{1,0:T(8,128)(2,1)S(1)}, bf16[8,7168]{1,0:T(8,128)(2,1)S(1)}, u32[]{:S(2)}, u32[]{:S(2)}) collective-permute-start(bf16[8,7168]{1,0:T(8,128)(2,1)S(1)} %collective-permute-done.32.refs_1_), channel_id=1, source_target_pairs={{0,2},{1,7},{2,4},{3,1},{4,6},{5,3},{6,0},{7,5},{8,10},{9,15},{10,... | collective-permute-start | bytes 344072 | tf_op jit(solution)/shard_map/ppermute | solution.py:52
  172.0 5.7 %collective-permute-start.35 = (bf16[8,7168]{1,0:T(8,128)(2,1)}, bf16[8,7168]{1,0:T(8,128)(2,1)S(1)}, u32[]{:S(2)}, u32[]{:S(2)}) collective-permute-start(bf16[8,7168]{1,0:T(8,128)(2,1)} %join_columns.1.refs_0_), channel_id=1, source_target_pairs={{0,1},{1,0},{2,3},{3,2},{4,5},{5,4},{6,7},{7,6},{8,9},{9,8},{10,11... | collective-permute-start | bytes 344072 | tf_op jit(solution)/shard_map/ppermute | solution.py:60
  178.2 5.5 %collective-permute-start.38 = (bf16[8,7168]{1,0:T(8,128)(2,1)S(1)}, bf16[8,7168]{1,0:T(8,128)(2,1)S(1)}, u32[]{:S(2)}, u32[]{:S(2)}) collective-permute-start(bf16[8,7168]{1,0:T(8,128)(2,1)S(1)} %collective-permute-done.34.refs_3_), channel_id=1, source_target_pairs={{0,1},{1,0},{2,3},{3,2},{4,5},{5,4},{6,7},{7,6},{8,9},{9,8},{10,11... | collective-permute-start | bytes 344072 | tf_op jit(solution)/shard_map/ppermute | solution.py:60
  (170 shorter events, 78.4 us)
Async XLA Ops:
  4.6 8.5 %collective-permute-start = (bf16[4,128,1024]{2,1,0:T(8,128)(2,1)}, bf16[4,128,1024]{2,1,0:T(8,128)(2,1)}, u32[]{:S(2)}, u32[]{:S(2)}) collective-permute-start(bf16[4,128,1024]{2,1,0:T(8,128)(2,1)} %pack_columns.1), channel_id=1, source_target_pairs={{0,1},{1,0},{2,3},{3,2},{4,5},{5,4},{6,7},{7,6},{8,9},{9,8},{10,11... | collective-permute-start | bytes 3145736 | tf_op jit(solution)/shard_map/ppermute | solution.py:60
  6.1 29.8 %collective-permute-start.4 = (bf16[448,1024]{1,0:T(8,128)(2,1)S(1)}, bf16[448,1024]{1,0:T(8,128)(2,1)S(1)}, u32[]{:S(2)}, u32[]{:S(2)}) collective-permute-start(bf16[448,1024]{1,0:T(8,128)(2,1)S(1)} %bitcast.39), channel_id=1, source_target_pairs={{0,8},{1,25},{2,10},{3,27},{4,12},{5,29},{6,14},{7,31},{8,16},{9,1... | collective-permute-start | bytes 2752520 | tf_op jit(solution)/shard_map/ppermute | solution.py:52
  8.7 121.2 %collective-permute-start.23 = (bf16[448,1024]{1,0:T(8,128)(2,1)S(1)}, bf16[448,1024]{1,0:T(8,128)(2,1)S(1)}, u32[]{:S(2)}, u32[]{:S(2)}) collective-permute-start(bf16[448,1024]{1,0:T(8,128)(2,1)S(1)} %bitcast.40), channel_id=1, source_target_pairs={{0,24},{1,9},{2,26},{3,11},{4,28},{5,13},{6,30},{7,15},{8,0},{9,17... | collective-permute-start | bytes 2752520 | tf_op jit(solution)/shard_map/ppermute | solution.py:56
  16.7 7.5 %collective-permute-start.1 = (bf16[128,1024]{1,0:T(8,128)(2,1)}, bf16[128,1024]{1,0:T(8,128)(2,1)}, u32[]{:S(2)}, u32[]{:S(2)}) collective-permute-start(bf16[128,1024]{1,0:T(8,128)(2,1)} %get-tuple-element.32), channel_id=1, source_target_pairs={{0,2},{1,7},{2,4},{3,1},{4,6},{5,3},{6,0},{7,5},{8,10},{9,15},{10,... | collective-permute-start | bytes 786440 | tf_op jit(solution)/shard_map/ppermute | solution.py:52
  19.7 12.6 %collective-permute-start.3 = (bf16[128,1024]{1,0:T(8,128)(2,1)}, bf16[128,1024]{1,0:T(8,128)(2,1)S(1)}, u32[]{:S(2)}, u32[]{:S(2)}) collective-permute-start(bf16[128,1024]{1,0:T(8,128)(2,1)} %get-tuple-element.33), channel_id=1, source_target_pairs={{0,6},{1,3},{2,0},{3,5},{4,2},{5,7},{6,4},{7,1},{8,14},{9,11},{10,... | collective-permute-start | bytes 786440 | tf_op jit(solution)/shard_map/ppermute | solution.py:56
  26.0 6.9 %collective-permute-start.2 = (bf16[128,1024]{1,0:T(8,128)(2,1)}, bf16[128,1024]{1,0:T(8,128)(2,1)}, u32[]{:S(2)}, u32[]{:S(2)}) collective-permute-start(bf16[128,1024]{1,0:T(8,128)(2,1)} %add_convert_fusion), channel_id=1, source_target_pairs={{0,2},{1,7},{2,4},{3,1},{4,6},{5,3},{6,0},{7,5},{8,10},{9,15},{10,... | collective-permute-start | bytes 786440 | tf_op jit(solution)/shard_map/ppermute | solution.py:52
  36.0 11.2 %collective-permute-start.5 = (bf16[64,1024]{1,0:T(8,128)(2,1)}, bf16[64,1024]{1,0:T(8,128)(2,1)S(1)}, u32[]{:S(2)}, u32[]{:S(2)}) collective-permute-start(bf16[64,1024]{1,0:T(8,128)(2,1)} %get-tuple-element.39.refs_0_), channel_id=1, source_target_pairs={{0,8},{1,25},{2,10},{3,27},{4,12},{5,29},{6,14},{7,31},{8,16},{9,1... | collective-permute-start | bytes 393224 | tf_op jit(solution)/shard_map/ppermute | solution.py:52
  40.1 9.7 %collective-permute-start.11 = (bf16[64,1024]{1,0:T(8,128)(2,1)}, bf16[64,1024]{1,0:T(8,128)(2,1)}, u32[]{:S(2)}, u32[]{:S(2)}) collective-permute-start(bf16[64,1024]{1,0:T(8,128)(2,1)} %get-tuple-element.40.refs_0_), channel_id=1, source_target_pairs={{0,32},{1,97},{2,34},{3,99},{4,36},{5,101},{6,38},{7,103},{8,40},{... | collective-permute-start | bytes 393224 | tf_op jit(solution)/shard_map/ppermute | solution.py:52
  47.1 9.2 %collective-permute-start.12 = (bf16[64,1024]{1,0:T(8,128)(2,1)}, bf16[64,1024]{1,0:T(8,128)(2,1)}, u32[]{:S(2)}, u32[]{:S(2)}) collective-permute-start(bf16[64,1024]{1,0:T(8,128)(2,1)} %get-tuple-element.40.refs_0_), channel_id=1, source_target_pairs={{0,96},{1,33},{2,98},{3,35},{4,100},{5,37},{6,102},{7,39},{8,104},... | collective-permute-start | bytes 393224 | tf_op jit(solution)/shard_map/ppermute | solution.py:56
  55.8 8.6 %collective-permute-start.8 = (bf16[256,1024]{1,0:T(8,128)(2,1)}, bf16[256,1024]{1,0:T(8,128)(2,1)}, u32[]{:S(2)}, u32[]{:S(2)}) collective-permute-start(bf16[256,1024]{1,0:T(8,128)(2,1)} %stack_rows.2.refs_0_), channel_id=1, source_target_pairs={{0,32},{1,97},{2,34},{3,99},{4,36},{5,101},{6,38},{7,103},{8,40},{... | collective-permute-start | bytes 1572872 | tf_op jit(solution)/shard_map/ppermute | solution.py:52
  58.2 9.6 %collective-permute-start.14 = (bf16[256,1024]{1,0:T(8,128)(2,1)}, bf16[256,1024]{1,0:T(8,128)(2,1)S(1)}, u32[]{:S(2)}, u32[]{:S(2)}) collective-permute-start(bf16[256,1024]{1,0:T(8,128)(2,1)} %stack_rows.3.refs_4_), channel_id=1, source_target_pairs={{0,8},{1,25},{2,10},{3,27},{4,12},{5,29},{6,14},{7,31},{8,16},{9,1... | collective-permute-start | bytes 1572872 | tf_op jit(solution)/shard_map/ppermute | solution.py:52
  62.9 10.7 %collective-permute-start.9 = (bf16[256,1024]{1,0:T(8,128)(2,1)S(1)}, bf16[256,1024]{1,0:T(8,128)(2,1)S(1)}, u32[]{:S(2)}, u32[]{:S(2)}) collective-permute-start(bf16[256,1024]{1,0:T(8,128)(2,1)S(1)} %copy-done.2), channel_id=1, source_target_pairs={{0,96},{1,33},{2,98},{3,35},{4,100},{5,37},{6,102},{7,39},{8,104},... | collective-permute-start | bytes 1572872 | tf_op jit(solution)/shard_map/ppermute | solution.py:56
  63.0 13.1 %collective-permute-start.15 = (bf16[256,1024]{1,0:T(8,128)(2,1)}, bf16[256,1024]{1,0:T(8,128)(2,1)S(1)}, u32[]{:S(2)}, u32[]{:S(2)}) collective-permute-start(bf16[256,1024]{1,0:T(8,128)(2,1)} %stack_rows.3.refs_4_), channel_id=1, source_target_pairs={{0,24},{1,9},{2,26},{3,11},{4,28},{5,13},{6,30},{7,15},{8,0},{9,17... | collective-permute-start | bytes 1572872 | tf_op jit(solution)/shard_map/ppermute | solution.py:56
  64.5 14.3 %collective-permute-start.10 = (bf16[256,1024]{1,0:T(8,128)(2,1)}, bf16[256,1024]{1,0:T(8,128)(2,1)S(1)}, u32[]{:S(2)}, u32[]{:S(2)}) collective-permute-start(bf16[256,1024]{1,0:T(8,128)(2,1)} %collective-permute-done.8.refs_1_), channel_id=1, source_target_pairs={{0,32},{1,97},{2,34},{3,99},{4,36},{5,101},{6,38},{7,103},{8,40},{... | collective-permute-start | bytes 1572872 | tf_op jit(solution)/shard_map/ppermute | solution.py:52
  67.9 12.3 %collective-permute-start.16 = (bf16[256,1024]{1,0:T(8,128)(2,1)S(1)}, bf16[256,1024]{1,0:T(8,128)(2,1)S(1)}, u32[]{:S(2)}, u32[]{:S(2)}) collective-permute-start(bf16[256,1024]{1,0:T(8,128)(2,1)S(1)} %collective-permute-done.14.refs_5_), channel_id=1, source_target_pairs={{0,8},{1,25},{2,10},{3,27},{4,12},{5,29},{6,14},{7,31},{8,16},{9,1... | collective-permute-start | bytes 1572872 | tf_op jit(solution)/shard_map/ppermute | solution.py:52
  73.6 18.5 %collective-permute-start.18 = (bf16[4,64,64]{2,1,0:T(8,128)(2,1)S(1)}, bf16[4,64,64]{2,1,0:T(8,128)(2,1)S(1)}, u32[]{:S(2)}, u32[]{:S(2)}) collective-permute-start(bf16[4,64,64]{2,1,0:T(8,128)(2,1)S(1)} %get-tuple-element.64), channel_id=1, source_target_pairs={{0,1},{1,0},{2,3},{3,2},{4,5},{5,4},{6,7},{7,6},{8,9},{9,8},{10,11... | collective-permute-start | bytes 98312 | tf_op jit(solution)/shard_map/ppermute | solution.py:60
  76.2 53.7 %collective-permute-start.24 = (bf16[448,1024]{1,0:T(8,128)(2,1)S(1)}, bf16[448,1024]{1,0:T(8,128)(2,1)S(1)}, u32[]{:S(2)}, u32[]{:S(2)}) collective-permute-start(bf16[448,1024]{1,0:T(8,128)(2,1)S(1)} %collective-permute-done.4.refs_5_), channel_id=1, source_target_pairs={{0,8},{1,25},{2,10},{3,27},{4,12},{5,29},{6,14},{7,31},{8,16},{9,1... | collective-permute-start | bytes 2752520 | tf_op jit(solution)/shard_map/ppermute | solution.py:52
  120.8 9.1 %collective-permute-start.20 = (bf16[64,1024]{1,0:T(8,128)(2,1)S(1)}, bf16[64,1024]{1,0:T(8,128)(2,1)S(1)}, u32[]{:S(2)}, u32[]{:S(2)}) collective-permute-start(bf16[64,1024]{1,0:T(8,128)(2,1)S(1)} %project_values.1.refs_0_), channel_id=1, source_target_pairs={{0,32},{1,97},{2,34},{3,99},{4,36},{5,101},{6,38},{7,103},{8,40},{... | collective-permute-start | bytes 393224 | tf_op jit(solution)/shard_map/ppermute | solution.py:52
  123.1 7.2 %collective-permute-start.21 = (bf16[64,1024]{1,0:T(8,128)(2,1)S(1)}, bf16[64,1024]{1,0:T(8,128)(2,1)S(1)}, u32[]{:S(2)}, u32[]{:S(2)}) collective-permute-start(bf16[64,1024]{1,0:T(8,128)(2,1)S(1)} %project_values.1.refs_0_), channel_id=1, source_target_pairs={{0,96},{1,33},{2,98},{3,35},{4,100},{5,37},{6,102},{7,39},{8,104},... | collective-permute-start | bytes 393224 | tf_op jit(solution)/shard_map/ppermute | solution.py:56
  167.0 10.8 %collective-permute-start.33 = (bf16[8,7168]{1,0:T(8,128)(2,1)}, bf16[8,7168]{1,0:T(8,128)(2,1)S(1)}, u32[]{:S(2)}, u32[]{:S(2)}) collective-permute-start(bf16[8,7168]{1,0:T(8,128)(2,1)} %join_columns.1.refs_0_), channel_id=1, source_target_pairs={{0,6},{1,3},{2,0},{3,5},{4,2},{5,7},{6,4},{7,1},{8,14},{9,11},{10,... | collective-permute-start | bytes 344072 | tf_op jit(solution)/shard_map/ppermute | solution.py:56
  169.1 9.1 %collective-permute-start.34 = (bf16[8,7168]{1,0:T(8,128)(2,1)S(1)}, bf16[8,7168]{1,0:T(8,128)(2,1)S(1)}, u32[]{:S(2)}, u32[]{:S(2)}) collective-permute-start(bf16[8,7168]{1,0:T(8,128)(2,1)S(1)} %collective-permute-done.32.refs_1_), channel_id=1, source_target_pairs={{0,2},{1,7},{2,4},{3,1},{4,6},{5,3},{6,0},{7,5},{8,10},{9,15},{10,... | collective-permute-start | bytes 344072 | tf_op jit(solution)/shard_map/ppermute | solution.py:52
  172.0 12.3 %collective-permute-start.35 = (bf16[8,7168]{1,0:T(8,128)(2,1)}, bf16[8,7168]{1,0:T(8,128)(2,1)S(1)}, u32[]{:S(2)}, u32[]{:S(2)}) collective-permute-start(bf16[8,7168]{1,0:T(8,128)(2,1)} %join_columns.1.refs_0_), channel_id=1, source_target_pairs={{0,1},{1,0},{2,3},{3,2},{4,5},{5,4},{6,7},{7,6},{8,9},{9,8},{10,11... | collective-permute-start | bytes 344072 | tf_op jit(solution)/shard_map/ppermute | solution.py:60
  177.7 6.6 %collective-permute-start.36 = (bf16[8,7168]{1,0:T(8,128)(2,1)S(1)}, bf16[8,7168]{1,0:T(8,128)(2,1)S(1)}, u32[]{:S(2)}, u32[]{:S(2)}) collective-permute-start(bf16[8,7168]{1,0:T(8,128)(2,1)S(1)} %collective-permute-done.32.refs_1_), channel_id=1, source_target_pairs={{0,1},{1,0},{2,3},{3,2},{4,5},{5,4},{6,7},{7,6},{8,9},{9,8},{10,11... | collective-permute-start | bytes 344072 | tf_op jit(solution)/shard_map/ppermute | solution.py:60
  177.8 6.6 %collective-permute-start.37 = (bf16[8,7168]{1,0:T(8,128)(2,1)S(1)}, bf16[8,7168]{1,0:T(8,128)(2,1)S(1)}, u32[]{:S(2)}, u32[]{:S(2)}) collective-permute-start(bf16[8,7168]{1,0:T(8,128)(2,1)S(1)} %collective-permute-done.33.refs_2_), channel_id=1, source_target_pairs={{0,1},{1,0},{2,3},{3,2},{4,5},{5,4},{6,7},{7,6},{8,9},{9,8},{10,11... | collective-permute-start | bytes 344072 | tf_op jit(solution)/shard_map/ppermute | solution.py:60
  (49 other events, 423.0 us)

commit v2 on v1

v2 whole, which is shorter than its diff:
```python
import functools
import itertools
import math

import jax
import jax.numpy as jnp
import numpy as np
from jax import lax
from jax.experimental import pallas as pl
from jax.experimental.pallas import tpu as pltpu
from jax.sharding import PartitionSpec as P

HDIM = 128
ROPE = 64
SIDE = 4
BLOCK = 1024
SLOTS = 12
MIB = 1024 * 1024

first_fix = 1.0 - math.exp(100.0 * math.log(0.9))
second_fix = 1.0 - math.exp(100.0 * math.log(0.999))
NEG = -1e30
LOG2E = math.log2(math.e)

NT = (((1,), (1,)), ((), ()))
NN = (((1,), (0,)), ((), ()))


def dot(a, b, dims):
    return lax.dot_general(a, b, dims, preferred_element_type=jnp.float32)


def moves(step):
    perm = []
    for z in range(SIDE):
        for x in range(SIDE):
            for y in range(SIDE):
                for c in range(2):
                    axis, d = step(c)
                    to = {"x": x, "y": y, "z": z}
                    to[axis] = (to[axis] + d) % SIDE
                    perm.append(
                        (
                            (z * SIDE + x) * 2 * SIDE + y * 2 + c,
                            (to["z"] * SIDE + to["x"]) * 2 * SIDE + to["y"] * 2 + c,
                        )
                    )
    return perm


def shift(v, step):
    return lax.ppermute(v, ("fsdp", "head"), moves(step))


def forth(v, axis):
    return shift(v, lambda c: (axis, 1 - 2 * c))


def back(v, axis):
    return shift(v, lambda c: (axis, 2 * c - 1))


def first(v, d):
    return shift(v, lambda c: (("x", "z")[c], d))


def second(v, d):
    return shift(v, lambda c: (("z", "x")[c], d))


def other_core(v):
    return lax.ppermute(v, "head", [(i, i ^ 1) for i in range(2 * SIDE)])


def ring(own, axis):
    one = forth(own, axis)
    two = back(own, axis)
    return own, one, two, forth(one, axis)


def ring_sum(blocks, axis):
    far = forth(blocks[3], axis)
    two = back(blocks[2], axis)
    one = forth(add_two(blocks[1], far), axis)
    return blocks[0], one, two


def here():
    f = lax.axis_index("fsdp")
    h = lax.axis_index("head")
    return lax.div(f, SIDE), lax.rem(f, SIDE), lax.div(h, 2), lax.rem(h, 2)


def turned(base, s):
    return [lax.rem(base + d, SIDE) for d in (0, SIDE + s, SIDE - s, 2)]


VMEM = pl.BlockSpec(memory_space=pltpu.VMEM)
SMEM = pl.BlockSpec(memory_space=pltpu.SMEM)
HBM = pl.BlockSpec(memory_space=pltpu.HBM)
F32 = jnp.float32
BF16 = jnp.bfloat16


def room(mib):
    return pltpu.CompilerParams(vmem_limit_bytes=mib * MIB)


def add_two_body(a, b, o):
    o[...] = (a[...].astype(F32) + b[...].astype(F32)).astype(o.dtype)


def add_two(a, b):
    return pl.pallas_call(
        add_two_body,
        in_specs=[VMEM] * 2,
        out_specs=VMEM,
        out_shape=jax.ShapeDtypeStruct(a.shape, BF16),
        compiler_params=room(8),
        name="add_two",
    )(a, b)


def pack_body(g_ref, send_ref, keep_ref, sem):
    _, _, y, core = here()
    sign = 1 - 2 * core
    cols = send_ref.shape[2]
    copies = []
    for ref, ys, c in (
        (send_ref, turned(y, -sign), 1 - core),
        (keep_ref, turned(y, sign), core),
    ):
        for j in range(SIDE):
            at = pl.multiple_of((2 * ys[j] + c) * cols, 128)
            copies.append(
                pltpu.make_async_copy(
                    g_ref.at[:, pl.ds(at, cols)], ref.at[j], sem.at[len(copies)]
                )
            )
    for copy in copies:
        copy.start()
    for copy in copies:
        copy.wait()


def pack(g):
    out = jax.ShapeDtypeStruct((SIDE, g.shape[0], g.shape[1] // (2 * SIDE)), g.dtype)
    return pl.pallas_call(
        pack_body,
        in_specs=[HBM],
        out_specs=[VMEM] * 2,
        out_shape=[out] * 2,
        scratch_shapes=[pltpu.SemaphoreType.DMA((2 * SIDE,))],
        compiler_params=room(8),
        name="pack_columns",
    )(g)


def add_body(keep, got, o0, o1, o2, o3):
    for j, o in ((3, o3), (2, o2), (1, o1), (0, o0)):
        o[...] = (keep[j].astype(F32) + got[j].astype(F32)).astype(o.dtype)


def add_pairs(keep, got, kind):
    shape = got.shape[1:]
    return pl.pallas_call(
        add_body,
        in_specs=[VMEM] * 2,
        out_specs=[VMEM] * SIDE,
        out_shape=[jax.ShapeDtypeStruct(shape, kind)] + [jax.ShapeDtypeStruct(shape, BF16)] * 3,
        compiler_params=room(8),
        name="add_pairs",
    )(keep, got)


def adam_body(r0, r1, r2, p, one, two, new_p, new_one, new_two, w):
    grad = r0[...] + r1[...].astype(F32) + r2[...].astype(F32)
    moment = 0.9 * one[...] + 0.1 * grad
    second_moment = 0.999 * two[...] + 0.001 * grad * grad
    step_size = 0.003 / first_fix
    denom = jnp.sqrt(second_moment / second_fix) + 1e-08
    params = p[...] - step_size * moment / denom
    w[...] = params.astype(BF16)
    new_p[...] = params
    new_one[...] = moment
    new_two[...] = second_moment


def adam(parts, p, one, two):
    full = jax.ShapeDtypeStruct(p.shape, F32)
    return pl.pallas_call(
        adam_body,
        in_specs=[VMEM] * 6,
        out_specs=[VMEM] * 4,
        out_shape=[full] * 3 + [jax.ShapeDtypeStruct(p.shape, BF16)],
        compiler_params=room(12),
        name="adam",
    )(*parts, p, one, two)


def stack_body(a, b, out):
    rows = a.shape[0]
    out[:rows, :] = a[...]
    out[rows:, :] = b[...]


def stack_rows(a, b):
    rows, cols = a.shape
    return pl.pallas_call(
        stack_body,
        in_specs=[VMEM] * 2,
        out_specs=VMEM,
        out_shape=jax.ShapeDtypeStruct((2 * rows, cols), a.dtype),
        compiler_params=room(8),
        name="stack_rows",
    )(a, b)


def query_body(ql_ref, *refs, seqs, steps, heads, q_rank):
    units = refs[:8]
    keep_ref, send_ref, w_buf, lat_buf = refs[8:]
    z, x, _, core = here()
    shard = w_buf.shape[0] // (SIDE * SIDE)
    far = (0, SIDE - 1, 1, 2)
    for k in range(SIDE):
        for m in range(SIDE):
            zo = jnp.where(core == 0, far[k], far[m])
            xo = jnp.where(core == 0, far[m], far[k])
            f = lax.rem(z + zo, SIDE) * SIDE + lax.rem(x + xo, SIDE)
            at = pl.multiple_of(f * shard, shard)
            rows = slice((m % 2) * shard, (m % 2 + 1) * shard)
            w_buf[pl.ds(at, shard), :] = units[2 * k + m // 2][rows, :]
    nope = dot(ql_ref[...], w_buf[:q_rank, :], NN).astype(BF16)
    for h in range(heads):
        cols = slice(h * HDIM, (h + 1) * HDIM)
        lat = dot(nope[:, cols], w_buf[q_rank:, cols], NT)
        lat_buf[:, h * steps : (h + 1) * steps, :] = lat.reshape(seqs, steps, -1)
    keep_ref[...] = lat_buf[: seqs // 2].astype(BF16)
    send_ref[...] = lat_buf[seqs // 2 :].astype(BF16)


def queries(ql, units, w_rows, seqs, q_rank):
    cols = units[0].shape[1]
    heads = cols // HDIM
    steps = ql.shape[0] // seqs
    lat_rank = w_rows - q_rank
    out = jax.ShapeDtypeStruct((seqs // 2, heads * steps, lat_rank), BF16)
    return pl.pallas_call(
        functools.partial(query_body, seqs=seqs, steps=steps, heads=heads, q_rank=q_rank),
        in_specs=[VMEM] * 9,
        out_specs=[VMEM] * 2,
        out_shape=[out] * 2,
        scratch_shapes=[
            pltpu.VMEM((w_rows, cols), BF16),
            pltpu.VMEM((seqs, heads * steps, lat_rank), F32),
        ],
        compiler_params=room(16),
        name="queries",
    )(ql, *units)


def attention_body(
    order_ref,
    len_ref,
    q_own,
    q_got,
    r_own,
    r_got,
    nl_ref,
    nr_ref,
    lat_hbm,
    rope_hbm,
    keep_ref,
    send_ref,
    lat_buf,
    rope_buf,
    q_buf,
    qr_buf,
    acc,
    m_ref,
    l_ref,
    p0,
    p1,
    a0,
    a1,
    seq_of,
    blk_of,
    lat_sem,
    rope_sem,
    *,
    steps,
):
    seqs, rows, _ = q_buf.shape
    part = rows // 2
    factor = LOG2E / math.sqrt(HDIM + ROPE)

    def listing(s, at):
        blocks = lax.div(len_ref[s] + (BLOCK - 1), BLOCK)

        def put(j, at):
            seq_of[at] = s
            blk_of[at] = j
            return at + 1

        return lax.fori_loop(0, blocks, put, at)

    count = lax.fori_loop(0, seqs, listing, 0)

    def lat_copy(i):
        slot = lax.rem(i, SLOTS)
        start = pl.multiple_of(blk_of[i] * BLOCK, BLOCK)
        return pltpu.make_async_copy(
            lat_hbm.at[order_ref[seq_of[i]], pl.ds(start, BLOCK), :],
            lat_buf.at[slot],
            lat_sem.at[slot],
        )

    def rope_copy(i):
        slot = lax.rem(i, SLOTS)
        start = pl.multiple_of(blk_of[i] * BLOCK, BLOCK)
        return pltpu.make_async_copy(
            rope_hbm.at[order_ref[seq_of[i]], :, pl.ds(start, BLOCK)],
            rope_buf.at[slot],
            rope_sem.at[slot],
        )

    def fetch(i):
        @pl.when(i < count)
        def _():
            lat_copy(i).start()
            rope_copy(i).start()

    for i in range(SLOTS - 2):
        fetch(i)

    q_buf[:, :part, :] = q_own[...]
    q_buf[:, part:, :] = q_got[...]
    qr_buf[:, :part, :] = r_own[...]
    qr_buf[:, part:, :] = r_got[...]

    width = nl_ref.shape[1]
    token = lax.broadcasted_iota(jnp.int32, (rows, width), 1)
    step = lax.rem(lax.broadcasted_iota(jnp.int32, (rows, width), 0), steps)
    seen = token <= step
    for s in range(seqs):
        score = dot(q_buf[s], nl_ref[s], NT) + dot(qr_buf[s], nr_ref[s], NT)
        score = jnp.where(seen, score, NEG)
        top = jnp.max(score, axis=1, keepdims=True)
        prob = jnp.exp2((score - top) * factor)
        m_ref[s] = jnp.broadcast_to(top, (rows, 128))
        l_ref[s] = prob
        acc[s] = dot(prob.astype(BF16), nl_ref[s], NN)

    lane = lax.broadcasted_iota(jnp.int32, (rows, BLOCK), 1)

    def arrive(i):
        lat_copy(i).wait()
        rope_copy(i).wait()

    def scores(i):
        slot = lax.rem(i, SLOTS)
        s = seq_of[i]
        return dot(q_buf[s], lat_buf[slot], NT) + dot(qr_buf[s], rope_buf[slot], NN)

    def weigh(i, score, p_ref, a_ref):
        s = seq_of[i]
        score = jnp.where(lane < len_ref[s] - blk_of[i] * BLOCK, score, NEG)
        before = m_ref[s]
        top = jnp.maximum(before, jnp.max(score, axis=1, keepdims=True))
        prob = jnp.exp2((score - top[:, :1]) * factor)
        alpha = jnp.exp2((before - top) * factor)
        total = l_ref[s] * alpha
        for k in range(BLOCK // 128):
            total += prob[:, k * 128 : (k + 1) * 128]
        m_ref[s] = top
        l_ref[s] = total
        a_ref[...] = alpha
        p_ref[...] = prob.astype(BF16)

    def gather(i, p_ref, a_ref):
        slot = lax.rem(i, SLOTS)
        s = seq_of[i]
        acc[s] = acc[s] * a_ref[:, :1] + dot(p_ref[...], lat_buf[slot], NN)

    arrive(0)
    weigh(0, scores(0), p0, a0)

    def pair(k, carry):
        i = 2 * k
        fetch(i + SLOTS - 2)
        fetch(i + SLOTS - 1)
        arrive(i + 1)
        arrive(i + 2)
        odd = scores(i + 1)
        gather(i, p0, a0)
        even = scores(i + 2)
        weigh(i + 1, odd, p1, a1)
        gather(i + 1, p1, a1)
        weigh(i + 2, even, p0, a0)
        return carry

    pairs = lax.div(count - 1, 2)
    lax.fori_loop(0, pairs, pair, 0)

    @pl.when(2 * pairs + 1 < count)
    def _():
        arrive(2 * pairs + 1)
        odd = scores(2 * pairs + 1)
        gather(2 * pairs, p0, a0)
        weigh(2 * pairs + 1, odd, p1, a1)
        gather(2 * pairs + 1, p1, a1)

    @pl.when(2 * pairs + 1 >= count)
    def _():
        gather(2 * pairs, p0, a0)

    for s in range(seqs):
        mixed = (acc[s] / jnp.sum(l_ref[s], axis=1, keepdims=True)).astype(BF16)
        keep_ref[s] = mixed[:part]
        send_ref[s] = mixed[part:]


def attention(order, lengths, q_own, q_got, r_own, r_got, nl, nr, lat, rope, steps):
    seqs, part, lat_rank = q_own.shape
    rows = 2 * part
    most = seqs * (lat.shape[1] // BLOCK) + 1
    out = jax.ShapeDtypeStruct(q_own.shape, BF16)
    return pl.pallas_call(
        functools.partial(attention_body, steps=steps),
        in_specs=[SMEM, SMEM] + [VMEM] * 6 + [HBM] * 2,
        out_specs=[VMEM] * 2,
        out_shape=[out] * 2,
        scratch_shapes=[
            pltpu.VMEM((SLOTS, BLOCK, lat_rank), BF16),
            pltpu.VMEM((SLOTS, ROPE, BLOCK), BF16),
            pltpu.VMEM((seqs, rows, lat_rank), BF16),
            pltpu.VMEM((seqs, rows, ROPE), BF16),
            pltpu.VMEM((seqs, rows, lat_rank), F32),
            pltpu.VMEM((seqs, rows, 128), F32),
            pltpu.VMEM((seqs, rows, 128), F32),
            pltpu.VMEM((rows, BLOCK), BF16),
            pltpu.VMEM((rows, BLOCK), BF16),
            pltpu.VMEM((rows, 128), F32),
            pltpu.VMEM((rows, 128), F32),
            pltpu.SMEM((most,), jnp.int32),
            pltpu.SMEM((most,), jnp.int32),
            pltpu.SemaphoreType.DMA((SLOTS,)),
            pltpu.SemaphoreType.DMA((SLOTS,)),
        ],
        compiler_params=room(36),
        name="attention",
    )(order, lengths, q_own, q_got, r_own, r_got, nl, nr, lat, rope)


def values_body(order_ref, own, got, vw_ref, out_ref, mixed, flat):
    half, rows, lat_rank = own.shape
    seqs = 2 * half
    heads = vw_ref.shape[1] // HDIM
    steps = rows // heads
    mixed[:half] = own[...].astype(F32)
    mixed[half:] = got[...].astype(F32)
    for h in range(heads):
        cols = slice(h * HDIM, (h + 1) * HDIM)
        part = mixed[:, h * steps : (h + 1) * steps, :].reshape(seqs * steps, lat_rank)
        flat[:, cols] = dot(part.astype(BF16), vw_ref[:, cols], NN).astype(BF16)
    _, _, y, core = here()
    sign = 1 - 2 * core
    step_of = [2 * v + (1 - core) for v in turned(y, -sign)]
    step_of += [2 * v + core for v in turned(y, sign)]
    count = seqs * steps
    row = lax.broadcasted_iota(jnp.int32, (count, count), 0)
    col = lax.broadcasted_iota(jnp.int32, (count, count), 1)
    want_step = jnp.zeros((count, count), jnp.int32)
    want_seq = jnp.zeros((count, count), jnp.int32)
    for k in range(steps):
        want_step = jnp.where(lax.div(row, seqs) == k, step_of[k], want_step)
    for k in range(seqs):
        want_seq = jnp.where(lax.div(col, steps) == k, order_ref[k], want_seq)
    same = (want_step == lax.rem(col, steps)) & (want_seq == lax.rem(row, seqs))
    pick = jnp.where(same, 1.0, 0.0).astype(BF16)
    out_ref[...] = dot(pick, flat[...], NN).astype(BF16)


def project_values(order, own, got, vw):
    half, rows, lat_rank = own.shape
    cols = vw.shape[1]
    count = 2 * half * rows * HDIM // cols
    return pl.pallas_call(
        values_body,
        in_specs=[SMEM] + [VMEM] * 3,
        out_specs=VMEM,
        out_shape=jax.ShapeDtypeStruct((count, cols), BF16),
        scratch_shapes=[
            pltpu.VMEM((2 * half, rows, lat_rank), F32),
            pltpu.VMEM((count, cols), BF16),
        ],
        compiler_params=room(12),
        name="project_values",
    )(order, own, got, vw)


def output_body(*refs, seqs):
    tokens, weights = refs[:4], refs[4:8]
    send_ref, keep_ref, v_buf, w_buf = refs[8:]
    _, x, _, core = here()
    sign = 1 - 2 * core
    offsets = (0, SIDE - sign, SIDE + sign, 2)
    depth = v_buf.shape[2]
    part = weights[0].shape[0]
    for k in range(SIDE):
        v_buf[lax.rem(offsets[k], SIDE) if k in (1, 2) else offsets[k]] = tokens[k][...]
        at = pl.multiple_of(lax.rem(x + offsets[k], SIDE) * part, 64)
        w_buf[pl.ds(at, part), :] = weights[k][...]
    tokens_all = v_buf[...].reshape(-1, depth)
    width = 256
    for n in range(w_buf.shape[0] // width):
        cols = slice(n * width, (n + 1) * width)
        res = dot(tokens_all, w_buf[cols, :], NT).reshape(SIDE, 2 * SIDE, seqs, width)
        for b in range(SIDE):
            for z in range(SIDE):
                send_ref[b, z, :, cols] = res[z, b].astype(BF16)
                keep_ref[b, z, :, cols] = res[z, SIDE + b].astype(BF16)


def output_blocks(tokens, weights, seqs):
    count, depth = tokens[0].shape
    cols = SIDE * weights[0].shape[0]
    out = jax.ShapeDtypeStruct((SIDE, SIDE, seqs, cols), BF16)
    return pl.pallas_call(
        functools.partial(output_body, seqs=seqs),
        in_specs=[VMEM] * 8,
        out_specs=[VMEM] * 2,
        out_shape=[out] * 2,
        scratch_shapes=[
            pltpu.VMEM((SIDE, count, depth), BF16),
            pltpu.VMEM((cols, depth), BF16),
        ],
        compiler_params=room(16),
        name="output_blocks",
    )(*tokens, *weights)


def total_body(a, b, c, o0, o1, o2, o3):
    for j, o in enumerate((o0, o1, o2, o3)):
        o[...] = (a[j].astype(F32) + b[j].astype(F32) + c[j].astype(F32)).astype(o.dtype)


def total_blocks(parts):
    out = jax.ShapeDtypeStruct(parts[0].shape[1:], BF16)
    return pl.pallas_call(
        total_body,
        in_specs=[VMEM] * 3,
        out_specs=[VMEM] * SIDE,
        out_shape=[out] * SIDE,
        compiler_params=room(8),
        name="total_blocks",
    )(*parts)


def columns_body(*refs):
    out = refs[-1]
    width = refs[0].shape[1]
    z = here()[0]
    for d, ref in enumerate(refs[:-1]):
        at = lax.rem(z + SIDE - d, SIDE) * width
        out[:, pl.ds(pl.multiple_of(at, 128), width)] = ref[...]


def join_columns(blocks):
    rows, width = blocks[0].shape
    return pl.pallas_call(
        columns_body,
        in_specs=[VMEM] * SIDE,
        out_specs=VMEM,
        out_shape=jax.ShapeDtypeStruct((rows, SIDE * width), BF16),
        compiler_params=room(8),
        name="join_columns",
    )(*blocks)


def settle_body(*refs):
    out = refs[-1]
    _, _, y, core = here()
    sign = 1 - 2 * core
    steps = [2 * v + core for v in turned(y, -sign)]
    steps += [2 * v + (1 - core) for v in turned(y, sign)]
    for step, ref in zip(steps, refs[:-1]):
        out[step] = ref[...]


def settle(blocks):
    return pl.pallas_call(
        settle_body,
        in_specs=[VMEM] * 8,
        out_specs=VMEM,
        out_shape=jax.ShapeDtypeStruct((8,) + blocks[0].shape, BF16),
        compiler_params=room(8),
        name="settle",
    )(*blocks)


def splits(seqs):
    table = []
    for rest in itertools.combinations(range(1, seqs), seqs // 2 - 1):
        mine = (0,) + rest
        table.append(mine + tuple(s for s in range(seqs) if s not in mine))
    return np.array(table, np.int32)


def balanced_order(lengths):
    seqs = lengths.shape[0]
    table = splits(seqs)
    member = np.zeros((table.shape[0], seqs), np.int32)
    for i, row in enumerate(table):
        member[i, row[: seqs // 2]] = 1
    blocks = lax.div(lengths + (BLOCK - 1), BLOCK)
    first = jnp.sum(member * blocks[None, :], axis=1)
    larger = jnp.maximum(first, jnp.sum(blocks) - first)
    index = np.arange(table.shape[0], dtype=np.int32)
    score = larger * table.shape[0] + index
    chosen = (score == jnp.min(score)).astype(jnp.int32)
    return jnp.sum(chosen[:, None] * table, axis=0)


def rotate(vector, position):
    half = vector.shape[-1] // 2
    index_f = jnp.arange(half, dtype=jnp.float32)
    frequency = jnp.exp(-math.log(10000.0) * 2.0 * index_f / vector.shape[-1])
    angle = position[..., None] * frequency
    first = vector[..., :half]
    second = vector[..., half:]
    cosine = jnp.cos(angle)
    sine = jnp.sin(angle)
    return jnp.concatenate(
        [first * cosine - second * sine, first * sine + second * cosine], axis=-1
    )


def body(
    grad_parts,
    params,
    moment_one,
    moment_two,
    query_latent,
    rope_weight,
    value_weight,
    out_weight,
    latent_cache,
    rope_cache,
    new_latent,
    new_rope,
    lengths,
):
    core = lax.rem(lax.axis_index("head"), 2)

    send, keep = pack(grad_parts[0])
    sums = add_pairs(keep, other_core(send), F32)
    parts = ring_sum(sums, "y")
    new_params, new_one, new_two, w = adam(parts, params, moment_one, moment_two)

    w_t = out_weight.T
    w_one, w_two = forth(w_t, "x"), back(w_t, "x")
    w_one, w = lax.optimization_barrier((w_one, w))

    above, below = first(w, 1), first(w, -1)
    top = stack_rows(w, above)
    bottom = stack_rows(below, first(above, 1))
    top_above, top_below = second(top, 1), second(top, -1)
    bottom_above, bottom_below = second(bottom, 1), second(bottom, -1)
    units = [top, bottom, top_above, bottom_above, top_below, bottom_below]
    units += [second(top_above, 1), second(bottom_below, -1)]
    out_weights = (w_t, w_one, w_two, forth(w_one, "x"))

    steps_n, seq_local, q_rank = query_latent.shape
    heads_local = value_weight.shape[1] // HDIM
    half = seq_local // 2
    lengths, _ = lax.optimization_barrier((lengths, sums[3]))
    order = balanced_order(lengths)
    order = jnp.where(core == 0, order, jnp.concatenate([order[half:], order[:half]]))
    chosen = order[:, None] == jnp.arange(seq_local, dtype=jnp.int32)[None, :]
    lengths_in = jnp.sum(jnp.where(chosen, lengths[None, :], 0), axis=1)
    chosen = chosen.astype(BF16)

    def arrange(which, arrays):
        return jnp.einsum("ps,tsq->ptq", which, arrays, preferred_element_type=F32).astype(BF16)

    by_seq = arrange(chosen, query_latent).reshape(seq_local * steps_n, q_rank)
    by_seq_late, rope_late, _ = lax.optimization_barrier((by_seq, rope_weight, bottom))
    query_rope = jnp.dot(by_seq_late, rope_late, preferred_element_type=F32).reshape(
        seq_local, steps_n, heads_local, ROPE
    )
    position = (lengths_in[:, None] + jnp.arange(steps_n, dtype=jnp.int32)[None, :]).astype(F32)[
        :, :, None
    ]
    query_rope = rotate(query_rope, position).astype(BF16)
    query_rope = jnp.transpose(query_rope, (0, 2, 1, 3)).reshape(
        seq_local, heads_local * steps_n, ROPE
    )
    r_own, r_got = query_rope[:half], other_core(query_rope[half:])
    pad = ((0, 0), (0, 128 - steps_n), (0, 0))
    nl = jnp.pad(arrange(chosen[:half], new_latent), pad)
    nr = jnp.pad(arrange(chosen[:half], new_rope), pad)

    w_rows = SIDE * SIDE * params.shape[0]
    q_own, q_send = queries(by_seq, units, w_rows, seq_local, q_rank)
    mixed, mixed_send = attention(
        order,
        lengths_in[:half],
        q_own,
        other_core(q_send),
        r_own,
        r_got,
        nl,
        nr,
        latent_cache,
        rope_cache,
        steps_n,
    )
    values = project_values(order, mixed, other_core(mixed_send), value_weight)

    send, keep = output_blocks(ring(values, "z"), out_weights, seq_local)
    parts = ring_sum(add_pairs(keep, other_core(send), BF16), "y")
    blocks = total_blocks(parts)

    arrived = [blocks[0]]
    for d in range(1, SIDE):
        perm = [
            (zz * SIDE + xx, ((zz + d) % SIDE) * SIDE + xx)
            for zz in range(SIDE)
            for xx in range(SIDE)
        ]
        arrived.append(lax.ppermute(blocks[d], "fsdp", perm))
    mine = join_columns(arrived)

    column = list(ring(mine, "y"))
    column += [other_core(b) for b in column]
    decoded = settle(column)
    return (new_params, new_one, new_two, decoded)


def solution(mesh):
    return jax.shard_map(
        body,
        mesh=mesh,
        in_specs=(
            P("head", "fsdp", None),
            P("fsdp", "head"),
            P("fsdp", "head"),
            P("fsdp", "head"),
            P(None, "fsdp", None),
            P(None, "head"),
            P(None, "head"),
            P("head", "fsdp"),
            P("fsdp", None, None),
            P("fsdp", None, None),
            P(None, "fsdp", None),
            P(None, "fsdp", None),
            P("fsdp"),
        ),
        out_specs=(P("fsdp", "head"), P("fsdp", "head"), P("fsdp", "head"), P(None, "fsdp", None)),
        check_vma=False,
    )
```

time: 190 us -> 149 us (0.78)
  Pallas kernels: 54.3 us -> 30.9 us
  starting transfers between devices: 75 us -> 62.4 us
  waiting for transfers between devices: 31.1 us -> 40.3 us
  other arithmetic: 11.6 us -> 5.64 us
  local copies, waits for them, and re-layouts: 11.4 us -> 7.33 us
  matrix products: 3.49 us -> 0.89 us
    pallas_call x10 -> x12, Pallas kernels: 23.2 us -> 9.56 us  [the longest x1 3.09 us: output_blocks(): pl.pallas_call(functools.partial(output_body, seqs=seqs), in_specs=[VMEM]...]
    ppermute x27 -> x24, starting transfers between devices: 48.5 us -> 38.9 us  [shift(): return lax.ppermute(v, ('fsdp', 'head'), moves(step))]
    ppermute x27 -> x24, waiting for transfers between devices: 26 us -> 33.5 us  [shift(): return lax.ppermute(v, ('fsdp', 'head'), moves(step))]
    unnamed x69 -> x32, local copies, waits for them, and re-layouts: 10.5 us -> 5.15 us
    pallas_call x1, Pallas kernels: 7.55 us -> 2.67 us  [queries(): pl.pallas_call(functools.partial(query_body, seqs=seqs, steps=steps, head...]
    pallas_call x1, Pallas kernels: 21.9 us -> 18.6 us  [attention(): pl.pallas_call(functools.partial(attention_body, steps=steps), in_specs=[...]
    convert_element_type x2 -> x0, other arithmetic: 2.73 us -> none  [ring_sum(): (near.astype(jnp.float32) + far.astype(jnp.float32)).astype(near.dtype)]
    dot_general x1, matrix products: 2.98 us -> 0.38 us  [body(): jnp.dot(by_seq_late, rope_late, preferred_element_type=F32)]
  transfers between devices with their start and end apart: 39 -> 36, of which waited for: 19 -> 23; matrix products, arithmetic and copies ran while one was open for 9% -> 6% of each run, Pallas kernels for 22% -> 17%
where the time goes in v2:
time: 149 us; the launch traced here: 148 us
  starting transfers between devices  62.4 us (42%)
  waiting for transfers between devices  40.3 us (27%)
  Pallas kernels  30.9 us (21%)
  local copies, waits for them, and re-layouts  7.33 us (5%)
  other arithmetic  5.64 us (4%)
    ppermute x24, starting transfers between devices, shift(): return lax.ppermute(v, ('fsdp', 'head'), moves(step))  38.9 us
    ppermute x24, waiting for transfers between devices, shift(): return lax.ppermute(v, ('fsdp', 'head'), moves(step))  33.5 us
    ppermute x9, starting transfers between devices, other_core(): return lax.ppermute(v, 'head', [(i, i ^ 1) for i in range(2 * SIDE)])  20.8 us
    pallas_call x1, Pallas kernels, attention(): pl.pallas_call(functools.partial(attention_body, steps=steps), in_specs=[...  18.6 us
    unnamed x32, local copies, waits for them, and re-layouts  5.15 us
    ppermute x9, waiting for transfers between devices, other_core(): return lax.ppermute(v, 'head', [(i, i ^ 1) for i in range(2 * SIDE)])  4.7 us
    pallas_call x1, Pallas kernels, output_blocks(): pl.pallas_call(functools.partial(output_body, seqs=seqs), in_specs=[VMEM]...  3.09 us
  transfers between devices with their start and end apart: 36, of which 23 were waited for; matrix products, arithmetic and copies ran while one was open for 6% of the time, Pallas kernels for 17%

profile of v2, /device:TPU:1, one launch (start us, length us, event | category | flops | bytes accessed | tf_op | source)
XLA Modules:
  0.0 148.4 jit_solution(6879891394223353417)
XLA Ops:
  5.1 2.6 %collective-permute-start.4 = (bf16[448,1024]{1,0:T(8,128)(2,1)}, bf16[448,1024]{1,0:T(8,128)(2,1)S(1)}, u32[]{:S(2)}, u32[]{:S(2)}) collective-permute-start(bf16[448,1024]{1,0:T(8,128)(2,1)} %bitcast.3.refs_4_), channel_id=1, source_target_pairs={{0,8},{1,25},{2,10},{3,27},{4,12},{5,29},{6,14},{7,31},{8,16},{9,1... | collective-permute-start | bytes 2752520 | tf_op jit(solution)/shard_map/ppermute | solution.py:52
  9.3 2.9 %collective-permute-start.1 = (bf16[128,1024]{1,0:T(8,128)(2,1)S(1)}, bf16[128,1024]{1,0:T(8,128)(2,1)S(1)}, u32[]{:S(2)}, u32[]{:S(2)}) collective-permute-start(bf16[128,1024]{1,0:T(8,128)(2,1)S(1)} %get-tuple-element.37), channel_id=1, source_target_pairs={{0,2},{1,7},{2,4},{3,1},{4,6},{5,3},{6,0},{7,5},{8,10},{9,15},{10,... | collective-permute-start | bytes 786440 | tf_op jit(solution)/shard_map/ppermute | solution.py:52
  17.0 3.5 %collective-permute-start.2 = (bf16[128,1024]{1,0:T(8,128)(2,1)S(1)}, bf16[128,1024]{1,0:T(8,128)(2,1)S(1)}, u32[]{:S(2)}, u32[]{:S(2)}) collective-permute-start(bf16[128,1024]{1,0:T(8,128)(2,1)S(1)} %add_two.2), channel_id=1, source_target_pairs={{0,2},{1,7},{2,4},{3,1},{4,6},{5,3},{6,0},{7,5},{8,10},{9,15},{10,... | collective-permute-start | bytes 786440 | tf_op jit(solution)/shard_map/ppermute | solution.py:52
  20.6 3.2 %collective-permute-done.2.r1 = bf16[128,1024]{1,0:T(8,128)(2,1)S(1)} collective-permute-done((bf16[128,1024]{1,0:T(8,128)(2,1)S(1)}, bf16[128,1024]{1,0:T(8,128)(2,1)S(1)}, u32[]{:S(2)}, u32[]{:S(2)}) %collective-permute-start.2) | collective-permute-done | bytes 262176 | tf_op jit(solution)/shard_map/ppermute | solution.py:52
  31.2 3.8 %collective-permute-done.5.b = bf16[128,1024]{1,0:T(8,128)(2,1)S(1)} collective-permute-done((bf16[128,1024]{1,0:T(8,128)(2,1)S(1)}, bf16[128,1024]{1,0:T(8,128)(2,1)S(1)}, u32[]{:S(2)}, u32[]{:S(2)}) %collective-permute-start.5) | collective-permute-done | bytes 262176 | tf_op jit(solution)/shard_map/ppermute | solution.py:52
  36.2 5.5 %collective-permute-done.7.b = bf16[128,1024]{1,0:T(8,128)(2,1)S(1)} collective-permute-done((bf16[128,1024]{1,0:T(8,128)(2,1)S(1)}, bf16[128,1024]{1,0:T(8,128)(2,1)S(1)}, u32[]{:S(2)}, u32[]{:S(2)}) %collective-permute-start.7) | collective-permute-done | bytes 262176 | tf_op jit(solution)/shard_map/ppermute | solution.py:52
  41.7 3.2 %collective-permute-start.11 = (bf16[256,1024]{1,0:T(8,128)(2,1)S(1)}, bf16[256,1024]{1,0:T(8,128)(2,1)}, u32[]{:S(2)}, u32[]{:S(2)}) collective-permute-start(bf16[256,1024]{1,0:T(8,128)(2,1)S(1)} %stack_rows.3.refs_1_), channel_id=1, source_target_pairs={{0,96},{1,25},{2,98},{3,27},{4,100},{5,29},{6,102},{7,31},{8,104},... | collective-permute-start | bytes 1572872 | tf_op jit(solution)/shard_map/ppermute | solution.py:52
  48.4 2.6 %collective-permute-done.11.refs_5_ = bf16[256,1024]{1,0:T(8,128)(2,1)} collective-permute-done((bf16[256,1024]{1,0:T(8,128)(2,1)S(1)}, bf16[256,1024]{1,0:T(8,128)(2,1)}, u32[]{:S(2)}, u32[]{:S(2)}) %collective-permute-start.11) | collective-permute-done | bytes 524320 | tf_op jit(solution)/shard_map/ppermute | solution.py:52
  51.0 3.2 %collective-permute-start.13 = (bf16[256,1024]{1,0:T(8,128)(2,1)}, bf16[256,1024]{1,0:T(8,128)(2,1)S(1)}, u32[]{:S(2)}, u32[]{:S(2)}) collective-permute-start(bf16[256,1024]{1,0:T(8,128)(2,1)} %collective-permute-done.11.refs_5_), channel_id=1, source_target_pairs={{0,96},{1,25},{2,98},{3,27},{4,100},{5,29},{6,102},{7,31},{8,104},... | collective-permute-start | bytes 1572872 | tf_op jit(solution)/shard_map/ppermute | solution.py:52
  56.7 3.5 %collective-permute-start.21 = (bf16[448,1024]{1,0:T(8,128)(2,1)S(1)}, bf16[448,1024]{1,0:T(8,128)(2,1)S(1)}, u32[]{:S(2)}, u32[]{:S(2)}) collective-permute-start(bf16[448,1024]{1,0:T(8,128)(2,1)S(1)} %copy-done.5), channel_id=1, source_target_pairs={{0,8},{1,25},{2,10},{3,27},{4,12},{5,29},{6,14},{7,31},{8,16},{9,1... | collective-permute-start | bytes 2752520 | tf_op jit(solution)/shard_map/ppermute | solution.py:52
  62.4 2.7 %queries.1 = (bf16[4,64,512]{2,1,0:T(8,128)(2,1)S(1)}, bf16[4,64,512]{2,1,0:T(8,128)(2,1)S(1)}) custom-call(bf16[64,1536]{1,0:T(8,128)(2,1)S(1)} %bitcast.27, bf16[256,1024]{1,0:T(8,128)(2,1)S(1)} %stack_rows.2.refs_0_, bf16[256,1024]{1,0:T(8,128)(2,1)S(1)} %stack_rows.3.refs_1_, bf16[256,1024]{1,0:T(8,128)(2,1)} %collective-permute-done.8.refs_2_, ...), custom_call_target="tpu_custom_call" | custom-call | tf_op jit(solution)/shard_map/queries/pallas_call | solution.py:248
  65.1 6.0 %collective-permute-start.14 = (bf16[4,64,512]{2,1,0:T(8,128)(2,1)S(1)}, bf16[4,64,512]{2,1,0:T(8,128)(2,1)S(1)}, u32[]{:S(2)}, u32[]{:S(2)}) collective-permute-start(bf16[4,64,512]{2,1,0:T(8,128)(2,1)S(1)} %get-tuple-element.46), channel_id=1, source_target_pairs={{0,1},{1,0},{2,3},{3,2},{4,5},{5,4},{6,7},{7,6},{8,9},{9,8},{10,11... | collective-permute-start | bytes 786440 | tf_op jit(solution)/shard_map/ppermute | solution.py:72
  72.4 3.4 %copy-done.1 = bf16[8,64,8192]{2,1,0:T(8,128)(2,1)S(1)} copy-done((bf16[8,64,8192]{2,1,0:T(8,128)(2,1)S(1)}, bf16[8,64,8192]{2,1,0:T(8,128)(2,1)}, u32[]{:S(2)}) %copy-start.1) | copy-done | bytes 8388632
  75.8 18.6 %attention.1 = (bf16[4,64,512]{2,1,0:T(8,128)(2,1)S(1)}, bf16[4,64,512]{2,1,0:T(8,128)(2,1)S(1)}) custom-call(s32[8]{0:T(128)S(1)} %broadcast_select_fusion.order_ref, s32[4]{0:T(128)S(1)} %bitcast.28, bf16[4,64,512]{2,1,0:T(8,128)(2,1)S(1)} %get-tuple-element.45.q_own, bf16[4,64,512]{2,1,0:T(8,128)(2,1)S(1)} %collective-permute-done.14.q_got, ...), custom_call_target="tpu_custom_call" | custom-call | tf_op jit(solution)/shard_map/attention/pallas_call | solution.py:428
  98.6 3.2 %collective-permute-done.17.refs_1_ = bf16[64,1024]{1,0:T(8,128)(2,1)S(1)} collective-permute-done((bf16[64,1024]{1,0:T(8,128)(2,1)S(1)}, bf16[64,1024]{1,0:T(8,128)(2,1)S(1)}, u32[]{:S(2)}, u32[]{:S(2)}) %collective-permute-start.17) | collective-permute-done | bytes 131104 | tf_op jit(solution)/shard_map/ppermute | solution.py:52
  103.4 2.3 %collective-permute-done.19.refs_3_ = bf16[64,1024]{1,0:T(8,128)(2,1)S(1)} collective-permute-done((bf16[64,1024]{1,0:T(8,128)(2,1)S(1)}, bf16[64,1024]{1,0:T(8,128)(2,1)S(1)}, u32[]{:S(2)}, u32[]{:S(2)}) %collective-permute-start.19) | collective-permute-done | bytes 131104 | tf_op jit(solution)/shard_map/ppermute | solution.py:52
  105.7 3.1 %output_blocks.1 = (bf16[4,4,8,1792]{3,2,1,0:T(8,128)(2,1)S(1)}, bf16[4,4,8,1792]{3,2,1,0:T(8,128)(2,1)S(1)}) custom-call(bf16[64,1024]{1,0:T(8,128)(2,1)S(1)} %project_values.1.refs_0_, bf16[64,1024]{1,0:T(8,128)(2,1)S(1)} %collective-permute-done.17.refs_1_, bf16[64,1024]{1,0:T(8,128)(2,1)S(1)} %collective-permute-done.18.refs_2_, ...), custom_call_target="tpu_custom_call" | custom-call | tf_op jit(solution)/shard_map/output_blocks/pallas_call | solution.py:529
  108.8 4.9 %collective-permute-start.22 = (bf16[4,4,8,1792]{3,2,1,0:T(8,128)(2,1)S(1)}, bf16[4,4,8,1792]{3,2,1,0:T(8,128)(2,1)S(1)}, u32[]{:S(2)}, u32[]{:S(2)}) collective-permute-start(bf16[4,4,8,1792]{3,2,1,0:T(8,128)(2,1)S(1)} %get-tuple-element.53), channel_id=1, source_target_pairs={{0,1},{1,0},{2,3},{3,2},{4,5},{5,4},{6,7},{7,6},{8,9},{9,8},{10,11... | collective-permute-start | bytes 1376264 | tf_op jit(solution)/shard_map/ppermute | solution.py:72
  115.3 2.8 %collective-permute-start.23 = (bf16[4,8,1792]{2,1,0:T(8,128)(2,1)S(1)}, bf16[4,8,1792]{2,1,0:T(8,128)(2,1)S(1)}, u32[]{:S(2)}, u32[]{:S(2)}) collective-permute-start(bf16[4,8,1792]{2,1,0:T(8,128)(2,1)S(1)} %get-tuple-element.56), channel_id=1, source_target_pairs={{0,2},{1,7},{2,4},{3,1},{4,6},{5,3},{6,0},{7,5},{8,10},{9,15},{10,... | collective-permute-start | bytes 344072 | tf_op jit(solution)/shard_map/ppermute | solution.py:52
  119.9 3.6 %collective-permute-start.24 = (bf16[4,8,1792]{2,1,0:T(8,128)(2,1)S(1)}, bf16[4,8,1792]{2,1,0:T(8,128)(2,1)S(1)}, u32[]{:S(2)}, u32[]{:S(2)}) collective-permute-start(bf16[4,8,1792]{2,1,0:T(8,128)(2,1)S(1)} %add_two.3), channel_id=1, source_target_pairs={{0,2},{1,7},{2,4},{3,1},{4,6},{5,3},{6,0},{7,5},{8,10},{9,15},{10,... | collective-permute-start | bytes 344072 | tf_op jit(solution)/shard_map/ppermute | solution.py:52
  125.9 2.2 %collective-permute-start.28 = (bf16[8,1792]{1,0:T(8,128)(2,1)S(1)}, bf16[8,1792]{1,0:T(8,128)(2,1)S(1)}, u32[]{:S(2)}, u32[]{:S(2)}) collective-permute-start(bf16[8,1792]{1,0:T(8,128)(2,1)S(1)} %get-tuple-element.61), channel_id=1, source_target_pairs={{0,96},{8,104},{16,112},{24,120},{32,0},{40,8},{48,16},{56,24},{64... | collective-permute-start | bytes 86024 | tf_op jit(solution)/shard_map/ppermute | solution.py:732
  130.3 3.4 %collective-permute-start.29 = (bf16[8,7168]{1,0:T(8,128)(2,1)S(1)}, bf16[8,7168]{1,0:T(8,128)(2,1)S(1)}, u32[]{:S(2)}, u32[]{:S(2)}) collective-permute-start(bf16[8,7168]{1,0:T(8,128)(2,1)S(1)} %join_columns.1.refs_0_), channel_id=1, source_target_pairs={{0,2},{1,7},{2,4},{3,1},{4,6},{5,3},{6,0},{7,5},{8,10},{9,15},{10,... | collective-permute-start | bytes 344072 | tf_op jit(solution)/shard_map/ppermute | solution.py:52
  135.5 3.1 %collective-permute-start.31 = (bf16[8,7168]{1,0:T(8,128)(2,1)S(1)}, bf16[8,7168]{1,0:T(8,128)(2,1)S(1)}, u32[]{:S(2)}, u32[]{:S(2)}) collective-permute-start(bf16[8,7168]{1,0:T(8,128)(2,1)S(1)} %collective-permute-done.29.refs_1_), channel_id=1, source_target_pairs={{0,2},{1,7},{2,4},{3,1},{4,6},{5,3},{6,0},{7,5},{8,10},{9,15},{10,... | collective-permute-start | bytes 344072 | tf_op jit(solution)/shard_map/ppermute | solution.py:52
  141.0 5.5 %collective-permute-start.35 = (bf16[8,7168]{1,0:T(8,128)(2,1)S(1)}, bf16[8,7168]{1,0:T(8,128)(2,1)S(1)}, u32[]{:S(2)}, u32[]{:S(2)}) collective-permute-start(bf16[8,7168]{1,0:T(8,128)(2,1)S(1)} %collective-permute-done.31.refs_3_), channel_id=1, source_target_pairs={{0,1},{1,0},{2,3},{3,2},{4,5},{5,4},{6,7},{7,6},{8,9},{9,8},{10,11... | collective-permute-start | bytes 344072 | tf_op jit(solution)/shard_map/ppermute | solution.py:72
  (121 shorter events, 48.8 us)
Async XLA Ops:
  5.1 22.1 %collective-permute-start.4 = (bf16[448,1024]{1,0:T(8,128)(2,1)}, bf16[448,1024]{1,0:T(8,128)(2,1)S(1)}, u32[]{:S(2)}, u32[]{:S(2)}) collective-permute-start(bf16[448,1024]{1,0:T(8,128)(2,1)} %bitcast.3.refs_4_), channel_id=1, source_target_pairs={{0,8},{1,25},{2,10},{3,27},{4,12},{5,29},{6,14},{7,31},{8,16},{9,1... | collective-permute-start | bytes 2752520 | tf_op jit(solution)/shard_map/ppermute | solution.py:52
  7.7 94.5 %collective-permute-start.20 = (bf16[448,1024]{1,0:T(8,128)(2,1)}, bf16[448,1024]{1,0:T(8,128)(2,1)}, u32[]{:S(2)}, u32[]{:S(2)}) collective-permute-start(bf16[448,1024]{1,0:T(8,128)(2,1)} %bitcast.3.refs_4_), channel_id=1, source_target_pairs={{0,24},{1,9},{2,26},{3,11},{4,28},{5,13},{6,30},{7,15},{8,0},{9,17... | collective-permute-start | bytes 2752520 | tf_op jit(solution)/shard_map/ppermute | solution.py:52
  9.3 7.6 %collective-permute-start.1 = (bf16[128,1024]{1,0:T(8,128)(2,1)S(1)}, bf16[128,1024]{1,0:T(8,128)(2,1)S(1)}, u32[]{:S(2)}, u32[]{:S(2)}) collective-permute-start(bf16[128,1024]{1,0:T(8,128)(2,1)S(1)} %get-tuple-element.37), channel_id=1, source_target_pairs={{0,2},{1,7},{2,4},{3,1},{4,6},{5,3},{6,0},{7,5},{8,10},{9,15},{10,... | collective-permute-start | bytes 786440 | tf_op jit(solution)/shard_map/ppermute | solution.py:52
  12.2 8.4 %collective-permute-start.3 = (bf16[128,1024]{1,0:T(8,128)(2,1)S(1)}, bf16[128,1024]{1,0:T(8,128)(2,1)S(1)}, u32[]{:S(2)}, u32[]{:S(2)}) collective-permute-start(bf16[128,1024]{1,0:T(8,128)(2,1)S(1)} %get-tuple-element.38), channel_id=1, source_target_pairs={{0,6},{1,3},{2,0},{3,5},{4,2},{5,7},{6,4},{7,1},{8,14},{9,11},{10,... | collective-permute-start | bytes 786440 | tf_op jit(solution)/shard_map/ppermute | solution.py:52
  17.0 6.8 %collective-permute-start.2 = (bf16[128,1024]{1,0:T(8,128)(2,1)S(1)}, bf16[128,1024]{1,0:T(8,128)(2,1)S(1)}, u32[]{:S(2)}, u32[]{:S(2)}) collective-permute-start(bf16[128,1024]{1,0:T(8,128)(2,1)S(1)} %add_two.2), channel_id=1, source_target_pairs={{0,2},{1,7},{2,4},{3,1},{4,6},{5,3},{6,0},{7,5},{8,10},{9,15},{10,... | collective-permute-start | bytes 786440 | tf_op jit(solution)/shard_map/ppermute | solution.py:52
  27.2 7.7 %collective-permute-start.5 = (bf16[128,1024]{1,0:T(8,128)(2,1)S(1)}, bf16[128,1024]{1,0:T(8,128)(2,1)S(1)}, u32[]{:S(2)}, u32[]{:S(2)}) collective-permute-start(bf16[128,1024]{1,0:T(8,128)(2,1)S(1)} %get-tuple-element.44.a), channel_id=1, source_target_pairs={{0,8},{1,33},{2,10},{3,35},{4,12},{5,37},{6,14},{7,39},{8,16},{9,4... | collective-permute-start | bytes 786440 | tf_op jit(solution)/shard_map/ppermute | solution.py:52
  29.0 7.1 %collective-permute-start.6 = (bf16[128,1024]{1,0:T(8,128)(2,1)S(1)}, bf16[128,1024]{1,0:T(8,128)(2,1)S(1)}, u32[]{:S(2)}, u32[]{:S(2)}) collective-permute-start(bf16[128,1024]{1,0:T(8,128)(2,1)S(1)} %get-tuple-element.44.a), channel_id=1, source_target_pairs={{0,24},{1,97},{2,26},{3,99},{4,28},{5,101},{6,30},{7,103},{8,0},{9... | collective-permute-start | bytes 786440 | tf_op jit(solution)/shard_map/ppermute | solution.py:52
  35.0 6.7 %collective-permute-start.7 = (bf16[128,1024]{1,0:T(8,128)(2,1)S(1)}, bf16[128,1024]{1,0:T(8,128)(2,1)S(1)}, u32[]{:S(2)}, u32[]{:S(2)}) collective-permute-start(bf16[128,1024]{1,0:T(8,128)(2,1)S(1)} %collective-permute-done.5.b), channel_id=1, source_target_pairs={{0,8},{1,33},{2,10},{3,35},{4,12},{5,37},{6,14},{7,39},{8,16},{9,4... | collective-permute-start | bytes 786440 | tf_op jit(solution)/shard_map/ppermute | solution.py:52
  36.1 12.4 %collective-permute-start.8 = (bf16[256,1024]{1,0:T(8,128)(2,1)S(1)}, bf16[256,1024]{1,0:T(8,128)(2,1)}, u32[]{:S(2)}, u32[]{:S(2)}) collective-permute-start(bf16[256,1024]{1,0:T(8,128)(2,1)S(1)} %stack_rows.2.refs_0_), channel_id=1, source_target_pairs={{0,32},{1,9},{2,34},{3,11},{4,36},{5,13},{6,38},{7,15},{8,40},{9,1... | collective-permute-start | bytes 1572872 | tf_op jit(solution)/shard_map/ppermute | solution.py:52
  41.7 9.3 %collective-permute-start.11 = (bf16[256,1024]{1,0:T(8,128)(2,1)S(1)}, bf16[256,1024]{1,0:T(8,128)(2,1)}, u32[]{:S(2)}, u32[]{:S(2)}) collective-permute-start(bf16[256,1024]{1,0:T(8,128)(2,1)S(1)} %stack_rows.3.refs_1_), channel_id=1, source_target_pairs={{0,96},{1,25},{2,98},{3,27},{4,100},{5,29},{6,102},{7,31},{8,104},... | collective-permute-start | bytes 1572872 | tf_op jit(solution)/shard_map/ppermute | solution.py:52
  45.2 11.4 %collective-permute-start.10 = (bf16[256,1024]{1,0:T(8,128)(2,1)S(1)}, bf16[256,1024]{1,0:T(8,128)(2,1)S(1)}, u32[]{:S(2)}, u32[]{:S(2)}) collective-permute-start(bf16[256,1024]{1,0:T(8,128)(2,1)S(1)} %stack_rows.2.refs_0_), channel_id=1, source_target_pairs={{0,96},{1,25},{2,98},{3,27},{4,100},{5,29},{6,102},{7,31},{8,104},... | collective-permute-start | bytes 1572872 | tf_op jit(solution)/shard_map/ppermute | solution.py:52
  45.3 14.9 %collective-permute-start.9 = (bf16[256,1024]{1,0:T(8,128)(2,1)S(1)}, bf16[256,1024]{1,0:T(8,128)(2,1)}, u32[]{:S(2)}, u32[]{:S(2)}) collective-permute-start(bf16[256,1024]{1,0:T(8,128)(2,1)S(1)} %stack_rows.3.refs_1_), channel_id=1, source_target_pairs={{0,32},{1,9},{2,34},{3,11},{4,36},{5,13},{6,38},{7,15},{8,40},{9,1... | collective-permute-start | bytes 1572872 | tf_op jit(solution)/shard_map/ppermute | solution.py:52
  48.4 12.2 %collective-permute-start.12 = (bf16[256,1024]{1,0:T(8,128)(2,1)}, bf16[256,1024]{1,0:T(8,128)(2,1)S(1)}, u32[]{:S(2)}, u32[]{:S(2)}) collective-permute-start(bf16[256,1024]{1,0:T(8,128)(2,1)} %collective-permute-done.8.refs_2_), channel_id=1, source_target_pairs={{0,32},{1,9},{2,34},{3,11},{4,36},{5,13},{6,38},{7,15},{8,40},{9,1... | collective-permute-start | bytes 1572872 | tf_op jit(solution)/shard_map/ppermute | solution.py:52
  51.0 11.3 %collective-permute-start.13 = (bf16[256,1024]{1,0:T(8,128)(2,1)}, bf16[256,1024]{1,0:T(8,128)(2,1)S(1)}, u32[]{:S(2)}, u32[]{:S(2)}) collective-permute-start(bf16[256,1024]{1,0:T(8,128)(2,1)} %collective-permute-done.11.refs_5_), channel_id=1, source_target_pairs={{0,96},{1,25},{2,98},{3,27},{4,100},{5,29},{6,102},{7,31},{8,104},... | collective-permute-start | bytes 1572872 | tf_op jit(solution)/shard_map/ppermute | solution.py:52
  56.7 45.6 %collective-permute-start.21 = (bf16[448,1024]{1,0:T(8,128)(2,1)S(1)}, bf16[448,1024]{1,0:T(8,128)(2,1)S(1)}, u32[]{:S(2)}, u32[]{:S(2)}) collective-permute-start(bf16[448,1024]{1,0:T(8,128)(2,1)S(1)} %copy-done.5), channel_id=1, source_target_pairs={{0,8},{1,25},{2,10},{3,27},{4,12},{5,29},{6,14},{7,31},{8,16},{9,1... | collective-permute-start | bytes 2752520 | tf_op jit(solution)/shard_map/ppermute | solution.py:52
  65.1 7.4 %collective-permute-start.14 = (bf16[4,64,512]{2,1,0:T(8,128)(2,1)S(1)}, bf16[4,64,512]{2,1,0:T(8,128)(2,1)S(1)}, u32[]{:S(2)}, u32[]{:S(2)}) collective-permute-start(bf16[4,64,512]{2,1,0:T(8,128)(2,1)S(1)} %get-tuple-element.46), channel_id=1, source_target_pairs={{0,1},{1,0},{2,3},{3,2},{4,5},{5,4},{6,7},{7,6},{8,9},{9,8},{10,11... | collective-permute-start | bytes 786440 | tf_op jit(solution)/shard_map/ppermute | solution.py:72
  97.2 6.2 %collective-permute-start.18 = (bf16[64,1024]{1,0:T(8,128)(2,1)S(1)}, bf16[64,1024]{1,0:T(8,128)(2,1)S(1)}, u32[]{:S(2)}, u32[]{:S(2)}) collective-permute-start(bf16[64,1024]{1,0:T(8,128)(2,1)S(1)} %project_values.1.refs_0_), channel_id=1, source_target_pairs={{0,96},{1,33},{2,98},{3,35},{4,100},{5,37},{6,102},{7,39},{8,104},... | collective-permute-start | bytes 393224 | tf_op jit(solution)/shard_map/ppermute | solution.py:52
  108.8 6.4 %collective-permute-start.22 = (bf16[4,4,8,1792]{3,2,1,0:T(8,128)(2,1)S(1)}, bf16[4,4,8,1792]{3,2,1,0:T(8,128)(2,1)S(1)}, u32[]{:S(2)}, u32[]{:S(2)}) collective-permute-start(bf16[4,4,8,1792]{3,2,1,0:T(8,128)(2,1)S(1)} %get-tuple-element.53), channel_id=1, source_target_pairs={{0,1},{1,0},{2,3},{3,2},{4,5},{5,4},{6,7},{7,6},{8,9},{9,8},{10,11... | collective-permute-start | bytes 1376264 | tf_op jit(solution)/shard_map/ppermute | solution.py:72
  133.7 6.8 %collective-permute-start.30 = (bf16[8,7168]{1,0:T(8,128)(2,1)S(1)}, bf16[8,7168]{1,0:T(8,128)(2,1)S(1)}, u32[]{:S(2)}, u32[]{:S(2)}) collective-permute-start(bf16[8,7168]{1,0:T(8,128)(2,1)S(1)} %join_columns.1.refs_0_), channel_id=1, source_target_pairs={{0,6},{1,3},{2,0},{3,5},{4,2},{5,7},{6,4},{7,1},{8,14},{9,11},{10,... | collective-permute-start | bytes 344072 | tf_op jit(solution)/shard_map/ppermute | solution.py:52
  135.5 5.5 %collective-permute-start.31 = (bf16[8,7168]{1,0:T(8,128)(2,1)S(1)}, bf16[8,7168]{1,0:T(8,128)(2,1)S(1)}, u32[]{:S(2)}, u32[]{:S(2)}) collective-permute-start(bf16[8,7168]{1,0:T(8,128)(2,1)S(1)} %collective-permute-done.29.refs_1_), channel_id=1, source_target_pairs={{0,2},{1,7},{2,4},{3,1},{4,6},{5,3},{6,0},{7,5},{8,10},{9,15},{10,... | collective-permute-start | bytes 344072 | tf_op jit(solution)/shard_map/ppermute | solution.py:52
  138.5 7.9 %collective-permute-start.32 = (bf16[8,7168]{1,0:T(8,128)(2,1)S(1)}, bf16[8,7168]{1,0:T(8,128)(2,1)S(1)}, u32[]{:S(2)}, u32[]{:S(2)}) collective-permute-start(bf16[8,7168]{1,0:T(8,128)(2,1)S(1)} %join_columns.1.refs_0_), channel_id=1, source_target_pairs={{0,1},{1,0},{2,3},{3,2},{4,5},{5,4},{6,7},{7,6},{8,9},{9,8},{10,11... | collective-permute-start | bytes 344072 | tf_op jit(solution)/shard_map/ppermute | solution.py:72
  140.5 6.0 %collective-permute-start.33 = (bf16[8,7168]{1,0:T(8,128)(2,1)S(1)}, bf16[8,7168]{1,0:T(8,128)(2,1)S(1)}, u32[]{:S(2)}, u32[]{:S(2)}) collective-permute-start(bf16[8,7168]{1,0:T(8,128)(2,1)S(1)} %collective-permute-done.29.refs_1_), channel_id=1, source_target_pairs={{0,1},{1,0},{2,3},{3,2},{4,5},{5,4},{6,7},{7,6},{8,9},{9,8},{10,11... | collective-permute-start | bytes 344072 | tf_op jit(solution)/shard_map/ppermute | solution.py:72
  140.5 6.0 %collective-permute-start.34 = (bf16[8,7168]{1,0:T(8,128)(2,1)S(1)}, bf16[8,7168]{1,0:T(8,128)(2,1)S(1)}, u32[]{:S(2)}, u32[]{:S(2)}) collective-permute-start(bf16[8,7168]{1,0:T(8,128)(2,1)S(1)} %collective-permute-done.30.refs_2_), channel_id=1, source_target_pairs={{0,1},{1,0},{2,3},{3,2},{4,5},{5,4},{6,7},{7,6},{8,9},{9,8},{10,11... | collective-permute-start | bytes 344072 | tf_op jit(solution)/shard_map/ppermute | solution.py:72
  141.0 6.4 %collective-permute-start.35 = (bf16[8,7168]{1,0:T(8,128)(2,1)S(1)}, bf16[8,7168]{1,0:T(8,128)(2,1)S(1)}, u32[]{:S(2)}, u32[]{:S(2)}) collective-permute-start(bf16[8,7168]{1,0:T(8,128)(2,1)S(1)} %collective-permute-done.31.refs_3_), channel_id=1, source_target_pairs={{0,1},{1,0},{2,3},{3,2},{4,5},{5,4},{6,7},{7,6},{8,9},{9,8},{10,11... | collective-permute-start | bytes 344072 | tf_op jit(solution)/shard_map/ppermute | solution.py:72
  (28 other events, 287.1 us)

commit v3 on v2

--- a/solution.py
+++ b/solution.py
@@ -36,9 +36,9 @@
         for x in range(SIDE):
             for y in range(SIDE):
                 for c in range(2):
-                    axis, d = step(c)
+                    axis, to_place = step(c)
                     to = {"x": x, "y": y, "z": z}
-                    to[axis] = (to[axis] + d) % SIDE
+                    to[axis] = to_place(to[axis]) % SIDE
                     perm.append(
                         (
                             (z * SIDE + x) * 2 * SIDE + y * 2 + c,
@@ -53,36 +53,35 @@
 
 
 def forth(v, axis):
-    return shift(v, lambda c: (axis, 1 - 2 * c))
+    return shift(v, lambda c: (axis, lambda i: i + 1 - 2 * c))
 
 
 def back(v, axis):
-    return shift(v, lambda c: (axis, 2 * c - 1))
+    return shift(v, lambda c: (axis, lambda i: i + 2 * c - 1))
 
 
 def first(v, d):
-    return shift(v, lambda c: (("x", "z")[c], d))
+    return shift(v, lambda c: (("x", "z")[c], lambda i: i + d))
 
 
 def second(v, d):
-    return shift(v, lambda c: (("z", "x")[c], d))
+    return shift(v, lambda c: (("z", "x")[c], lambda i: i + d))
+
+
+NEAR = ((1, 3), (3, 1))
+
+
+def swap(v, axis, turn):
+    return shift(v, lambda c: (axis, lambda i: i ^ NEAR[c][turn]))
 
 
 def other_core(v):
     return lax.ppermute(v, "head", [(i, i ^ 1) for i in range(2 * SIDE)])
 
 
-def ring(own, axis):
-    one = forth(own, axis)
-    two = back(own, axis)
-    return own, one, two, forth(one, axis)
-
-
-def ring_sum(blocks, axis):
-    far = forth(blocks[3], axis)
-    two = back(blocks[2], axis)
-    one = forth(add_two(blocks[1], far), axis)
-    return blocks[0], one, two
+def gather_pairs(own, axis):
+    pair = stack_two(own, swap(own, axis, 0))
+    return pair, swap(pair, axis, 1)
 
 
 def here():
@@ -91,8 +90,13 @@
     return lax.div(f, SIDE), lax.rem(f, SIDE), lax.div(h, 2), lax.rem(h, 2)
 
 
-def turned(base, s):
-    return [lax.rem(base + d, SIDE) for d in (0, SIDE + s, SIDE - s, 2)]
+def near(core):
+    return jnp.where(core == 0, 1, 3), jnp.where(core == 0, 3, 1)
+
+
+def spots(base, core):
+    one, two = near(core)
+    return [base, base ^ two, base ^ one, base ^ 2]
 
 
 VMEM = pl.BlockSpec(memory_space=pltpu.VMEM)
@@ -106,84 +110,102 @@
     return pltpu.CompilerParams(vmem_limit_bytes=mib * MIB)
 
 
-def add_two_body(a, b, o):
-    o[...] = (a[...].astype(F32) + b[...].astype(F32)).astype(o.dtype)
-
-
-def add_two(a, b):
-    return pl.pallas_call(
-        add_two_body,
+def stack_two_body(a, b, o):
+    o[0] = a[...]
+    o[1] = b[...]
+
+
+def stack_two(a, b):
+    return pl.pallas_call(
+        stack_two_body,
+        in_specs=[VMEM] * 2,
+        out_specs=VMEM,
+        out_shape=jax.ShapeDtypeStruct((2,) + a.shape, a.dtype),
+        compiler_params=room(8),
+        name="stack_two",
+    )(a, b)
+
+
+def add_last_body(a, b, o):
+    o[...] = (a[...].astype(F32) + b[1].astype(F32)).astype(o.dtype)
+
+
+def add_last(a, b):
+    return pl.pallas_call(
+        add_last_body,
         in_specs=[VMEM] * 2,
         out_specs=VMEM,
         out_shape=jax.ShapeDtypeStruct(a.shape, BF16),
         compiler_params=room(8),
-        name="add_two",
+        name="add_last",
     )(a, b)
 
 
-def pack_body(g_ref, send_ref, keep_ref, sem):
+def sum_pairs(own, second_sum, send, axis):
+    got = swap(send, axis, 0)
+    return own, got, swap(add_last(second_sum, got), axis, 1)
+
+
+def pack_body(g_ref, o_ref):
     _, _, y, core = here()
-    sign = 1 - 2 * core
-    cols = send_ref.shape[2]
-    copies = []
-    for ref, ys, c in (
-        (send_ref, turned(y, -sign), 1 - core),
-        (keep_ref, turned(y, sign), core),
-    ):
-        for j in range(SIDE):
-            at = pl.multiple_of((2 * ys[j] + c) * cols, 128)
-            copies.append(
-                pltpu.make_async_copy(
-                    g_ref.at[:, pl.ds(at, cols)], ref.at[j], sem.at[len(copies)]
-                )
-            )
-    for copy in copies:
-        copy.start()
-    for copy in copies:
-        copy.wait()
+    cols = o_ref.shape[2]
+    for j, place in enumerate(spots(y, 1 - core)):
+        at = pl.multiple_of((2 * place + 1 - core) * cols, 128)
+        o_ref[j] = g_ref[:, pl.ds(at, cols)]
 
 
 def pack(g):
-    out = jax.ShapeDtypeStruct((SIDE, g.shape[0], g.shape[1] // (2 * SIDE)), g.dtype)
     return pl.pallas_call(
         pack_body,
-        in_specs=[HBM],
-        out_specs=[VMEM] * 2,
-        out_shape=[out] * 2,
-        scratch_shapes=[pltpu.SemaphoreType.DMA((2 * SIDE,))],
+        in_specs=[VMEM],
+        out_specs=VMEM,
+        out_shape=jax.ShapeDtypeStruct((SIDE, g.shape[0], g.shape[1] // (2 * SIDE)), g.dtype),
         compiler_params=room(8),
         name="pack_columns",
     )(g)
 
 
-def add_body(keep, got, o0, o1, o2, o3):
-    for j, o in ((3, o3), (2, o2), (1, o1), (0, o0)):
-        o[...] = (keep[j].astype(F32) + got[j].astype(F32)).astype(o.dtype)
-
-
-def add_pairs(keep, got, kind):
+def add_columns_body(g_ref, got, own, second_sum, send):
+    _, _, y, core = here()
+    rows, cols = own.shape
+    places = spots(y, core)
+    for j, ref in ((2, send.at[0]), (3, send.at[1]), (1, second_sum), (0, own)):
+        at = pl.multiple_of((2 * places[j] + core) * cols, 128)
+        for r in range(0, rows, 16):
+            part = slice(r, r + 16)
+            mine = g_ref[part, pl.ds(at, cols)].astype(F32)
+            ref[part, :] = (mine + got[j, part, :].astype(F32)).astype(ref.dtype)
+
+
+def add_columns(g, got):
     shape = got.shape[1:]
     return pl.pallas_call(
-        add_body,
+        add_columns_body,
         in_specs=[VMEM] * 2,
-        out_specs=[VMEM] * SIDE,
-        out_shape=[jax.ShapeDtypeStruct(shape, kind)] + [jax.ShapeDtypeStruct(shape, BF16)] * 3,
-        compiler_params=room(8),
-        name="add_pairs",
-    )(keep, got)
+        out_specs=[VMEM] * 3,
+        out_shape=[
+            jax.ShapeDtypeStruct(shape, F32),
+            jax.ShapeDtypeStruct(shape, BF16),
+            jax.ShapeDtypeStruct((2,) + shape, BF16),
+        ],
+        compiler_params=room(8),
+        name="add_columns",
+    )(g, got)
 
 
 def adam_body(r0, r1, r2, p, one, two, new_p, new_one, new_two, w):
-    grad = r0[...] + r1[...].astype(F32) + r2[...].astype(F32)
-    moment = 0.9 * one[...] + 0.1 * grad
-    second_moment = 0.999 * two[...] + 0.001 * grad * grad
     step_size = 0.003 / first_fix
-    denom = jnp.sqrt(second_moment / second_fix) + 1e-08
-    params = p[...] - step_size * moment / denom
-    w[...] = params.astype(BF16)
-    new_p[...] = params
-    new_one[...] = moment
-    new_two[...] = second_moment
+    for r in range(0, p.shape[0], 16):
+        part = slice(r, r + 16)
+        grad = r0[part] + r1[0, part, :].astype(F32) + r2[part].astype(F32)
+        moment = 0.9 * one[part] + 0.1 * grad
+        second_moment = 0.999 * two[part] + 0.001 * grad * grad
+        denom = jnp.sqrt(second_moment / second_fix) + 1e-08
+        params = p[part] - step_size * moment / denom
+        w[part] = params.astype(BF16)
+        new_p[part] = params
+        new_one[part] = moment
+        new_two[part] = second_moment
 
 
 def adam(parts, p, one, two):
@@ -447,7 +469,7 @@
             pltpu.SemaphoreType.DMA((SLOTS,)),
             pltpu.SemaphoreType.DMA((SLOTS,)),
         ],
-        compiler_params=room(36),
+        compiler_params=room(54),
         name="attention",
     )(order, lengths, q_own, q_got, r_own, r_got, nl, nr, lat, rope)
 
@@ -464,9 +486,8 @@
         part = mixed[:, h * steps : (h + 1) * steps, :].reshape(seqs * steps, lat_rank)
         flat[:, cols] = dot(part.astype(BF16), vw_ref[:, cols], NN).astype(BF16)
     _, _, y, core = here()
-    sign = 1 - 2 * core
-    step_of = [2 * v + (1 - core) for v in turned(y, -sign)]
-    step_of += [2 * v + core for v in turned(y, sign)]
+    step_of = [2 * v + (1 - core) for v in spots(y, 1 - core)]
+    step_of += [2 * v + core for v in spots(y, core)]
     count = seqs * steps
     row = lax.broadcasted_iota(jnp.int32, (count, count), 0)
     col = lax.broadcasted_iota(jnp.int32, (count, count), 1)
@@ -500,16 +521,19 @@
 
 
 def output_body(*refs, seqs):
-    tokens, weights = refs[:4], refs[4:8]
-    send_ref, keep_ref, v_buf, w_buf = refs[8:]
+    (pair, other), weights = refs[:2], refs[2:6]
+    send_ref, keep_ref, v_buf, w_buf = refs[6:]
     _, x, _, core = here()
+    one, two = near(core)
+    v_buf[0] = pair[0]
+    v_buf[one] = pair[1]
+    v_buf[two] = other[0]
+    v_buf[2] = other[1]
     sign = 1 - 2 * core
-    offsets = (0, SIDE - sign, SIDE + sign, 2)
     depth = v_buf.shape[2]
     part = weights[0].shape[0]
-    for k in range(SIDE):
-        v_buf[lax.rem(offsets[k], SIDE) if k in (1, 2) else offsets[k]] = tokens[k][...]
-        at = pl.multiple_of(lax.rem(x + offsets[k], SIDE) * part, 64)
+    for k, offset in enumerate((0, SIDE - sign, SIDE + sign, 2)):
+        at = pl.multiple_of(lax.rem(x + offset, SIDE) * part, 64)
         w_buf[pl.ds(at, part), :] = weights[k][...]
     tokens_all = v_buf[...].reshape(-1, depth)
     width = 256
@@ -523,12 +547,12 @@
 
 
 def output_blocks(tokens, weights, seqs):
-    count, depth = tokens[0].shape
+    _, count, depth = tokens[0].shape
     cols = SIDE * weights[0].shape[0]
     out = jax.ShapeDtypeStruct((SIDE, SIDE, seqs, cols), BF16)
     return pl.pallas_call(
         functools.partial(output_body, seqs=seqs),
-        in_specs=[VMEM] * 8,
+        in_specs=[VMEM] * 6,
         out_specs=[VMEM] * 2,
         out_shape=[out] * 2,
         scratch_shapes=[
@@ -540,60 +564,105 @@
     )(*tokens, *weights)
 
 
-def total_body(a, b, c, o0, o1, o2, o3):
-    for j, o in enumerate((o0, o1, o2, o3)):
-        o[...] = (a[j].astype(F32) + b[j].astype(F32) + c[j].astype(F32)).astype(o.dtype)
+def add_blocks_body(keep, got, own, second_sum, send):
+    for j, ref in ((2, send.at[0]), (3, send.at[1]), (1, second_sum), (0, own)):
+        for k in range(SIDE):
+            ref[k] = (keep[j, k].astype(F32) + got[j, k].astype(F32)).astype(ref.dtype)
+
+
+def add_blocks(keep, got):
+    one = jax.ShapeDtypeStruct(got.shape[1:], BF16)
+    return pl.pallas_call(
+        add_blocks_body,
+        in_specs=[VMEM] * 2,
+        out_specs=[VMEM] * 3,
+        out_shape=[one, one, jax.ShapeDtypeStruct((2,) + got.shape[1:], BF16)],
+        compiler_params=room(8),
+        name="add_blocks",
+    )(keep, got)
+
+
+def total_body(a, b, c, own, second_out, send):
+    one, two = near(here()[3])
+
+    def total(k):
+        return (a[k].astype(F32) + b[0, k].astype(F32) + c[k].astype(F32)).astype(BF16)
+
+    send[0] = total(one)
+    send[1] = total(2)
+    second_out[...] = total(two)
+    own[...] = total(0)
 
 
 def total_blocks(parts):
-    out = jax.ShapeDtypeStruct(parts[0].shape[1:], BF16)
+    one = jax.ShapeDtypeStruct(parts[0].shape[1:], BF16)
     return pl.pallas_call(
         total_body,
         in_specs=[VMEM] * 3,
-        out_specs=[VMEM] * SIDE,
-        out_shape=[out] * SIDE,
+        out_specs=[VMEM] * 3,
+        out_shape=[one, one, jax.ShapeDtypeStruct((2,) + one.shape, BF16)],
         compiler_params=room(8),
         name="total_blocks",
     )(*parts)
 
 
-def columns_body(*refs):
-    out = refs[-1]
-    width = refs[0].shape[1]
-    z = here()[0]
-    for d, ref in enumerate(refs[:-1]):
-        at = lax.rem(z + SIDE - d, SIDE) * width
-        out[:, pl.ds(pl.multiple_of(at, 128), width)] = ref[...]
-
-
-def join_columns(blocks):
-    rows, width = blocks[0].shape
+def pass_on_body(a, b, o):
+    o[0] = a[...]
+    o[1] = b[1]
+
+
+def pass_on(a, b):
+    return pl.pallas_call(
+        pass_on_body,
+        in_specs=[VMEM] * 2,
+        out_specs=VMEM,
+        out_shape=jax.ShapeDtypeStruct(b.shape, b.dtype),
+        compiler_params=room(8),
+        name="pass_on",
+    )(a, b)
+
+
+def columns_body(own, got, far, out):
+    width = own.shape[1]
+    z, _, _, core = here()
+    here_z, two, one, opposite = spots(z, core)
+    for place, block in (
+        (here_z, own[...]),
+        (one, got[0]),
+        (two, far[0]),
+        (opposite, far[1]),
+    ):
+        out[:, pl.ds(pl.multiple_of(place * width, 128), width)] = block
+
+
+def join_columns(own, got, far):
+    rows, width = own.shape
     return pl.pallas_call(
         columns_body,
-        in_specs=[VMEM] * SIDE,
+        in_specs=[VMEM] * 3,
         out_specs=VMEM,
         out_shape=jax.ShapeDtypeStruct((rows, SIDE * width), BF16),
         compiler_params=room(8),
         name="join_columns",
-    )(*blocks)
-
-
-def settle_body(*refs):
-    out = refs[-1]
+    )(own, got, far)
+
+
+def settle_body(pair, far, pair_other, far_other, out):
     _, _, y, core = here()
-    sign = 1 - 2 * core
-    steps = [2 * v + core for v in turned(y, -sign)]
-    steps += [2 * v + (1 - core) for v in turned(y, sign)]
-    for step, ref in zip(steps, refs[:-1]):
-        out[step] = ref[...]
+    for a, b, c in ((pair, far, core), (pair_other, far_other, 1 - core)):
+        here_y, two, one, opposite = spots(y, c)
+        out[2 * here_y + c] = a[0]
+        out[2 * one + c] = a[1]
+        out[2 * two + c] = b[0]
+        out[2 * opposite + c] = b[1]
 
 
 def settle(blocks):
     return pl.pallas_call(
         settle_body,
-        in_specs=[VMEM] * 8,
+        in_specs=[VMEM] * 4,
         out_specs=VMEM,
-        out_shape=jax.ShapeDtypeStruct((8,) + blocks[0].shape, BF16),
+        out_shape=jax.ShapeDtypeStruct((8,) + blocks[0].shape[1:], BF16),
         compiler_params=room(8),
         name="settle",
     )(*blocks)
@@ -653,28 +722,27 @@
 ):
     core = lax.rem(lax.axis_index("head"), 2)
 
-    send, keep = pack(grad_parts[0])
-    sums = add_pairs(keep, other_core(send), F32)
-    parts = ring_sum(sums, "y")
+    grad = grad_parts[0]
+    own_sum, second_sum, send_sum = add_columns(grad, other_core(pack(grad)))
+    parts = sum_pairs(own_sum, second_sum, send_sum, "y")
     new_params, new_one, new_two, w = adam(parts, params, moment_one, moment_two)
 
     w_t = out_weight.T
     w_one, w_two = forth(w_t, "x"), back(w_t, "x")
-    w_one, w = lax.optimization_barrier((w_one, w))
 
     above, below = first(w, 1), first(w, -1)
     top = stack_rows(w, above)
     bottom = stack_rows(below, first(above, 1))
     top_above, top_below = second(top, 1), second(top, -1)
     bottom_above, bottom_below = second(bottom, 1), second(bottom, -1)
+    bottom_on, top_above = lax.optimization_barrier((bottom_above, top_above))
     units = [top, bottom, top_above, bottom_above, top_below, bottom_below]
-    units += [second(top_above, 1), second(bottom_below, -1)]
-    out_weights = (w_t, w_one, w_two, forth(w_one, "x"))
+    units += [second(top_below, -1), second(bottom_on, 1)]
 
     steps_n, seq_local, q_rank = query_latent.shape
     heads_local = value_weight.shape[1] // HDIM
     half = seq_local // 2
-    lengths, _ = lax.optimization_barrier((lengths, sums[3]))
+    lengths, _ = lax.optimization_barrier((lengths, send_sum))
     order = balanced_order(lengths)
     order = jnp.where(core == 0, order, jnp.concatenate([order[half:], order[:half]]))
     chosen = order[:, None] == jnp.arange(seq_local, dtype=jnp.int32)[None, :]
@@ -703,6 +771,8 @@
 
     w_rows = SIDE * SIDE * params.shape[0]
     q_own, q_send = queries(by_seq, units, w_rows, seq_local, q_rank)
+    w_one, q_send = lax.optimization_barrier((w_one, q_send))
+    out_weights = (w_t, w_one, w_two, forth(w_one, "x"))
     mixed, mixed_send = attention(
         order,
         lengths_in[:half],
@@ -718,23 +788,16 @@
     )
     values = project_values(order, mixed, other_core(mixed_send), value_weight)
 
-    send, keep = output_blocks(ring(values, "z"), out_weights, seq_local)
-    parts = ring_sum(add_pairs(keep, other_core(send), BF16), "y")
-    blocks = total_blocks(parts)
-
-    arrived = [blocks[0]]
-    for d in range(1, SIDE):
-        perm = [
-            (zz * SIDE + xx, ((zz + d) % SIDE) * SIDE + xx)
-            for zz in range(SIDE)
-            for xx in range(SIDE)
-        ]
-        arrived.append(lax.ppermute(blocks[d], "fsdp", perm))
-    mine = join_columns(arrived)
-
-    column = list(ring(mine, "y"))
-    column += [other_core(b) for b in column]
-    decoded = settle(column)
+    send, keep = output_blocks(gather_pairs(values, "z"), out_weights, seq_local)
+    parts = sum_pairs(*add_blocks(keep, other_core(send)), "y")
+    own, second_out, send = total_blocks(parts)
+
+    got = swap(send, "z", 0)
+    far = swap(pass_on(second_out, got), "z", 1)
+    mine = join_columns(own, got, far)
+
+    pair, far = gather_pairs(mine, "y")
+    decoded = settle((pair, far, other_core(pair), other_core(far)))
     return (new_params, new_one, new_two, decoded)
 
 

time: 149 us -> 154 us (1.034); the launches traced: 148 us -> 151 us
  waiting for transfers between devices: 40.3 us -> 61.1 us
  starting transfers between devices: 62.4 us -> 45.9 us
  Pallas kernels: 30.9 us -> 27.2 us
  local copies, waits for them, and re-layouts: 7.33 us -> 9.27 us
    ppermute x24 -> x22, waiting for transfers between devices: 33.5 us -> 57.2 us  [shift(): return lax.ppermute(v, ('fsdp', 'head'), moves(step))]
    ppermute x24 -> x22, starting transfers between devices: 38.9 us -> 21.1 us  [shift(): return lax.ppermute(v, ('fsdp', 'head'), moves(step))]
    ppermute x9 -> x7, starting transfers between devices: 20.8 us -> 24.8 us  [other_core(): return lax.ppermute(v, 'head', [(i, i ^ 1) for i in range(2 * SIDE)])]
    ppermute x3 -> x0, starting transfers between devices: 2.74 us -> none  [body(): arrived.append(lax.ppermute(blocks[d], 'fsdp', perm))]
    pallas_call x1, Pallas kernels: 18.6 us -> 16.2 us  [attention(): pl.pallas_call(functools.partial(attention_body, steps=steps), in_specs=[...]
    ppermute x3 -> x0, waiting for transfers between devices: 2.14 us -> none  [body(): arrived.append(lax.ppermute(blocks[d], 'fsdp', perm))]
    pallas_call x8 -> x11, Pallas kernels: 4.05 us -> 2.63 us  [the longest x1 1.08 us: pack(): pl.pallas_call(pack_body, in_specs=[VMEM], out_specs=VMEM, out_shape=jax....]
    ppermute x9 -> x7, waiting for transfers between devices: 4.7 us -> 3.94 us  [other_core(): return lax.ppermute(v, 'head', [(i, i ^ 1) for i in range(2 * SIDE)])]
  transfers between devices with their start and end apart: 36 -> 29, of which waited for: 23 -> 19; matrix products, arithmetic and copies ran while one was open for 6% -> 7% of each run, Pallas kernels for 17% -> 14%
where the time goes in v3:
time: 154 us; the launch traced here: 151 us
  waiting for transfers between devices  61.1 us (40%)
  starting transfers between devices  45.9 us (30%)
  Pallas kernels  27.2 us (18%)
  local copies, waits for them, and re-layouts  9.27 us (6%)
  other arithmetic  5.62 us (4%)
    ppermute x22, waiting for transfers between devices, shift(): return lax.ppermute(v, ('fsdp', 'head'), moves(step))  57.2 us
    ppermute x7, starting transfers between devices, other_core(): return lax.ppermute(v, 'head', [(i, i ^ 1) for i in range(2 * SIDE)])  24.8 us
    ppermute x22, starting transfers between devices, shift(): return lax.ppermute(v, ('fsdp', 'head'), moves(step))  21.1 us
    pallas_call x1, Pallas kernels, attention(): pl.pallas_call(functools.partial(attention_body, steps=steps), in_specs=[...  16.2 us
    unnamed x40, local copies, waits for them, and re-layouts  5.03 us
    ppermute x7, waiting for transfers between devices, other_core(): return lax.ppermute(v, 'head', [(i, i ^ 1) for i in range(2 * SIDE)])  3.94 us
    pallas_call x1, Pallas kernels, output_blocks(): pl.pallas_call(functools.partial(output_body, seqs=seqs), in_specs=[VMEM]...  3.37 us
  transfers between devices with their start and end apart: 29, of which 19 were waited for; matrix products, arithmetic and copies ran while one was open for 7% of the time, Pallas kernels for 14%

profile of v3, /device:TPU:1, one launch (start us, length us, event | category | flops | bytes accessed | tf_op | source)
XLA Modules:
  0.0 151.0 jit_solution(473112140434457797)
XLA Ops:
  4.9 2.6 %collective-permute-start.12 = (bf16[448,1024]{1,0:T(8,128)(2,1)}, bf16[448,1024]{1,0:T(8,128)(2,1)}, u32[]{:S(2)}, u32[]{:S(2)}) collective-permute-start(bf16[448,1024]{1,0:T(8,128)(2,1)} %bitcast.3.refs_2_), channel_id=1, source_target_pairs={{0,8},{1,25},{2,10},{3,27},{4,12},{5,29},{6,14},{7,31},{8,16},{9,1... | collective-permute-start | bytes 2752520 | tf_op jit(solution)/shard_map/ppermute | solution.py:52
  9.3 2.8 %collective-permute-start.1 = (bf16[2,128,1024]{2,1,0:T(8,128)(2,1)S(1)}, bf16[2,128,1024]{2,1,0:T(8,128)(2,1)S(1)}, u32[]{:S(2)}, u32[]{:S(2)}) collective-permute-start(bf16[2,128,1024]{2,1,0:T(8,128)(2,1)S(1)} %get-tuple-element.31), channel_id=1, source_target_pairs={{0,2},{1,7},{2,0},{3,5},{4,6},{5,3},{6,4},{7,1},{8,10},{9,15},{10,... | collective-permute-start | bytes 1572872 | tf_op jit(solution)/shard_map/ppermute | solution.py:52
  15.6 3.5 %collective-permute-done.1.b.r1 = bf16[2,128,1024]{2,1,0:T(8,128)(2,1)S(1)} collective-permute-done((bf16[2,128,1024]{2,1,0:T(8,128)(2,1)S(1)}, bf16[2,128,1024]{2,1,0:T(8,128)(2,1)S(1)}, u32[]{:S(2)}, u32[]{:S(2)}) %collective-permute-start.1) | collective-permute-done | bytes 524320 | tf_op jit(solution)/shard_map/ppermute | solution.py:52
  19.5 5.4 %collective-permute-done.2.r2 = bf16[128,1024]{1,0:T(8,128)(2,1)S(1)} collective-permute-done((bf16[128,1024]{1,0:T(8,128)(2,1)S(1)}, bf16[128,1024]{1,0:T(8,128)(2,1)S(1)}, u32[]{:S(2)}, u32[]{:S(2)}) %collective-permute-start.2) | collective-permute-done | bytes 262176 | tf_op jit(solution)/shard_map/ppermute | solution.py:52
  30.3 3.8 %collective-permute-done.3.b = bf16[128,1024]{1,0:T(8,128)(2,1)S(1)} collective-permute-done((bf16[128,1024]{1,0:T(8,128)(2,1)S(1)}, bf16[128,1024]{1,0:T(8,128)(2,1)S(1)}, u32[]{:S(2)}, u32[]{:S(2)}) %collective-permute-start.3) | collective-permute-done | bytes 262176 | tf_op jit(solution)/shard_map/ppermute | solution.py:52
  37.4 3.4 %collective-permute-done.5.b = bf16[128,1024]{1,0:T(8,128)(2,1)S(1)} collective-permute-done((bf16[128,1024]{1,0:T(8,128)(2,1)S(1)}, bf16[128,1024]{1,0:T(8,128)(2,1)S(1)}, u32[]{:S(2)}, u32[]{:S(2)}) %collective-permute-start.5) | collective-permute-done | bytes 262176 | tf_op jit(solution)/shard_map/ppermute | solution.py:52
  43.3 3.7 %collective-permute-done.7.refs_2_ = bf16[256,1024]{1,0:T(8,128)(2,1)S(1)} collective-permute-done((bf16[256,1024]{1,0:T(8,128)(2,1)S(1)}, bf16[256,1024]{1,0:T(8,128)(2,1)S(1)}, u32[]{:S(2)}, u32[]{:S(2)}) %collective-permute-start.7) | collective-permute-done | bytes 524320 | tf_op jit(solution)/shard_map/ppermute | solution.py:52
  48.6 4.1 %collective-permute-done.6.refs_3_ = bf16[256,1024]{1,0:T(8,128)(2,1)} collective-permute-done((bf16[256,1024]{1,0:T(8,128)(2,1)S(1)}, bf16[256,1024]{1,0:T(8,128)(2,1)}, u32[]{:S(2)}, u32[]{:S(2)}) %collective-permute-start.6) | collective-permute-done | bytes 524320 | tf_op jit(solution)/shard_map/ppermute | solution.py:52
  55.4 5.5 %collective-permute-done.10.refs_6_ = bf16[256,1024]{1,0:T(8,128)(2,1)S(1)} collective-permute-done((bf16[256,1024]{1,0:T(8,128)(2,1)}, bf16[256,1024]{1,0:T(8,128)(2,1)S(1)}, u32[]{:S(2)}, u32[]{:S(2)}) %collective-permute-start.10) | collective-permute-done | bytes 524320 | tf_op jit(solution)/shard_map/ppermute | solution.py:52
  62.2 2.5 %queries.1 = (bf16[4,64,512]{2,1,0:T(8,128)(2,1)S(1)}, bf16[4,64,512]{2,1,0:T(8,128)(2,1)S(1)}) custom-call(bf16[64,1536]{1,0:T(8,128)(2,1)S(1)} %bitcast.28, bf16[256,1024]{1,0:T(8,128)(2,1)S(1)} %stack_rows.2.refs_0_, bf16[256,1024]{1,0:T(8,128)(2,1)S(1)} %stack_rows.3.refs_1_, bf16[256,1024]{1,0:T(8,128)(2,1)S(1)} %collective-permute-done.7.refs_2_, ...), custom_call_target="tpu_custom_call" | custom-call | tf_op jit(solution)/shard_map/queries/pallas_call | solution.py:270
  64.7 6.4 %collective-permute-start.13 = (bf16[4,64,512]{2,1,0:T(8,128)(2,1)S(1)}, bf16[4,64,512]{2,1,0:T(8,128)(2,1)S(1)}, u32[]{:S(2)}, u32[]{:S(2)}) collective-permute-start(bf16[4,64,512]{2,1,0:T(8,128)(2,1)S(1)} %get-tuple-element.42), channel_id=1, source_target_pairs={{0,1},{1,0},{2,3},{3,2},{4,5},{5,4},{6,7},{7,6},{8,9},{9,8},{10,11... | collective-permute-start | bytes 786440 | tf_op jit(solution)/shard_map/ppermute | solution.py:79
  74.3 16.2 %attention.1 = (bf16[4,64,512]{2,1,0:T(8,128)(2,1)}, bf16[4,64,512]{2,1,0:T(8,128)(2,1)}) custom-call(s32[8]{0:T(128)} %copy-done.9, s32[4]{0:T(128)} %bitcast.29, bf16[4,64,512]{2,1,0:T(8,128)(2,1)} %copy-done.7, bf16[4,64,512]{2,1,0:T(8,128)(2,1)} %copy-done.11, bf16[4,64,64]{2,1,0:T(8,128)(2,1)} %get-tuple-element.63.r_own, ...), custom_call_target="tpu_custom_call" | custom-call | tf_op jit(solution)/shard_map/attention/pallas_call | solution.py:450
  95.1 5.0 %collective-permute-done.16.b = bf16[64,1024]{1,0:T(8,128)(2,1)S(1)} collective-permute-done((bf16[64,1024]{1,0:T(8,128)(2,1)S(1)}, bf16[64,1024]{1,0:T(8,128)(2,1)S(1)}, u32[]{:S(2)}, u32[]{:S(2)}) %collective-permute-start.16) | collective-permute-done | bytes 131104 | tf_op jit(solution)/shard_map/ppermute | solution.py:52
  101.4 4.4 %collective-permute-done.17.refs_1_ = bf16[2,64,1024]{2,1,0:T(8,128)(2,1)S(1)} collective-permute-done((bf16[2,64,1024]{2,1,0:T(8,128)(2,1)S(1)}, bf16[2,64,1024]{2,1,0:T(8,128)(2,1)S(1)}, u32[]{:S(2)}, u32[]{:S(2)}) %collective-permute-start.17) | collective-permute-done | bytes 262176 | tf_op jit(solution)/shard_map/ppermute | solution.py:52
  105.8 3.4 %output_blocks.1 = (bf16[4,4,8,1792]{3,2,1,0:T(8,128)(2,1)S(1)}, bf16[4,4,8,1792]{3,2,1,0:T(8,128)(2,1)S(1)}) custom-call(bf16[2,64,1024]{2,1,0:T(8,128)(2,1)S(1)} %stack_two.2.refs_0_, bf16[2,64,1024]{2,1,0:T(8,128)(2,1)S(1)} %collective-permute-done.17.refs_1_, bf16[448,1024]{1,0:T(8,128)(2,1)} %bitcast.3.refs_2_, ...), custom_call_target="tpu_custom_call" | custom-call | tf_op jit(solution)/shard_map/output_blocks/pallas_call | solution.py:553
  109.1 2.5 %collective-permute-start.20 = (bf16[4,4,8,1792]{3,2,1,0:T(8,128)(2,1)S(1)}, bf16[4,4,8,1792]{3,2,1,0:T(8,128)(2,1)S(1)}, u32[]{:S(2)}, u32[]{:S(2)}) collective-permute-start(bf16[4,4,8,1792]{3,2,1,0:T(8,128)(2,1)S(1)} %get-tuple-element.49), channel_id=1, source_target_pairs={{0,1},{1,0},{2,3},{3,2},{4,5},{5,4},{6,7},{7,6},{8,9},{9,8},{10,11... | collective-permute-start | bytes 1376264 | tf_op jit(solution)/shard_map/ppermute | solution.py:79
  113.2 2.8 %collective-permute-start.21 = (bf16[2,4,8,1792]{3,2,1,0:T(8,128)(2,1)S(1)}, bf16[2,4,8,1792]{3,2,1,0:T(8,128)(2,1)S(1)}, u32[]{:S(2)}, u32[]{:S(2)}) collective-permute-start(bf16[2,4,8,1792]{3,2,1,0:T(8,128)(2,1)S(1)} %get-tuple-element.51), channel_id=1, source_target_pairs={{0,2},{1,7},{2,0},{3,5},{4,6},{5,3},{6,4},{7,1},{8,10},{9,15},{10,... | collective-permute-start | bytes 688136 | tf_op jit(solution)/shard_map/ppermute | solution.py:52
  116.0 3.4 %collective-permute-done.21.b = bf16[2,4,8,1792]{3,2,1,0:T(8,128)(2,1)S(1)} collective-permute-done((bf16[2,4,8,1792]{3,2,1,0:T(8,128)(2,1)S(1)}, bf16[2,4,8,1792]{3,2,1,0:T(8,128)(2,1)S(1)}, u32[]{:S(2)}, u32[]{:S(2)}) %collective-permute-start.21) | collective-permute-done | bytes 229408 | tf_op jit(solution)/shard_map/ppermute | solution.py:52
  119.6 3.6 %collective-permute-done.22.c = bf16[4,8,1792]{2,1,0:T(8,128)(2,1)S(1)} collective-permute-done((bf16[4,8,1792]{2,1,0:T(8,128)(2,1)S(1)}, bf16[4,8,1792]{2,1,0:T(8,128)(2,1)S(1)}, u32[]{:S(2)}, u32[]{:S(2)}) %collective-permute-start.22) | collective-permute-done | bytes 114720 | tf_op jit(solution)/shard_map/ppermute | solution.py:52
  123.3 4.2 %collective-permute-done.23.b.got = bf16[2,8,1792]{2,1,0:T(8,128)(2,1)S(1)} collective-permute-done((bf16[2,8,1792]{2,1,0:T(8,128)(2,1)S(1)}, bf16[2,8,1792]{2,1,0:T(8,128)(2,1)S(1)}, u32[]{:S(2)}, u32[]{:S(2)}) %collective-permute-start.23) | collective-permute-done | bytes 57376 | tf_op jit(solution)/shard_map/ppermute | solution.py:52
  127.6 3.0 %collective-permute-done.24.far = bf16[2,8,1792]{2,1,0:T(8,128)(2,1)S(1)} collective-permute-done((bf16[2,8,1792]{2,1,0:T(8,128)(2,1)S(1)}, bf16[2,8,1792]{2,1,0:T(8,128)(2,1)S(1)}, u32[]{:S(2)}, u32[]{:S(2)}) %collective-permute-start.24) | collective-permute-done | bytes 57376 | tf_op jit(solution)/shard_map/ppermute | solution.py:52
  130.6 2.8 %collective-permute-start.25 = (bf16[8,7168]{1,0:T(8,128)(2,1)S(1)}, bf16[8,7168]{1,0:T(8,128)(2,1)S(1)}, u32[]{:S(2)}, u32[]{:S(2)}) collective-permute-start(bf16[8,7168]{1,0:T(8,128)(2,1)S(1)} %join_columns.1.a), channel_id=1, source_target_pairs={{0,2},{1,7},{2,0},{3,5},{4,6},{5,3},{6,4},{7,1},{8,10},{9,15},{10,... | collective-permute-start | bytes 344072 | tf_op jit(solution)/shard_map/ppermute | solution.py:52
  135.6 9.0 %collective-permute-start.27 = (bf16[2,8,7168]{2,1,0:T(8,128)(2,1)S(1)}, bf16[2,8,7168]{2,1,0:T(8,128)(2,1)S(1)}, u32[]{:S(2)}, u32[]{:S(2)}) collective-permute-start(bf16[2,8,7168]{2,1,0:T(8,128)(2,1)S(1)} %stack_two.3.pair), channel_id=1, source_target_pairs={{0,1},{1,0},{2,3},{3,2},{4,5},{5,4},{6,7},{7,6},{8,9},{9,8},{10,11... | collective-permute-start | bytes 688136 | tf_op jit(solution)/shard_map/ppermute | solution.py:79
  144.7 4.2 %collective-permute-start.28 = (bf16[2,8,7168]{2,1,0:T(8,128)(2,1)S(1)}, bf16[2,8,7168]{2,1,0:T(8,128)(2,1)S(1)}, u32[]{:S(2)}, u32[]{:S(2)}) collective-permute-start(bf16[2,8,7168]{2,1,0:T(8,128)(2,1)S(1)} %collective-permute-done.26.far), channel_id=1, source_target_pairs={{0,1},{1,0},{2,3},{3,2},{4,5},{5,4},{6,7},{7,6},{8,9},{9,8},{10,11... | collective-permute-start | bytes 688136 | tf_op jit(solution)/shard_map/ppermute | solution.py:79
  (118 shorter events, 41.7 us)
Async XLA Ops:
  3.4 4.0 %collective-permute-start = (bf16[4,128,1024]{2,1,0:T(8,128)(2,1)}, bf16[4,128,1024]{2,1,0:T(8,128)(2,1)S(1)}, u32[]{:S(2)}, u32[]{:S(2)}) collective-permute-start(bf16[4,128,1024]{2,1,0:T(8,128)(2,1)} %pack_columns.1), channel_id=1, source_target_pairs={{0,1},{1,0},{2,3},{3,2},{4,5},{5,4},{6,7},{7,6},{8,9},{9,8},{10,11... | collective-permute-start | bytes 3145736 | tf_op jit(solution)/shard_map/ppermute | solution.py:79
  4.9 59.9 %collective-permute-start.12 = (bf16[448,1024]{1,0:T(8,128)(2,1)}, bf16[448,1024]{1,0:T(8,128)(2,1)}, u32[]{:S(2)}, u32[]{:S(2)}) collective-permute-start(bf16[448,1024]{1,0:T(8,128)(2,1)} %bitcast.3.refs_2_), channel_id=1, source_target_pairs={{0,8},{1,25},{2,10},{3,27},{4,12},{5,29},{6,14},{7,31},{8,16},{9,1... | collective-permute-start | bytes 2752520 | tf_op jit(solution)/shard_map/ppermute | solution.py:52
  7.4 93.9 %collective-permute-start.18 = (bf16[448,1024]{1,0:T(8,128)(2,1)}, bf16[448,1024]{1,0:T(8,128)(2,1)}, u32[]{:S(2)}, u32[]{:S(2)}) collective-permute-start(bf16[448,1024]{1,0:T(8,128)(2,1)} %bitcast.3.refs_2_), channel_id=1, source_target_pairs={{0,24},{1,9},{2,26},{3,11},{4,28},{5,13},{6,30},{7,15},{8,0},{9,17... | collective-permute-start | bytes 2752520 | tf_op jit(solution)/shard_map/ppermute | solution.py:52
  9.3 9.8 %collective-permute-start.1 = (bf16[2,128,1024]{2,1,0:T(8,128)(2,1)S(1)}, bf16[2,128,1024]{2,1,0:T(8,128)(2,1)S(1)}, u32[]{:S(2)}, u32[]{:S(2)}) collective-permute-start(bf16[2,128,1024]{2,1,0:T(8,128)(2,1)S(1)} %get-tuple-element.31), channel_id=1, source_target_pairs={{0,2},{1,7},{2,0},{3,5},{4,6},{5,3},{6,4},{7,1},{8,10},{9,15},{10,... | collective-permute-start | bytes 1572872 | tf_op jit(solution)/shard_map/ppermute | solution.py:52
  19.2 5.7 %collective-permute-start.2 = (bf16[128,1024]{1,0:T(8,128)(2,1)S(1)}, bf16[128,1024]{1,0:T(8,128)(2,1)S(1)}, u32[]{:S(2)}, u32[]{:S(2)}) collective-permute-start(bf16[128,1024]{1,0:T(8,128)(2,1)S(1)} %add_last.2), channel_id=1, source_target_pairs={{0,6},{1,3},{2,4},{3,1},{4,2},{5,7},{6,0},{7,5},{8,14},{9,11},{10,... | collective-permute-start | bytes 786440 | tf_op jit(solution)/shard_map/ppermute | solution.py:52
  26.3 7.8 %collective-permute-start.3 = (bf16[128,1024]{1,0:T(8,128)(2,1)S(1)}, bf16[128,1024]{1,0:T(8,128)(2,1)S(1)}, u32[]{:S(2)}, u32[]{:S(2)}) collective-permute-start(bf16[128,1024]{1,0:T(8,128)(2,1)S(1)} %get-tuple-element.37.a), channel_id=1, source_target_pairs={{0,8},{1,33},{2,10},{3,35},{4,12},{5,37},{6,14},{7,39},{8,16},{9,4... | collective-permute-start | bytes 786440 | tf_op jit(solution)/shard_map/ppermute | solution.py:52
  28.1 7.0 %collective-permute-start.4 = (bf16[128,1024]{1,0:T(8,128)(2,1)S(1)}, bf16[128,1024]{1,0:T(8,128)(2,1)S(1)}, u32[]{:S(2)}, u32[]{:S(2)}) collective-permute-start(bf16[128,1024]{1,0:T(8,128)(2,1)S(1)} %get-tuple-element.37.a), channel_id=1, source_target_pairs={{0,24},{1,97},{2,26},{3,99},{4,28},{5,101},{6,30},{7,103},{8,0},{9... | collective-permute-start | bytes 786440 | tf_op jit(solution)/shard_map/ppermute | solution.py:52
  34.1 6.7 %collective-permute-start.5 = (bf16[128,1024]{1,0:T(8,128)(2,1)S(1)}, bf16[128,1024]{1,0:T(8,128)(2,1)S(1)}, u32[]{:S(2)}, u32[]{:S(2)}) collective-permute-start(bf16[128,1024]{1,0:T(8,128)(2,1)S(1)} %collective-permute-done.3.b), channel_id=1, source_target_pairs={{0,8},{1,33},{2,10},{3,35},{4,12},{5,37},{6,14},{7,39},{8,16},{9,4... | collective-permute-start | bytes 786440 | tf_op jit(solution)/shard_map/ppermute | solution.py:52
  34.6 12.4 %collective-permute-start.7 = (bf16[256,1024]{1,0:T(8,128)(2,1)S(1)}, bf16[256,1024]{1,0:T(8,128)(2,1)S(1)}, u32[]{:S(2)}, u32[]{:S(2)}) collective-permute-start(bf16[256,1024]{1,0:T(8,128)(2,1)S(1)} %stack_rows.2.refs_0_), channel_id=1, source_target_pairs={{0,32},{1,9},{2,34},{3,11},{4,36},{5,13},{6,38},{7,15},{8,40},{9,1... | collective-permute-start | bytes 1572872 | tf_op jit(solution)/shard_map/ppermute | solution.py:52
  35.2 13.4 %collective-permute-start.8 = (bf16[256,1024]{1,0:T(8,128)(2,1)S(1)}, bf16[256,1024]{1,0:T(8,128)(2,1)}, u32[]{:S(2)}, u32[]{:S(2)}) collective-permute-start(bf16[256,1024]{1,0:T(8,128)(2,1)S(1)} %stack_rows.2.refs_0_), channel_id=1, source_target_pairs={{0,96},{1,25},{2,98},{3,27},{4,100},{5,29},{6,102},{7,31},{8,104},... | collective-permute-start | bytes 1572872 | tf_op jit(solution)/shard_map/ppermute | solution.py:52
  40.8 11.9 %collective-permute-start.6 = (bf16[256,1024]{1,0:T(8,128)(2,1)S(1)}, bf16[256,1024]{1,0:T(8,128)(2,1)}, u32[]{:S(2)}, u32[]{:S(2)}) collective-permute-start(bf16[256,1024]{1,0:T(8,128)(2,1)S(1)} %stack_rows.3.refs_1_), channel_id=1, source_target_pairs={{0,32},{1,9},{2,34},{3,11},{4,36},{5,13},{6,38},{7,15},{8,40},{9,1... | collective-permute-start | bytes 1572872 | tf_op jit(solution)/shard_map/ppermute | solution.py:52
  47.0 8.4 %collective-permute-start.9 = (bf16[256,1024]{1,0:T(8,128)(2,1)S(1)}, bf16[256,1024]{1,0:T(8,128)(2,1)S(1)}, u32[]{:S(2)}, u32[]{:S(2)}) collective-permute-start(bf16[256,1024]{1,0:T(8,128)(2,1)S(1)} %stack_rows.3.refs_1_), channel_id=1, source_target_pairs={{0,96},{1,25},{2,98},{3,27},{4,100},{5,29},{6,102},{7,31},{8,104},... | collective-permute-start | bytes 1572872 | tf_op jit(solution)/shard_map/ppermute | solution.py:52
  48.6 12.4 %collective-permute-start.10 = (bf16[256,1024]{1,0:T(8,128)(2,1)}, bf16[256,1024]{1,0:T(8,128)(2,1)S(1)}, u32[]{:S(2)}, u32[]{:S(2)}) collective-permute-start(bf16[256,1024]{1,0:T(8,128)(2,1)} %collective-permute-done.8.refs_4_), channel_id=1, source_target_pairs={{0,96},{1,25},{2,98},{3,27},{4,100},{5,29},{6,102},{7,31},{8,104},... | collective-permute-start | bytes 1572872 | tf_op jit(solution)/shard_map/ppermute | solution.py:52
  52.7 9.5 %collective-permute-start.11 = (bf16[256,1024]{1,0:T(8,128)(2,1)}, bf16[256,1024]{1,0:T(8,128)(2,1)S(1)}, u32[]{:S(2)}, u32[]{:S(2)}) collective-permute-start(bf16[256,1024]{1,0:T(8,128)(2,1)} %collective-permute-done.6.refs_3_), channel_id=1, source_target_pairs={{0,32},{1,9},{2,34},{3,11},{4,36},{5,13},{6,38},{7,15},{8,40},{9,1... | collective-permute-start | bytes 1572872 | tf_op jit(solution)/shard_map/ppermute | solution.py:52
  64.7 8.8 %collective-permute-start.13 = (bf16[4,64,512]{2,1,0:T(8,128)(2,1)S(1)}, bf16[4,64,512]{2,1,0:T(8,128)(2,1)S(1)}, u32[]{:S(2)}, u32[]{:S(2)}) collective-permute-start(bf16[4,64,512]{2,1,0:T(8,128)(2,1)S(1)} %get-tuple-element.42), channel_id=1, source_target_pairs={{0,1},{1,0},{2,3},{3,2},{4,5},{5,4},{6,7},{7,6},{8,9},{9,8},{10,11... | collective-permute-start | bytes 786440 | tf_op jit(solution)/shard_map/ppermute | solution.py:79
  71.1 30.2 %collective-permute-start.19 = (bf16[448,1024]{1,0:T(8,128)(2,1)}, bf16[448,1024]{1,0:T(8,128)(2,1)S(1)}, u32[]{:S(2)}, u32[]{:S(2)}) collective-permute-start(bf16[448,1024]{1,0:T(8,128)(2,1)} %collective-permute-done.12.refs_3_), channel_id=1, source_target_pairs={{0,8},{1,25},{2,10},{3,27},{4,12},{5,29},{6,14},{7,31},{8,16},{9,1... | collective-permute-start | bytes 2752520 | tf_op jit(solution)/shard_map/ppermute | solution.py:52
  95.0 5.1 %collective-permute-start.16 = (bf16[64,1024]{1,0:T(8,128)(2,1)S(1)}, bf16[64,1024]{1,0:T(8,128)(2,1)S(1)}, u32[]{:S(2)}, u32[]{:S(2)}) collective-permute-start(bf16[64,1024]{1,0:T(8,128)(2,1)S(1)} %project_values.1.a), channel_id=1, source_target_pairs={{0,32},{1,97},{2,34},{3,99},{4,36},{5,101},{6,38},{7,103},{8,40},{... | collective-permute-start | bytes 393224 | tf_op jit(solution)/shard_map/ppermute | solution.py:52
  100.2 5.6 %collective-permute-start.17 = (bf16[2,64,1024]{2,1,0:T(8,128)(2,1)S(1)}, bf16[2,64,1024]{2,1,0:T(8,128)(2,1)S(1)}, u32[]{:S(2)}, u32[]{:S(2)}) collective-permute-start(bf16[2,64,1024]{2,1,0:T(8,128)(2,1)S(1)} %stack_two.2.refs_0_), channel_id=1, source_target_pairs={{0,96},{1,33},{2,98},{3,35},{4,100},{5,37},{6,102},{7,39},{8,104},... | collective-permute-start | bytes 786440 | tf_op jit(solution)/shard_map/ppermute | solution.py:52
  113.2 6.2 %collective-permute-start.21 = (bf16[2,4,8,1792]{3,2,1,0:T(8,128)(2,1)S(1)}, bf16[2,4,8,1792]{3,2,1,0:T(8,128)(2,1)S(1)}, u32[]{:S(2)}, u32[]{:S(2)}) collective-permute-start(bf16[2,4,8,1792]{3,2,1,0:T(8,128)(2,1)S(1)} %get-tuple-element.51), channel_id=1, source_target_pairs={{0,2},{1,7},{2,0},{3,5},{4,6},{5,3},{6,4},{7,1},{8,10},{9,15},{10,... | collective-permute-start | bytes 688136 | tf_op jit(solution)/shard_map/ppermute | solution.py:52
  123.2 4.3 %collective-permute-start.23 = (bf16[2,8,1792]{2,1,0:T(8,128)(2,1)S(1)}, bf16[2,8,1792]{2,1,0:T(8,128)(2,1)S(1)}, u32[]{:S(2)}, u32[]{:S(2)}) collective-permute-start(bf16[2,8,1792]{2,1,0:T(8,128)(2,1)S(1)} %get-tuple-element.54), channel_id=1, source_target_pairs={{0,32},{1,97},{2,34},{3,99},{4,36},{5,101},{6,38},{7,103},{8,40},{... | collective-permute-start | bytes 172040 | tf_op jit(solution)/shard_map/ppermute | solution.py:52
  130.6 4.9 %collective-permute-start.25 = (bf16[8,7168]{1,0:T(8,128)(2,1)S(1)}, bf16[8,7168]{1,0:T(8,128)(2,1)S(1)}, u32[]{:S(2)}, u32[]{:S(2)}) collective-permute-start(bf16[8,7168]{1,0:T(8,128)(2,1)S(1)} %join_columns.1.a), channel_id=1, source_target_pairs={{0,2},{1,7},{2,0},{3,5},{4,6},{5,3},{6,4},{7,1},{8,10},{9,15},{10,... | collective-permute-start | bytes 344072 | tf_op jit(solution)/shard_map/ppermute | solution.py:52
  135.6 9.1 %collective-permute-start.26 = (bf16[2,8,7168]{2,1,0:T(8,128)(2,1)S(1)}, bf16[2,8,7168]{2,1,0:T(8,128)(2,1)S(1)}, u32[]{:S(2)}, u32[]{:S(2)}) collective-permute-start(bf16[2,8,7168]{2,1,0:T(8,128)(2,1)S(1)} %stack_two.3.pair), channel_id=1, source_target_pairs={{0,6},{1,3},{2,4},{3,1},{4,2},{5,7},{6,0},{7,5},{8,14},{9,11},{10,... | collective-permute-start | bytes 688136 | tf_op jit(solution)/shard_map/ppermute | solution.py:52
  135.6 13.2 %collective-permute-start.27 = (bf16[2,8,7168]{2,1,0:T(8,128)(2,1)S(1)}, bf16[2,8,7168]{2,1,0:T(8,128)(2,1)S(1)}, u32[]{:S(2)}, u32[]{:S(2)}) collective-permute-start(bf16[2,8,7168]{2,1,0:T(8,128)(2,1)S(1)} %stack_two.3.pair), channel_id=1, source_target_pairs={{0,1},{1,0},{2,3},{3,2},{4,5},{5,4},{6,7},{7,6},{8,9},{9,8},{10,11... | collective-permute-start | bytes 688136 | tf_op jit(solution)/shard_map/ppermute | solution.py:79
  144.7 5.3 %collective-permute-start.28 = (bf16[2,8,7168]{2,1,0:T(8,128)(2,1)S(1)}, bf16[2,8,7168]{2,1,0:T(8,128)(2,1)S(1)}, u32[]{:S(2)}, u32[]{:S(2)}) collective-permute-start(bf16[2,8,7168]{2,1,0:T(8,128)(2,1)S(1)} %collective-permute-done.26.far), channel_id=1, source_target_pairs={{0,1},{1,0},{2,3},{3,2},{4,5},{5,4},{6,7},{7,6},{8,9},{9,8},{10,11... | collective-permute-start | bytes 688136 | tf_op jit(solution)/shard_map/ppermute | solution.py:79
  (25 other events, 233.5 us)

commit v4 on v2

--- a/solution.py
+++ b/solution.py
@@ -36,9 +36,9 @@
         for x in range(SIDE):
             for y in range(SIDE):
                 for c in range(2):
-                    axis, d = step(c)
+                    axis, to_place = step(c)
                     to = {"x": x, "y": y, "z": z}
-                    to[axis] = (to[axis] + d) % SIDE
+                    to[axis] = to_place(to[axis]) % SIDE
                     perm.append(
                         (
                             (z * SIDE + x) * 2 * SIDE + y * 2 + c,
@@ -53,19 +53,19 @@
 
 
 def forth(v, axis):
-    return shift(v, lambda c: (axis, 1 - 2 * c))
+    return shift(v, lambda c: (axis, lambda i: i + 1 - 2 * c))
 
 
 def back(v, axis):
-    return shift(v, lambda c: (axis, 2 * c - 1))
+    return shift(v, lambda c: (axis, lambda i: i + 2 * c - 1))
 
 
 def first(v, d):
-    return shift(v, lambda c: (("x", "z")[c], d))
+    return shift(v, lambda c: (("x", "z")[c], lambda i: i + d))
 
 
 def second(v, d):
-    return shift(v, lambda c: (("z", "x")[c], d))
+    return shift(v, lambda c: (("z", "x")[c], lambda i: i + d))
 
 
 def other_core(v):
@@ -79,10 +79,9 @@
 
 
 def ring_sum(blocks, axis):
-    far = forth(blocks[3], axis)
-    two = back(blocks[2], axis)
-    one = forth(add_two(blocks[1], far), axis)
-    return blocks[0], one, two
+    far = forth(blocks[2], axis)
+    two = back(blocks[1], axis)
+    return forth(add_two(blocks[0], far), axis), two
 
 
 def here():
@@ -100,6 +99,10 @@
 HBM = pl.BlockSpec(memory_space=pltpu.HBM)
 F32 = jnp.float32
 BF16 = jnp.bfloat16
+
+
+def in_hbm(v):
+    return pltpu.with_memory_space_constraint(v, pltpu.HBM)
 
 
 def room(mib):
@@ -121,99 +124,155 @@
     )(a, b)
 
 
-def pack_body(g_ref, send_ref, keep_ref, sem):
+def pack_body(g_ref, p, one, two, send_ref, keep_ref, p_out, one_out, two_out, sem):
     _, _, y, core = here()
     sign = 1 - 2 * core
     cols = send_ref.shape[2]
     copies = []
-    for ref, ys, c in (
+    for ref, places, c in (
         (send_ref, turned(y, -sign), 1 - core),
         (keep_ref, turned(y, sign), core),
     ):
-        for j in range(SIDE):
-            at = pl.multiple_of((2 * ys[j] + c) * cols, 128)
+        for j, place in enumerate(places):
+            at = pl.multiple_of((2 * place + c) * cols, 128)
             copies.append(
                 pltpu.make_async_copy(
                     g_ref.at[:, pl.ds(at, cols)], ref.at[j], sem.at[len(copies)]
                 )
             )
+    for src, dst in ((p, p_out), (one, one_out), (two, two_out)):
+        copies.append(pltpu.make_async_copy(src, dst, sem.at[len(copies)]))
     for copy in copies:
         copy.start()
     for copy in copies:
         copy.wait()
 
 
-def pack(g):
+def pack(g, p, one, two):
     out = jax.ShapeDtypeStruct((SIDE, g.shape[0], g.shape[1] // (2 * SIDE)), g.dtype)
     return pl.pallas_call(
         pack_body,
-        in_specs=[HBM],
-        out_specs=[VMEM] * 2,
-        out_shape=[out] * 2,
-        scratch_shapes=[pltpu.SemaphoreType.DMA((2 * SIDE,))],
+        in_specs=[HBM] * 4,
+        out_specs=[VMEM] * 5,
+        out_shape=[out] * 2 + [jax.ShapeDtypeStruct(p.shape, F32)] * 3,
+        scratch_shapes=[pltpu.SemaphoreType.DMA((2 * SIDE + 3,))],
         compiler_params=room(8),
         name="pack_columns",
-    )(g)
-
-
-def add_body(keep, got, o0, o1, o2, o3):
-    for j, o in ((3, o3), (2, o2), (1, o1), (0, o0)):
-        o[...] = (keep[j].astype(F32) + got[j].astype(F32)).astype(o.dtype)
-
-
-def add_pairs(keep, got, kind):
-    shape = got.shape[1:]
-    return pl.pallas_call(
-        add_body,
+    )(*(in_hbm(v) for v in (g, p, one, two)))
+
+
+def add_columns_body(keep, got, own, *parts):
+    rows, cols = own.shape
+    width = cols // 2
+    for j in (3, 2, 1, 0):
+        for r in range(0, rows, 16):
+            part = slice(r, r + 16)
+            total = keep[j, part, :].astype(F32) + got[j, part, :].astype(F32)
+            if j == 0:
+                own[part, :] = total
+            else:
+                parts[j - 1][part, :] = total[:, :width].astype(BF16)
+                parts[j + 2][part, :] = total[:, width:].astype(BF16)
+
+
+def add_columns(keep, got):
+    rows, cols = got.shape[1:]
+    half = jax.ShapeDtypeStruct((rows, cols // 2), BF16)
+    return pl.pallas_call(
+        add_columns_body,
         in_specs=[VMEM] * 2,
-        out_specs=[VMEM] * SIDE,
-        out_shape=[jax.ShapeDtypeStruct(shape, kind)] + [jax.ShapeDtypeStruct(shape, BF16)] * 3,
+        out_specs=[VMEM] * 7,
+        out_shape=[jax.ShapeDtypeStruct((rows, cols), F32)] + [half] * 6,
         compiler_params=room(8),
-        name="add_pairs",
+        name="add_columns",
     )(keep, got)
 
 
-def adam_body(r0, r1, r2, p, one, two, new_p, new_one, new_two, w):
-    grad = r0[...] + r1[...].astype(F32) + r2[...].astype(F32)
-    moment = 0.9 * one[...] + 0.1 * grad
-    second_moment = 0.999 * two[...] + 0.001 * grad * grad
+def adam_step(grad, p, one, two):
     step_size = 0.003 / first_fix
+    moment = 0.9 * one + 0.1 * grad
+    second_moment = 0.999 * two + 0.001 * grad * grad
     denom = jnp.sqrt(second_moment / second_fix) + 1e-08
-    params = p[...] - step_size * moment / denom
-    w[...] = params.astype(BF16)
-    new_p[...] = params
-    new_one[...] = moment
-    new_two[...] = second_moment
-
-
-def adam(parts, p, one, two):
+    return p - step_size * moment / denom, moment, second_moment
+
+
+def adam_first_body(r0, r1, r2, p, one, two, w):
+    width = w.shape[1]
+    cols = slice(0, width)
+    for r in range(0, p.shape[0], 16):
+        part = slice(r, r + 16)
+        grad = r0[part, cols] + r1[part].astype(F32) + r2[part].astype(F32)
+        w[part] = adam_step(grad, p[part, cols], one[part, cols], two[part, cols])[0].astype(BF16)
+
+
+def adam_first(own, parts, p, one, two):
+    rows, cols = p.shape
+    return pl.pallas_call(
+        adam_first_body,
+        in_specs=[VMEM] * 6,
+        out_specs=VMEM,
+        out_shape=jax.ShapeDtypeStruct((rows, cols // 2), BF16),
+        compiler_params=room(12),
+        name="adam_first",
+    )(own, *parts, p, one, two)
+
+
+def adam_body(r0, a1, a2, b1, b2, p, one, two, after, new_p, new_one, new_two, w):
+    del after
+    width = w.shape[1]
+    for r in range(0, p.shape[0], 16):
+        part = slice(r, r + 16)
+        for k, (r1, r2) in ((1, (b1, b2)), (0, (a1, a2))):
+            cols = slice(k * width, (k + 1) * width)
+            grad = r0[part, cols] + r1[part].astype(F32) + r2[part].astype(F32)
+            params, moment, second_moment = adam_step(
+                grad, p[part, cols], one[part, cols], two[part, cols]
+            )
+            if k:
+                w[part] = params.astype(BF16)
+            new_p[part, cols] = params
+            new_one[part, cols] = moment
+            new_two[part, cols] = second_moment
+
+
+def adam(own, parts, p, one, two, after):
+    rows, cols = p.shape
     full = jax.ShapeDtypeStruct(p.shape, F32)
     return pl.pallas_call(
         adam_body,
-        in_specs=[VMEM] * 6,
+        in_specs=[VMEM] * 8 + [pl.BlockSpec(memory_space=pl.ANY)],
         out_specs=[VMEM] * 4,
-        out_shape=[full] * 3 + [jax.ShapeDtypeStruct(p.shape, BF16)],
+        out_shape=[full] * 3 + [jax.ShapeDtypeStruct((rows, cols // 2), BF16)],
         compiler_params=room(12),
         name="adam",
-    )(*parts, p, one, two)
-
-
-def stack_body(a, b, out):
-    rows = a.shape[0]
-    out[:rows, :] = a[...]
-    out[rows:, :] = b[...]
-
-
-def stack_rows(a, b):
-    rows, cols = a.shape
+    )(own, *parts, p, one, two, after)
+
+
+def stack_body(*refs):
+    out = refs[-1]
+    rows = refs[0].shape[0]
+    for k, ref in enumerate(refs[:-1]):
+        out[k * rows : (k + 1) * rows, :] = ref[...]
+
+
+def stack_rows(*blocks):
+    rows, cols = blocks[0].shape
     return pl.pallas_call(
         stack_body,
-        in_specs=[VMEM] * 2,
+        in_specs=[VMEM] * len(blocks),
         out_specs=VMEM,
-        out_shape=jax.ShapeDtypeStruct((2 * rows, cols), a.dtype),
+        out_shape=jax.ShapeDtypeStruct((len(blocks) * rows, cols), blocks[0].dtype),
         compiler_params=room(8),
         name="stack_rows",
-    )(a, b)
+    )(*blocks)
+
+
+def spread(w, d, also=()):
+    above, below = first(w, 1), first(w, -1)
+    unit = stack_rows(w, above, below, first(above if d > 0 else below, d))
+    unit, *also = lax.optimization_barrier((unit,) + tuple(also))
+    up, down = second(unit, 1), second(unit, -1)
+    return also, [unit, up, down, second(up if d > 0 else down, d)]
 
 
 def query_body(ql_ref, *refs, seqs, steps, heads, q_rank):
@@ -222,14 +281,17 @@
     z, x, _, core = here()
     shard = w_buf.shape[0] // (SIDE * SIDE)
     far = (0, SIDE - 1, 1, 2)
+    width = w_buf.shape[1] // 2
     for k in range(SIDE):
         for m in range(SIDE):
             zo = jnp.where(core == 0, far[k], far[m])
             xo = jnp.where(core == 0, far[m], far[k])
             f = lax.rem(z + zo, SIDE) * SIDE + lax.rem(x + xo, SIDE)
             at = pl.multiple_of(f * shard, shard)
-            rows = slice((m % 2) * shard, (m % 2 + 1) * shard)
-            w_buf[pl.ds(at, shard), :] = units[2 * k + m // 2][rows, :]
+            rows = slice(m * shard, (m + 1) * shard)
+            for h in range(2):
+                cols = slice(h * width, (h + 1) * width)
+                w_buf[pl.ds(at, shard), cols] = units[4 * h + k][rows, :]
     nope = dot(ql_ref[...], w_buf[:q_rank, :], NN).astype(BF16)
     for h in range(heads):
         cols = slice(h * HDIM, (h + 1) * HDIM)
@@ -240,7 +302,7 @@
 
 
 def queries(ql, units, w_rows, seqs, q_rank):
-    cols = units[0].shape[1]
+    cols = 2 * units[0].shape[1]
     heads = cols // HDIM
     steps = ql.shape[0] // seqs
     lat_rank = w_rows - q_rank
@@ -447,9 +509,9 @@
             pltpu.SemaphoreType.DMA((SLOTS,)),
             pltpu.SemaphoreType.DMA((SLOTS,)),
         ],
-        compiler_params=room(36),
+        compiler_params=room(40),
         name="attention",
-    )(order, lengths, q_own, q_got, r_own, r_got, nl, nr, lat, rope)
+    )(order, lengths, q_own, q_got, r_own, r_got, nl, nr, in_hbm(lat), in_hbm(rope))
 
 
 def values_body(order_ref, own, got, vw_ref, out_ref, mixed, flat):
@@ -504,12 +566,14 @@
     send_ref, keep_ref, v_buf, w_buf = refs[8:]
     _, x, _, core = here()
     sign = 1 - 2 * core
-    offsets = (0, SIDE - sign, SIDE + sign, 2)
+    v_buf[0] = tokens[0][...]
+    v_buf[lax.rem(SIDE - sign, SIDE)] = tokens[1][...]
+    v_buf[lax.rem(SIDE + sign, SIDE)] = tokens[2][...]
+    v_buf[2] = tokens[3][...]
     depth = v_buf.shape[2]
     part = weights[0].shape[0]
-    for k in range(SIDE):
-        v_buf[lax.rem(offsets[k], SIDE) if k in (1, 2) else offsets[k]] = tokens[k][...]
-        at = pl.multiple_of(lax.rem(x + offsets[k], SIDE) * part, 64)
+    for k, offset in enumerate((0, SIDE - sign, SIDE + sign, 2)):
+        at = pl.multiple_of(lax.rem(x + offset, SIDE) * part, 64)
         w_buf[pl.ds(at, part), :] = weights[k][...]
     tokens_all = v_buf[...].reshape(-1, depth)
     width = 256
@@ -540,18 +604,36 @@
     )(*tokens, *weights)
 
 
-def total_body(a, b, c, o0, o1, o2, o3):
-    for j, o in enumerate((o0, o1, o2, o3)):
-        o[...] = (a[j].astype(F32) + b[j].astype(F32) + c[j].astype(F32)).astype(o.dtype)
+def add_blocks_body(keep, got, *outs):
+    for j in (3, 2, 1, 0):
+        for k in range(SIDE):
+            outs[j][k] = (keep[j, k].astype(F32) + got[j, k].astype(F32)).astype(BF16)
+
+
+def add_blocks(keep, got):
+    one = jax.ShapeDtypeStruct(got.shape[1:], BF16)
+    return pl.pallas_call(
+        add_blocks_body,
+        in_specs=[VMEM] * 2,
+        out_specs=[VMEM] * 4,
+        out_shape=[one] * 4,
+        compiler_params=room(8),
+        name="add_blocks",
+    )(keep, got)
+
+
+def total_body(a, b, c, *outs):
+    for k in (2, 1, 3, 0):
+        outs[k][...] = (a[k].astype(F32) + b[k].astype(F32) + c[k].astype(F32)).astype(BF16)
 
 
 def total_blocks(parts):
-    out = jax.ShapeDtypeStruct(parts[0].shape[1:], BF16)
+    one = jax.ShapeDtypeStruct(parts[0].shape[1:], BF16)
     return pl.pallas_call(
         total_body,
         in_specs=[VMEM] * 3,
-        out_specs=[VMEM] * SIDE,
-        out_shape=[out] * SIDE,
+        out_specs=[VMEM] * 4,
+        out_shape=[one] * 4,
         compiler_params=room(8),
         name="total_blocks",
     )(*parts)
@@ -600,40 +682,119 @@
 
 
 def splits(seqs):
-    table = []
     for rest in itertools.combinations(range(1, seqs), seqs // 2 - 1):
         mine = (0,) + rest
-        table.append(mine + tuple(s for s in range(seqs) if s not in mine))
-    return np.array(table, np.int32)
-
-
-def balanced_order(lengths):
-    seqs = lengths.shape[0]
-    table = splits(seqs)
-    member = np.zeros((table.shape[0], seqs), np.int32)
-    for i, row in enumerate(table):
-        member[i, row[: seqs // 2]] = 1
-    blocks = lax.div(lengths + (BLOCK - 1), BLOCK)
-    first = jnp.sum(member * blocks[None, :], axis=1)
-    larger = jnp.maximum(first, jnp.sum(blocks) - first)
-    index = np.arange(table.shape[0], dtype=np.int32)
-    score = larger * table.shape[0] + index
-    chosen = (score == jnp.min(score)).astype(jnp.int32)
-    return jnp.sum(chosen[:, None] * table, axis=0)
-
-
-def rotate(vector, position):
-    half = vector.shape[-1] // 2
-    index_f = jnp.arange(half, dtype=jnp.float32)
-    frequency = jnp.exp(-math.log(10000.0) * 2.0 * index_f / vector.shape[-1])
-    angle = position[..., None] * frequency
-    first = vector[..., :half]
-    second = vector[..., half:]
-    cosine = jnp.cos(angle)
+        yield mine + tuple(s for s in range(seqs) if s not in mine)
+
+
+def prepare_body(
+    len_ref,
+    ql_ref,
+    rw_ref,
+    nl_ref,
+    nr_ref,
+    order_ref,
+    length_ref,
+    by_seq_ref,
+    r_own,
+    r_send,
+    nl_out,
+    nr_out,
+    r_buf,
+    *,
+    core_of,
+):
+    core = core_of()
+    steps, seqs, q_rank = ql_ref.shape
+    half = seqs // 2
+    count = steps * seqs
+
+    blocks = [lax.div(len_ref[s] + (BLOCK - 1), BLOCK) for s in range(seqs)]
+    whole = sum(blocks[1:], blocks[0])
+    least, code = None, None
+    for row in splits(seqs):
+        part = blocks[0] + blocks[row[1]] + blocks[row[2]] + blocks[row[3]]
+        larger = jnp.maximum(part, whole - part)
+        digits = sum(s << (3 * k) for k, s in enumerate(row))
+        if least is None:
+            least, code = larger, jnp.int32(digits)
+        else:
+            code = jnp.where(larger < least, digits, code)
+            least = jnp.minimum(larger, least)
+    order, lengths = [], []
+    for k in range(seqs):
+        shift_by = jnp.where(core == 0, 3 * k, 3 * ((k + half) % seqs))
+        order.append(lax.shift_right_logical(code, shift_by) & 7)
+        lengths.append(len_ref[order[k]])
+        order_ref[k] = order[k]
+        length_ref[k] = lengths[k]
+
+    def by_place(place, values):
+        out = jnp.zeros(place.shape, jnp.int32)
+        for k, value in enumerate(values):
+            out = jnp.where(place == k, value, out)
+        return out
+
+    def pick(rows, depth, used):
+        row = lax.broadcasted_iota(jnp.int32, (rows, count), 0)
+        col = lax.broadcasted_iota(jnp.int32, (rows, count), 1)
+        same = (by_place(lax.div(row, depth), order[:used]) == lax.rem(col, seqs)) & (
+            lax.rem(row, depth) == lax.div(col, seqs)
+        )
+        return jnp.where(same, 1.0, 0.0).astype(BF16)
+
+    by_seq = dot(pick(count, steps, seqs), ql_ref[...].reshape(count, q_rank), NN).astype(BF16)
+    by_seq_ref[...] = by_seq
+
+    turn = dot(by_seq, rw_ref[...], NN)
+    cols = turn.shape[1]
+    row = lax.broadcasted_iota(jnp.int32, (count, 128), 0)
+    lane = lax.broadcasted_iota(jnp.int32, (count, 128), 1)
+    position = (by_place(lax.div(row, steps), lengths) + lax.rem(row, steps)).astype(F32)
+    index_f = lax.rem(lane, ROPE // 2).astype(F32)
+    angle = position * jnp.exp(-math.log(10000.0) * 2.0 * index_f / ROPE)
+    is_first = lax.rem(lane, ROPE) < ROPE // 2
+    cosine = jnp.concatenate([jnp.cos(angle)] * (cols // 128), axis=1)
     sine = jnp.sin(angle)
-    return jnp.concatenate(
-        [first * cosine - second * sine, first * sine + second * cosine], axis=-1
+    sine = jnp.concatenate([jnp.where(is_first, -sine, sine)] * (cols // 128), axis=1)
+    is_first = lax.rem(lax.broadcasted_iota(jnp.int32, (count, cols), 1), ROPE) < ROPE // 2
+    other = jnp.where(
+        is_first,
+        pltpu.roll(turn, cols - ROPE // 2, 1),
+        pltpu.roll(turn, ROPE // 2, 1),
     )
+    turn = turn * cosine + other * sine
+    for h in range(cols // ROPE):
+        piece = turn[:, h * ROPE : (h + 1) * ROPE].reshape(seqs, steps, ROPE)
+        r_buf[:, h * steps : (h + 1) * steps, :] = piece
+    r_own[...] = r_buf[:half].astype(BF16)
+    r_send[...] = r_buf[half:].astype(BF16)
+
+    width = nl_out.shape[1]
+    chosen = pick(half * width, width, half)
+    for src, out in ((nl_ref, nl_out), (nr_ref, nr_out)):
+        rank = src.shape[2]
+        rows = dot(chosen, src[...].reshape(count, rank), NN).astype(BF16)
+        out[...] = rows.reshape(half, width, rank)
+
+
+def prepare(lengths, ql, rw, nl, nr, core_of):
+    steps, seqs, q_rank = ql.shape
+    half = seqs // 2
+    rows = rw.shape[1] // ROPE * steps
+    turned_rows = jax.ShapeDtypeStruct((half, rows, ROPE), BF16)
+    return pl.pallas_call(
+        functools.partial(prepare_body, core_of=core_of),
+        in_specs=[SMEM] + [VMEM] * 4,
+        out_specs=[SMEM] * 2 + [VMEM] * 5,
+        out_shape=[jax.ShapeDtypeStruct((seqs,), jnp.int32)] * 2
+        + [jax.ShapeDtypeStruct((steps * seqs, q_rank), BF16)]
+        + [turned_rows] * 2
+        + [jax.ShapeDtypeStruct((half, 128, v.shape[2]), BF16) for v in (nl, nr)],
+        scratch_shapes=[pltpu.VMEM((seqs, rows, ROPE), F32)],
+        compiler_params=room(12),
+        name="prepare",
+    )(lengths, ql, rw, nl, nr)
 
 
 def body(
@@ -651,61 +812,36 @@
     new_rope,
     lengths,
 ):
-    core = lax.rem(lax.axis_index("head"), 2)
-
-    send, keep = pack(grad_parts[0])
-    sums = add_pairs(keep, other_core(send), F32)
-    parts = ring_sum(sums, "y")
-    new_params, new_one, new_two, w = adam(parts, params, moment_one, moment_two)
+    send, keep, params, moment_one, moment_two = pack(
+        grad_parts[0], params, moment_one, moment_two
+    )
+    own_sum, *sums = add_columns(keep, other_core(send))
+    parts_a = ring_sum(sums[:3], "y")
+    parts_b = ring_sum(sums[3:], "y")
+    w_a = adam_first(own_sum, parts_a, params, moment_one, moment_two)
+    new_params, new_one, new_two, w_b = adam(
+        own_sum, parts_a + parts_b, params, moment_one, moment_two, w_a
+    )
 
     w_t = out_weight.T
     w_one, w_two = forth(w_t, "x"), back(w_t, "x")
-    w_one, w = lax.optimization_barrier((w_one, w))
-
-    above, below = first(w, 1), first(w, -1)
-    top = stack_rows(w, above)
-    bottom = stack_rows(below, first(above, 1))
-    top_above, top_below = second(top, 1), second(top, -1)
-    bottom_above, bottom_below = second(bottom, 1), second(bottom, -1)
-    units = [top, bottom, top_above, bottom_above, top_below, bottom_below]
-    units += [second(top_above, 1), second(bottom_below, -1)]
-    out_weights = (w_t, w_one, w_two, forth(w_one, "x"))
-
+
+    lengths, _ = lax.optimization_barrier((lengths, sums[5]))
     steps_n, seq_local, q_rank = query_latent.shape
-    heads_local = value_weight.shape[1] // HDIM
-    half = seq_local // 2
-    lengths, _ = lax.optimization_barrier((lengths, sums[3]))
-    order = balanced_order(lengths)
-    order = jnp.where(core == 0, order, jnp.concatenate([order[half:], order[:half]]))
-    chosen = order[:, None] == jnp.arange(seq_local, dtype=jnp.int32)[None, :]
-    lengths_in = jnp.sum(jnp.where(chosen, lengths[None, :], 0), axis=1)
-    chosen = chosen.astype(BF16)
-
-    def arrange(which, arrays):
-        return jnp.einsum("ps,tsq->ptq", which, arrays, preferred_element_type=F32).astype(BF16)
-
-    by_seq = arrange(chosen, query_latent).reshape(seq_local * steps_n, q_rank)
-    by_seq_late, rope_late, _ = lax.optimization_barrier((by_seq, rope_weight, bottom))
-    query_rope = jnp.dot(by_seq_late, rope_late, preferred_element_type=F32).reshape(
-        seq_local, steps_n, heads_local, ROPE
+    order, lengths_in, by_seq, r_own, r_send, nl, nr = prepare(
+        lengths, query_latent, rope_weight, new_latent, new_rope, lambda: here()[3]
     )
-    position = (lengths_in[:, None] + jnp.arange(steps_n, dtype=jnp.int32)[None, :]).astype(F32)[
-        :, :, None
-    ]
-    query_rope = rotate(query_rope, position).astype(BF16)
-    query_rope = jnp.transpose(query_rope, (0, 2, 1, 3)).reshape(
-        seq_local, heads_local * steps_n, ROPE
-    )
-    r_own, r_got = query_rope[:half], other_core(query_rope[half:])
-    pad = ((0, 0), (0, 128 - steps_n), (0, 0))
-    nl = jnp.pad(arrange(chosen[:half], new_latent), pad)
-    nr = jnp.pad(arrange(chosen[:half], new_rope), pad)
+    r_got = other_core(r_send)
+
+    (w_one, w_two), units = spread(w_a, 1, (w_one, w_two))
+    _, more = spread(w_b, -1)
+    units += more
 
     w_rows = SIDE * SIDE * params.shape[0]
     q_own, q_send = queries(by_seq, units, w_rows, seq_local, q_rank)
     mixed, mixed_send = attention(
         order,
-        lengths_in[:half],
+        lengths_in,
         q_own,
         other_core(q_send),
         r_own,
@@ -716,11 +852,13 @@
         rope_cache,
         steps_n,
     )
+    w_one, mixed = lax.optimization_barrier((w_one, mixed))
+    out_weights = (w_t, w_one, w_two, forth(w_one, "x"))
     values = project_values(order, mixed, other_core(mixed_send), value_weight)
 
     send, keep = output_blocks(ring(values, "z"), out_weights, seq_local)
-    parts = ring_sum(add_pairs(keep, other_core(send), BF16), "y")
-    blocks = total_blocks(parts)
+    own, *sums = add_blocks(keep, other_core(send))
+    blocks = total_blocks((own,) + ring_sum(sums, "y"))
 
     arrived = [blocks[0]]
     for d in range(1, SIDE):

time: 149 us -> 139 us (0.933); the launches traced: 148 us -> 140 us
  starting transfers between devices: 62.4 us -> 74.4 us
  local copies, waits for them, and re-layouts: 7.33 us -> 0.03 us
  other arithmetic: 5.64 us -> 0 us
  Pallas kernels: 30.9 us -> 26.4 us
  waiting for transfers between devices: 40.3 us -> 38.3 us
    ppermute x24 -> x30, starting transfers between devices: 38.9 us -> 46.7 us  [shift(): return lax.ppermute(v, ('fsdp', 'head'), moves(step))]
    unnamed x32 -> x14, local copies, waits for them, and re-layouts: 5.15 us -> 0.03 us
    ppermute x9, starting transfers between devices: 20.8 us -> 24.9 us  [other_core(): return lax.ppermute(v, 'head', [(i, i ^ 1) for i in range(2 * SIDE)])]
    pallas_call x1, Pallas kernels: 18.6 us -> 15.4 us  [attention(): pl.pallas_call(functools.partial(attention_body, steps=steps), in_specs=[...]
    ppermute x24 -> x30, waiting for transfers between devices: 33.5 us -> 31.6 us  [shift(): return lax.ppermute(v, ('fsdp', 'head'), moves(step))]
    pallas_call x7 -> x9, Pallas kernels: 4.35 us -> 5.88 us  [the longest x1 2.24 us: pack(): pl.pallas_call(pack_body, in_specs=[HBM] * 4, out_specs=[VMEM] * 5, out_s...]
  transfers between devices with their start and end apart: 36 -> 42, of which waited for: 23 -> 24; matrix products, arithmetic and copies ran while one was open for 6% -> 0% of each run, Pallas kernels for 17% -> 3%
where the time goes in v4:
time: 139 us; the launch traced here: 140 us
  starting transfers between devices  74.4 us (54%)
  waiting for transfers between devices  38.3 us (28%)
  Pallas kernels  26.4 us (19%)
    ppermute x30, starting transfers between devices, shift(): return lax.ppermute(v, ('fsdp', 'head'), moves(step))  46.7 us
    ppermute x30, waiting for transfers between devices, shift(): return lax.ppermute(v, ('fsdp', 'head'), moves(step))  31.6 us
    ppermute x9, starting transfers between devices, other_core(): return lax.ppermute(v, 'head', [(i, i ^ 1) for i in range(2 * SIDE)])  24.9 us
    pallas_call x1, Pallas kernels, attention(): pl.pallas_call(functools.partial(attention_body, steps=steps), in_specs=[...  15.4 us
    ppermute x9, waiting for transfers between devices, other_core(): return lax.ppermute(v, 'head', [(i, i ^ 1) for i in range(2 * SIDE)])  4.55 us
  transfers between devices with their start and end apart: 42, of which 24 were waited for; matrix products, arithmetic and copies ran while one was open for 0% of the time, Pallas kernels for 3%

profile of v4, /device:TPU:1, one launch (start us, length us, event | category | flops | bytes accessed | tf_op | source)
XLA Modules:
  0.0 140.1 jit_solution(3229434371378543855)
XLA Ops:
  0.7 2.2 %pack_columns.1 = (bf16[4,128,1024]{2,1,0:T(8,128)(2,1)S(1)}, bf16[4,128,1024]{2,1,0:T(8,128)(2,1)S(1)}, f32[128,1024]{1,0:T(8,128)S(1)}, f32[128,1024]{1,0:T(8,128)S(1)}, f32[128,1024]{1,0:T(8,128)S(1)}) custom-call(bf16[128,8192]{1,0:T(8,128)(2,1)} %bitcast.5, f32[128,1024]{1,0:T(8,128)} %p.1, f32[128,1024]{1,0:T(8,128)} %one.1, f32[128,1024]{1,0:T(8,128)} %two.1), custom_call_target="tpu_custom_call" | custom-call | tf_op jit(solution)/shard_map/pack_columns/pallas_call | solution.py:153
  7.3 2.9 %collective-permute-start.1 = (bf16[128,512]{1,0:T(8,128)(2,1)S(1)}, bf16[128,512]{1,0:T(8,128)(2,1)S(1)}, u32[]{:S(2)}, u32[]{:S(2)}) collective-permute-start(bf16[128,512]{1,0:T(8,128)(2,1)S(1)} %get-tuple-element.51), channel_id=1, source_target_pairs={{0,2},{1,7},{2,4},{3,1},{4,6},{5,3},{6,0},{7,5},{8,10},{9,15},{10,... | collective-permute-start | bytes 393224 | tf_op jit(solution)/shard_map/ppermute | solution.py:52
  12.2 3.4 %collective-permute-start.2 = (bf16[128,512]{1,0:T(8,128)(2,1)S(1)}, bf16[128,512]{1,0:T(8,128)(2,1)S(1)}, u32[]{:S(2)}, u32[]{:S(2)}) collective-permute-start(bf16[128,512]{1,0:T(8,128)(2,1)S(1)} %add_two.3), channel_id=1, source_target_pairs={{0,2},{1,7},{2,4},{3,1},{4,6},{5,3},{6,0},{7,5},{8,10},{9,15},{10,... | collective-permute-start | bytes 393224 | tf_op jit(solution)/shard_map/ppermute | solution.py:52
  21.1 3.8 %collective-permute-start.8 = (bf16[128,512]{1,0:T(8,128)(2,1)S(1)}, bf16[128,512]{1,0:T(8,128)(2,1)S(1)}, u32[]{:S(2)}, u32[]{:S(2)}) collective-permute-start(bf16[128,512]{1,0:T(8,128)(2,1)S(1)} %adam_first.1.after.refs_0_), channel_id=1, source_target_pairs={{0,24},{1,97},{2,26},{3,99},{4,28},{5,101},{6,30},{7,103},{8,0},{9... | collective-permute-start | bytes 393224 | tf_op jit(solution)/shard_map/ppermute | solution.py:52
  27.8 2.6 %collective-permute-done.16.refs_2_ = bf16[128,512]{1,0:T(8,128)(2,1)S(1)} collective-permute-done((bf16[128,512]{1,0:T(8,128)(2,1)S(1)}, bf16[128,512]{1,0:T(8,128)(2,1)S(1)}, u32[]{:S(2)}, u32[]{:S(2)}) %collective-permute-start.16) | collective-permute-done | bytes 131104 | tf_op jit(solution)/shard_map/ppermute | solution.py:52
  34.5 3.0 %collective-permute-start.19 = (bf16[512,512]{1,0:T(8,128)(2,1)S(1)}, bf16[512,512]{1,0:T(8,128)(2,1)S(1)}, u32[]{:S(2)}, u32[]{:S(2)}) collective-permute-start(bf16[512,512]{1,0:T(8,128)(2,1)S(1)} %stack_rows.3.refs_4_), channel_id=1, source_target_pairs={{0,96},{1,25},{2,98},{3,27},{4,100},{5,29},{6,102},{7,31},{8,104},... | collective-permute-start | bytes 1572872 | tf_op jit(solution)/shard_map/ppermute | solution.py:52
  37.5 2.7 %collective-permute-start.13 = (bf16[512,512]{1,0:T(8,128)(2,1)S(1)}, bf16[512,512]{1,0:T(8,128)(2,1)S(1)}, u32[]{:S(2)}, u32[]{:S(2)}) collective-permute-start(bf16[512,512]{1,0:T(8,128)(2,1)S(1)} %stack_rows.2.refs_0_), channel_id=1, source_target_pairs={{0,96},{1,25},{2,98},{3,27},{4,100},{5,29},{6,102},{7,31},{8,104},... | collective-permute-start | bytes 1572872 | tf_op jit(solution)/shard_map/ppermute | solution.py:52
  40.2 3.4 %collective-permute-done.19.refs_6_ = bf16[512,512]{1,0:T(8,128)(2,1)S(1)} collective-permute-done((bf16[512,512]{1,0:T(8,128)(2,1)S(1)}, bf16[512,512]{1,0:T(8,128)(2,1)S(1)}, u32[]{:S(2)}, u32[]{:S(2)}) %collective-permute-start.19) | collective-permute-done | bytes 524320 | tf_op jit(solution)/shard_map/ppermute | solution.py:52
  43.7 3.1 %collective-permute-start.20 = (bf16[512,512]{1,0:T(8,128)(2,1)S(1)}, bf16[512,512]{1,0:T(8,128)(2,1)S(1)}, u32[]{:S(2)}, u32[]{:S(2)}) collective-permute-start(bf16[512,512]{1,0:T(8,128)(2,1)S(1)} %collective-permute-done.19.refs_6_), channel_id=1, source_target_pairs={{0,96},{1,25},{2,98},{3,27},{4,100},{5,29},{6,102},{7,31},{8,104},... | collective-permute-start | bytes 1572872 | tf_op jit(solution)/shard_map/ppermute | solution.py:52
  48.7 3.9 %collective-permute-done.18.refs_5_ = bf16[512,512]{1,0:T(8,128)(2,1)S(1)} collective-permute-done((bf16[512,512]{1,0:T(8,128)(2,1)S(1)}, bf16[512,512]{1,0:T(8,128)(2,1)S(1)}, u32[]{:S(2)}, u32[]{:S(2)}) %collective-permute-start.18) | collective-permute-done | bytes 524320 | tf_op jit(solution)/shard_map/ppermute | solution.py:52
  54.9 3.4 %collective-permute-done.14.refs_3_ = bf16[512,512]{1,0:T(8,128)(2,1)S(1)} collective-permute-done((bf16[512,512]{1,0:T(8,128)(2,1)S(1)}, bf16[512,512]{1,0:T(8,128)(2,1)S(1)}, u32[]{:S(2)}, u32[]{:S(2)}) %collective-permute-start.14) | collective-permute-done | bytes 524320 | tf_op jit(solution)/shard_map/ppermute | solution.py:52
  59.6 5.2 %collective-permute-start.21 = (bf16[4,64,512]{2,1,0:T(8,128)(2,1)S(1)}, bf16[4,64,512]{2,1,0:T(8,128)(2,1)S(1)}, u32[]{:S(2)}, u32[]{:S(2)}) collective-permute-start(bf16[4,64,512]{2,1,0:T(8,128)(2,1)S(1)} %get-tuple-element.70), channel_id=1, source_target_pairs={{0,1},{1,0},{2,3},{3,2},{4,5},{5,4},{6,7},{7,6},{8,9},{9,8},{10,11... | collective-permute-start | bytes 786440 | tf_op jit(solution)/shard_map/ppermute | solution.py:72
  66.1 15.4 %attention.1 = (bf16[4,64,512]{2,1,0:T(8,128)(2,1)S(1)}, bf16[4,64,512]{2,1,0:T(8,128)(2,1)S(1)}) custom-call(s32[8]{0:T(128)S(1)} %get-tuple-element.63.order_ref, s32[8]{0:T(128)S(1)} %get-tuple-element.65.len_ref, bf16[4,64,512]{2,1,0:T(8,128)(2,1)S(1)} %get-tuple-element.69.q_own, bf16[4,64,512]{2,1,0:T(8,128)(2,1)S(1)} %collective-permute-done.21.q_got, ...), custom_call_target="tpu_custom_call" | custom-call | tf_op jit(solution)/shard_map/attention/pallas_call | solution.py:490
  81.5 2.4 %collective-permute-start.27 = (bf16[448,1024]{1,0:T(8,128)(2,1)S(1)}, bf16[448,1024]{1,0:T(8,128)(2,1)S(1)}, u32[]{:S(2)}, u32[]{:S(2)}) collective-permute-start(bf16[448,1024]{1,0:T(8,128)(2,1)S(1)} %collective-permute-done.10.refs_5_), channel_id=1, source_target_pairs={{0,8},{1,25},{2,10},{3,27},{4,12},{5,29},{6,14},{7,31},{8,16},{9,1... | collective-permute-start | bytes 2752520 | tf_op jit(solution)/shard_map/ppermute | solution.py:52
  84.0 4.1 %collective-permute-start.23 = (bf16[4,64,512]{2,1,0:T(8,128)(2,1)S(1)}, bf16[4,64,512]{2,1,0:T(8,128)(2,1)S(1)}, u32[]{:S(2)}, u32[]{:S(2)}) collective-permute-start(bf16[4,64,512]{2,1,0:T(8,128)(2,1)S(1)} %get-tuple-element.77), channel_id=1, source_target_pairs={{0,1},{1,0},{2,3},{3,2},{4,5},{5,4},{6,7},{7,6},{8,9},{9,8},{10,11... | collective-permute-start | bytes 786440 | tf_op jit(solution)/shard_map/ppermute | solution.py:72
  91.8 3.2 %collective-permute-done.24.refs_1_ = bf16[64,1024]{1,0:T(8,128)(2,1)S(1)} collective-permute-done((bf16[64,1024]{1,0:T(8,128)(2,1)S(1)}, bf16[64,1024]{1,0:T(8,128)(2,1)S(1)}, u32[]{:S(2)}, u32[]{:S(2)}) %collective-permute-start.24) | collective-permute-done | bytes 131104 | tf_op jit(solution)/shard_map/ppermute | solution.py:52
  96.5 2.3 %collective-permute-done.26.refs_3_ = bf16[64,1024]{1,0:T(8,128)(2,1)S(1)} collective-permute-done((bf16[64,1024]{1,0:T(8,128)(2,1)S(1)}, bf16[64,1024]{1,0:T(8,128)(2,1)S(1)}, u32[]{:S(2)}, u32[]{:S(2)}) %collective-permute-start.26) | collective-permute-done | bytes 131104 | tf_op jit(solution)/shard_map/ppermute | solution.py:52
  100.5 5.0 %collective-permute-start.28 = (bf16[4,4,8,1792]{3,2,1,0:T(8,128)(2,1)S(1)}, bf16[4,4,8,1792]{3,2,1,0:T(8,128)(2,1)S(1)}, u32[]{:S(2)}, u32[]{:S(2)}) collective-permute-start(bf16[4,4,8,1792]{3,2,1,0:T(8,128)(2,1)S(1)} %get-tuple-element.81), channel_id=1, source_target_pairs={{0,1},{1,0},{2,3},{3,2},{4,5},{5,4},{6,7},{7,6},{8,9},{9,8},{10,11... | collective-permute-start | bytes 1376264 | tf_op jit(solution)/shard_map/ppermute | solution.py:72
  107.1 2.6 %collective-permute-start.29 = (bf16[4,8,1792]{2,1,0:T(8,128)(2,1)S(1)}, bf16[4,8,1792]{2,1,0:T(8,128)(2,1)S(1)}, u32[]{:S(2)}, u32[]{:S(2)}) collective-permute-start(bf16[4,8,1792]{2,1,0:T(8,128)(2,1)S(1)} %get-tuple-element.84), channel_id=1, source_target_pairs={{0,2},{1,7},{2,4},{3,1},{4,6},{5,3},{6,0},{7,5},{8,10},{9,15},{10,... | collective-permute-start | bytes 344072 | tf_op jit(solution)/shard_map/ppermute | solution.py:52
  111.4 3.1 %collective-permute-start.30 = (bf16[4,8,1792]{2,1,0:T(8,128)(2,1)S(1)}, bf16[4,8,1792]{2,1,0:T(8,128)(2,1)S(1)}, u32[]{:S(2)}, u32[]{:S(2)}) collective-permute-start(bf16[4,8,1792]{2,1,0:T(8,128)(2,1)S(1)} %add_two.5), channel_id=1, source_target_pairs={{0,2},{1,7},{2,4},{3,1},{4,6},{5,3},{6,0},{7,5},{8,10},{9,15},{10,... | collective-permute-start | bytes 344072 | tf_op jit(solution)/shard_map/ppermute | solution.py:52
  121.3 3.1 %collective-permute-start.35 = (bf16[8,7168]{1,0:T(8,128)(2,1)S(1)}, bf16[8,7168]{1,0:T(8,128)(2,1)S(1)}, u32[]{:S(2)}, u32[]{:S(2)}) collective-permute-start(bf16[8,7168]{1,0:T(8,128)(2,1)S(1)} %join_columns.1.refs_0_), channel_id=1, source_target_pairs={{0,2},{1,7},{2,4},{3,1},{4,6},{5,3},{6,0},{7,5},{8,10},{9,15},{10,... | collective-permute-start | bytes 344072 | tf_op jit(solution)/shard_map/ppermute | solution.py:52
  126.2 3.1 %collective-permute-start.37 = (bf16[8,7168]{1,0:T(8,128)(2,1)S(1)}, bf16[8,7168]{1,0:T(8,128)(2,1)S(1)}, u32[]{:S(2)}, u32[]{:S(2)}) collective-permute-start(bf16[8,7168]{1,0:T(8,128)(2,1)S(1)} %collective-permute-done.35.refs_1_), channel_id=1, source_target_pairs={{0,2},{1,7},{2,4},{3,1},{4,6},{5,3},{6,0},{7,5},{8,10},{9,15},{10,... | collective-permute-start | bytes 344072 | tf_op jit(solution)/shard_map/ppermute | solution.py:52
  129.3 2.8 %collective-permute-start.38 = (bf16[8,7168]{1,0:T(8,128)(2,1)S(1)}, bf16[8,7168]{1,0:T(8,128)(2,1)S(1)}, u32[]{:S(2)}, u32[]{:S(2)}) collective-permute-start(bf16[8,7168]{1,0:T(8,128)(2,1)S(1)} %join_columns.1.refs_0_), channel_id=1, source_target_pairs={{0,1},{1,0},{2,3},{3,2},{4,5},{5,4},{6,7},{7,6},{8,9},{9,8},{10,11... | collective-permute-start | bytes 344072 | tf_op jit(solution)/shard_map/ppermute | solution.py:72
  132.7 5.4 %collective-permute-start.41 = (bf16[8,7168]{1,0:T(8,128)(2,1)S(1)}, bf16[8,7168]{1,0:T(8,128)(2,1)S(1)}, u32[]{:S(2)}, u32[]{:S(2)}) collective-permute-start(bf16[8,7168]{1,0:T(8,128)(2,1)S(1)} %collective-permute-done.37.refs_3_), channel_id=1, source_target_pairs={{0,1},{1,0},{2,3},{3,2},{4,5},{5,4},{6,7},{7,6},{8,9},{9,8},{10,11... | collective-permute-start | bytes 344072 | tf_op jit(solution)/shard_map/ppermute | solution.py:72
  (92 shorter events, 47.0 us)
Async XLA Ops:
  4.4 27.8 %collective-permute-start.11 = (bf16[448,1024]{1,0:T(8,128)(2,1)}, bf16[448,1024]{1,0:T(8,128)(2,1)S(1)}, u32[]{:S(2)}, u32[]{:S(2)}) collective-permute-start(bf16[448,1024]{1,0:T(8,128)(2,1)} %bitcast.2), channel_id=1, source_target_pairs={{0,24},{1,9},{2,26},{3,11},{4,28},{5,13},{6,30},{7,15},{8,0},{9,17... | collective-permute-start | bytes 2752520 | tf_op jit(solution)/shard_map/ppermute | solution.py:52
  5.7 26.6 %collective-permute-start.10 = (bf16[448,1024]{1,0:T(8,128)(2,1)}, bf16[448,1024]{1,0:T(8,128)(2,1)S(1)}, u32[]{:S(2)}, u32[]{:S(2)}) collective-permute-start(bf16[448,1024]{1,0:T(8,128)(2,1)} %bitcast.3), channel_id=1, source_target_pairs={{0,8},{1,25},{2,10},{3,27},{4,12},{5,29},{6,14},{7,31},{8,16},{9,1... | collective-permute-start | bytes 2752520 | tf_op jit(solution)/shard_map/ppermute | solution.py:52
  10.7 5.7 %collective-permute-start.3 = (bf16[128,512]{1,0:T(8,128)(2,1)S(1)}, bf16[128,512]{1,0:T(8,128)(2,1)S(1)}, u32[]{:S(2)}, u32[]{:S(2)}) collective-permute-start(bf16[128,512]{1,0:T(8,128)(2,1)S(1)} %get-tuple-element.52), channel_id=1, source_target_pairs={{0,6},{1,3},{2,0},{3,5},{4,2},{5,7},{6,4},{7,1},{8,14},{9,11},{10,... | collective-permute-start | bytes 393224 | tf_op jit(solution)/shard_map/ppermute | solution.py:52
  12.2 6.2 %collective-permute-start.2 = (bf16[128,512]{1,0:T(8,128)(2,1)S(1)}, bf16[128,512]{1,0:T(8,128)(2,1)S(1)}, u32[]{:S(2)}, u32[]{:S(2)}) collective-permute-start(bf16[128,512]{1,0:T(8,128)(2,1)S(1)} %add_two.3), channel_id=1, source_target_pairs={{0,2},{1,7},{2,4},{3,1},{4,6},{5,3},{6,0},{7,5},{8,10},{9,15},{10,... | collective-permute-start | bytes 393224 | tf_op jit(solution)/shard_map/ppermute | solution.py:52
  16.4 8.5 %collective-permute-start.5 = (bf16[128,512]{1,0:T(8,128)(2,1)S(1)}, bf16[128,512]{1,0:T(8,128)(2,1)S(1)}, u32[]{:S(2)}, u32[]{:S(2)}) collective-permute-start(bf16[128,512]{1,0:T(8,128)(2,1)S(1)} %add_two.4), channel_id=1, source_target_pairs={{0,2},{1,7},{2,4},{3,1},{4,6},{5,3},{6,0},{7,5},{8,10},{9,15},{10,... | collective-permute-start | bytes 393224 | tf_op jit(solution)/shard_map/ppermute | solution.py:52
  18.7 8.2 %collective-permute-start.7 = (bf16[128,512]{1,0:T(8,128)(2,1)S(1)}, bf16[128,512]{1,0:T(8,128)(2,1)S(1)}, u32[]{:S(2)}, u32[]{:S(2)}) collective-permute-start(bf16[128,512]{1,0:T(8,128)(2,1)S(1)} %adam_first.1.after.refs_0_), channel_id=1, source_target_pairs={{0,8},{1,33},{2,10},{3,35},{4,12},{5,37},{6,14},{7,39},{8,16},{9,4... | collective-permute-start | bytes 393224 | tf_op jit(solution)/shard_map/ppermute | solution.py:52
  21.1 6.6 %collective-permute-start.8 = (bf16[128,512]{1,0:T(8,128)(2,1)S(1)}, bf16[128,512]{1,0:T(8,128)(2,1)S(1)}, u32[]{:S(2)}, u32[]{:S(2)}) collective-permute-start(bf16[128,512]{1,0:T(8,128)(2,1)S(1)} %adam_first.1.after.refs_0_), channel_id=1, source_target_pairs={{0,24},{1,97},{2,26},{3,99},{4,28},{5,101},{6,30},{7,103},{8,0},{9... | collective-permute-start | bytes 393224 | tf_op jit(solution)/shard_map/ppermute | solution.py:52
  27.7 5.6 %collective-permute-start.15 = (bf16[128,512]{1,0:T(8,128)(2,1)S(1)}, bf16[128,512]{1,0:T(8,128)(2,1)S(1)}, u32[]{:S(2)}, u32[]{:S(2)}) collective-permute-start(bf16[128,512]{1,0:T(8,128)(2,1)S(1)} %get-tuple-element.68.refs_0_), channel_id=1, source_target_pairs={{0,8},{1,33},{2,10},{3,35},{4,12},{5,37},{6,14},{7,39},{8,16},{9,4... | collective-permute-start | bytes 393224 | tf_op jit(solution)/shard_map/ppermute | solution.py:52
  34.5 9.1 %collective-permute-start.19 = (bf16[512,512]{1,0:T(8,128)(2,1)S(1)}, bf16[512,512]{1,0:T(8,128)(2,1)S(1)}, u32[]{:S(2)}, u32[]{:S(2)}) collective-permute-start(bf16[512,512]{1,0:T(8,128)(2,1)S(1)} %stack_rows.3.refs_4_), channel_id=1, source_target_pairs={{0,96},{1,25},{2,98},{3,27},{4,100},{5,29},{6,102},{7,31},{8,104},... | collective-permute-start | bytes 1572872 | tf_op jit(solution)/shard_map/ppermute | solution.py:52
  37.5 9.5 %collective-permute-start.12 = (bf16[512,512]{1,0:T(8,128)(2,1)S(1)}, bf16[512,512]{1,0:T(8,128)(2,1)S(1)}, u32[]{:S(2)}, u32[]{:S(2)}) collective-permute-start(bf16[512,512]{1,0:T(8,128)(2,1)S(1)} %stack_rows.2.refs_0_), channel_id=1, source_target_pairs={{0,32},{1,9},{2,34},{3,11},{4,36},{5,13},{6,38},{7,15},{8,40},{9,1... | collective-permute-start | bytes 1572872 | tf_op jit(solution)/shard_map/ppermute | solution.py:52
  37.5 15.2 %collective-permute-start.18 = (bf16[512,512]{1,0:T(8,128)(2,1)S(1)}, bf16[512,512]{1,0:T(8,128)(2,1)S(1)}, u32[]{:S(2)}, u32[]{:S(2)}) collective-permute-start(bf16[512,512]{1,0:T(8,128)(2,1)S(1)} %stack_rows.3.refs_4_), channel_id=1, source_target_pairs={{0,32},{1,9},{2,34},{3,11},{4,36},{5,13},{6,38},{7,15},{8,40},{9,1... | collective-permute-start | bytes 1572872 | tf_op jit(solution)/shard_map/ppermute | solution.py:52
  37.5 15.2 %collective-permute-start.13 = (bf16[512,512]{1,0:T(8,128)(2,1)S(1)}, bf16[512,512]{1,0:T(8,128)(2,1)S(1)}, u32[]{:S(2)}, u32[]{:S(2)}) collective-permute-start(bf16[512,512]{1,0:T(8,128)(2,1)S(1)} %stack_rows.2.refs_0_), channel_id=1, source_target_pairs={{0,96},{1,25},{2,98},{3,27},{4,100},{5,29},{6,102},{7,31},{8,104},... | collective-permute-start | bytes 1572872 | tf_op jit(solution)/shard_map/ppermute | solution.py:52
  43.7 11.2 %collective-permute-start.20 = (bf16[512,512]{1,0:T(8,128)(2,1)S(1)}, bf16[512,512]{1,0:T(8,128)(2,1)S(1)}, u32[]{:S(2)}, u32[]{:S(2)}) collective-permute-start(bf16[512,512]{1,0:T(8,128)(2,1)S(1)} %collective-permute-done.19.refs_6_), channel_id=1, source_target_pairs={{0,96},{1,25},{2,98},{3,27},{4,100},{5,29},{6,102},{7,31},{8,104},... | collective-permute-start | bytes 1572872 | tf_op jit(solution)/shard_map/ppermute | solution.py:52
  47.1 11.2 %collective-permute-start.14 = (bf16[512,512]{1,0:T(8,128)(2,1)S(1)}, bf16[512,512]{1,0:T(8,128)(2,1)S(1)}, u32[]{:S(2)}, u32[]{:S(2)}) collective-permute-start(bf16[512,512]{1,0:T(8,128)(2,1)S(1)} %collective-permute-done.12.refs_1_), channel_id=1, source_target_pairs={{0,32},{1,9},{2,34},{3,11},{4,36},{5,13},{6,38},{7,15},{8,40},{9,1... | collective-permute-start | bytes 1572872 | tf_op jit(solution)/shard_map/ppermute | solution.py:52
  59.6 6.5 %collective-permute-start.21 = (bf16[4,64,512]{2,1,0:T(8,128)(2,1)S(1)}, bf16[4,64,512]{2,1,0:T(8,128)(2,1)S(1)}, u32[]{:S(2)}, u32[]{:S(2)}) collective-permute-start(bf16[4,64,512]{2,1,0:T(8,128)(2,1)S(1)} %get-tuple-element.70), channel_id=1, source_target_pairs={{0,1},{1,0},{2,3},{3,2},{4,5},{5,4},{6,7},{7,6},{8,9},{9,8},{10,11... | collective-permute-start | bytes 786440 | tf_op jit(solution)/shard_map/ppermute | solution.py:72
  81.5 17.3 %collective-permute-start.27 = (bf16[448,1024]{1,0:T(8,128)(2,1)S(1)}, bf16[448,1024]{1,0:T(8,128)(2,1)S(1)}, u32[]{:S(2)}, u32[]{:S(2)}) collective-permute-start(bf16[448,1024]{1,0:T(8,128)(2,1)S(1)} %collective-permute-done.10.refs_5_), channel_id=1, source_target_pairs={{0,8},{1,25},{2,10},{3,27},{4,12},{5,29},{6,14},{7,31},{8,16},{9,1... | collective-permute-start | bytes 2752520 | tf_op jit(solution)/shard_map/ppermute | solution.py:52
  90.4 6.1 %collective-permute-start.25 = (bf16[64,1024]{1,0:T(8,128)(2,1)S(1)}, bf16[64,1024]{1,0:T(8,128)(2,1)S(1)}, u32[]{:S(2)}, u32[]{:S(2)}) collective-permute-start(bf16[64,1024]{1,0:T(8,128)(2,1)S(1)} %project_values.1.refs_0_), channel_id=1, source_target_pairs={{0,96},{1,33},{2,98},{3,35},{4,100},{5,37},{6,102},{7,39},{8,104},... | collective-permute-start | bytes 393224 | tf_op jit(solution)/shard_map/ppermute | solution.py:52
  100.5 6.5 %collective-permute-start.28 = (bf16[4,4,8,1792]{3,2,1,0:T(8,128)(2,1)S(1)}, bf16[4,4,8,1792]{3,2,1,0:T(8,128)(2,1)S(1)}, u32[]{:S(2)}, u32[]{:S(2)}) collective-permute-start(bf16[4,4,8,1792]{3,2,1,0:T(8,128)(2,1)S(1)} %get-tuple-element.81), channel_id=1, source_target_pairs={{0,1},{1,0},{2,3},{3,2},{4,5},{5,4},{6,7},{7,6},{8,9},{9,8},{10,11... | collective-permute-start | bytes 1376264 | tf_op jit(solution)/shard_map/ppermute | solution.py:72
  124.5 7.6 %collective-permute-start.36 = (bf16[8,7168]{1,0:T(8,128)(2,1)S(1)}, bf16[8,7168]{1,0:T(8,128)(2,1)S(1)}, u32[]{:S(2)}, u32[]{:S(2)}) collective-permute-start(bf16[8,7168]{1,0:T(8,128)(2,1)S(1)} %join_columns.1.refs_0_), channel_id=1, source_target_pairs={{0,6},{1,3},{2,0},{3,5},{4,2},{5,7},{6,4},{7,1},{8,14},{9,11},{10,... | collective-permute-start | bytes 344072 | tf_op jit(solution)/shard_map/ppermute | solution.py:52
  126.2 6.4 %collective-permute-start.37 = (bf16[8,7168]{1,0:T(8,128)(2,1)S(1)}, bf16[8,7168]{1,0:T(8,128)(2,1)S(1)}, u32[]{:S(2)}, u32[]{:S(2)}) collective-permute-start(bf16[8,7168]{1,0:T(8,128)(2,1)S(1)} %collective-permute-done.35.refs_1_), channel_id=1, source_target_pairs={{0,2},{1,7},{2,4},{3,1},{4,6},{5,3},{6,0},{7,5},{8,10},{9,15},{10,... | collective-permute-start | bytes 344072 | tf_op jit(solution)/shard_map/ppermute | solution.py:52
  129.3 8.8 %collective-permute-start.38 = (bf16[8,7168]{1,0:T(8,128)(2,1)S(1)}, bf16[8,7168]{1,0:T(8,128)(2,1)S(1)}, u32[]{:S(2)}, u32[]{:S(2)}) collective-permute-start(bf16[8,7168]{1,0:T(8,128)(2,1)S(1)} %join_columns.1.refs_0_), channel_id=1, source_target_pairs={{0,1},{1,0},{2,3},{3,2},{4,5},{5,4},{6,7},{7,6},{8,9},{9,8},{10,11... | collective-permute-start | bytes 344072 | tf_op jit(solution)/shard_map/ppermute | solution.py:72
  132.1 6.0 %collective-permute-start.39 = (bf16[8,7168]{1,0:T(8,128)(2,1)S(1)}, bf16[8,7168]{1,0:T(8,128)(2,1)S(1)}, u32[]{:S(2)}, u32[]{:S(2)}) collective-permute-start(bf16[8,7168]{1,0:T(8,128)(2,1)S(1)} %collective-permute-done.35.refs_1_), channel_id=1, source_target_pairs={{0,1},{1,0},{2,3},{3,2},{4,5},{5,4},{6,7},{7,6},{8,9},{9,8},{10,11... | collective-permute-start | bytes 344072 | tf_op jit(solution)/shard_map/ppermute | solution.py:72
  132.1 6.0 %collective-permute-start.40 = (bf16[8,7168]{1,0:T(8,128)(2,1)S(1)}, bf16[8,7168]{1,0:T(8,128)(2,1)S(1)}, u32[]{:S(2)}, u32[]{:S(2)}) collective-permute-start(bf16[8,7168]{1,0:T(8,128)(2,1)S(1)} %collective-permute-done.36.refs_2_), channel_id=1, source_target_pairs={{0,1},{1,0},{2,3},{3,2},{4,5},{5,4},{6,7},{7,6},{8,9},{9,8},{10,11... | collective-permute-start | bytes 344072 | tf_op jit(solution)/shard_map/ppermute | solution.py:72
  132.7 6.4 %collective-permute-start.41 = (bf16[8,7168]{1,0:T(8,128)(2,1)S(1)}, bf16[8,7168]{1,0:T(8,128)(2,1)S(1)}, u32[]{:S(2)}, u32[]{:S(2)}) collective-permute-start(bf16[8,7168]{1,0:T(8,128)(2,1)S(1)} %collective-permute-done.37.refs_3_), channel_id=1, source_target_pairs={{0,1},{1,0},{2,3},{3,2},{4,5},{5,4},{6,7},{7,6},{8,9},{9,8},{10,11... | collective-permute-start | bytes 344072 | tf_op jit(solution)/shard_map/ppermute | solution.py:72
  (25 other events, 368.2 us)

commit v5 on v4

--- a/solution.py
+++ b/solution.py
@@ -330,10 +330,11 @@
     r_got,
     nl_ref,
     nr_ref,
+    vw_own,
+    vw_got,
     lat_hbm,
     rope_hbm,
-    keep_ref,
-    send_ref,
+    out_ref,
     lat_buf,
     rope_buf,
     q_buf,
@@ -341,6 +342,7 @@
     acc,
     m_ref,
     l_ref,
+    flat,
     p0,
     p1,
     a0,
@@ -477,21 +479,39 @@
         gather(2 * pairs, p0, a0)
 
     for s in range(seqs):
-        mixed = (acc[s] / jnp.sum(l_ref[s], axis=1, keepdims=True)).astype(BF16)
-        keep_ref[s] = mixed[:part]
-        send_ref[s] = mixed[part:]
-
-
-def attention(order, lengths, q_own, q_got, r_own, r_got, nl, nr, lat, rope, steps):
+        acc[s] = acc[s] / jnp.sum(l_ref[s], axis=1, keepdims=True)
+    cols = vw_own.shape[1]
+    for k, vw in enumerate((vw_own, vw_got)):
+        for h in range(cols // HDIM):
+            at = k * part + h * steps
+            mixed = acc[:, at : at + steps, :].reshape(seqs * steps, -1).astype(BF16)
+            value = dot(mixed, vw[:, h * HDIM : (h + 1) * HDIM], NN)
+            flat[:, k * cols + h * HDIM : k * cols + (h + 1) * HDIM] = value.astype(BF16)
+    _, _, y, core = here()
+    count = seqs * steps
+    each = steps // SIDE
+    row = lax.broadcasted_iota(jnp.int32, (count, count), 0)
+    col = lax.broadcasted_iota(jnp.int32, (count, count), 1)
+    step = jnp.zeros((count, count), jnp.int32)
+    for j, place in enumerate(turned(y, 1 - 2 * core)):
+        step = jnp.where(lax.div(row, each * seqs) == j, each * place, step)
+    step += lax.rem(lax.div(row, seqs), each)
+    same = (step == lax.rem(col, steps)) & (lax.rem(row, seqs) == lax.div(col, steps))
+    pick = jnp.where(same, 1.0, 0.0).astype(BF16)
+    out_ref[...] = dot(pick, flat[...], NN).astype(BF16)
+
+
+def attention(order, lengths, q_own, q_got, r_own, r_got, nl, nr, vw_own, vw_got, lat, rope):
     seqs, part, lat_rank = q_own.shape
     rows = 2 * part
     most = seqs * (lat.shape[1] // BLOCK) + 1
-    out = jax.ShapeDtypeStruct(q_own.shape, BF16)
+    steps = part * HDIM // vw_own.shape[1]
+    out = jax.ShapeDtypeStruct((seqs * steps, 2 * vw_own.shape[1]), BF16)
     return pl.pallas_call(
         functools.partial(attention_body, steps=steps),
-        in_specs=[SMEM, SMEM] + [VMEM] * 6 + [HBM] * 2,
-        out_specs=[VMEM] * 2,
-        out_shape=[out] * 2,
+        in_specs=[SMEM, SMEM] + [VMEM] * 8 + [HBM] * 2,
+        out_specs=VMEM,
+        out_shape=out,
         scratch_shapes=[
             pltpu.VMEM((SLOTS, BLOCK, lat_rank), BF16),
             pltpu.VMEM((SLOTS, ROPE, BLOCK), BF16),
@@ -500,6 +520,7 @@
             pltpu.VMEM((seqs, rows, lat_rank), F32),
             pltpu.VMEM((seqs, rows, 128), F32),
             pltpu.VMEM((seqs, rows, 128), F32),
+            pltpu.VMEM(out.shape, BF16),
             pltpu.VMEM((rows, BLOCK), BF16),
             pltpu.VMEM((rows, BLOCK), BF16),
             pltpu.VMEM((rows, 128), F32),
@@ -511,115 +532,61 @@
         ],
         compiler_params=room(40),
         name="attention",
-    )(order, lengths, q_own, q_got, r_own, r_got, nl, nr, in_hbm(lat), in_hbm(rope))
-
-
-def values_body(order_ref, own, got, vw_ref, out_ref, mixed, flat):
-    half, rows, lat_rank = own.shape
-    seqs = 2 * half
-    heads = vw_ref.shape[1] // HDIM
-    steps = rows // heads
-    mixed[:half] = own[...].astype(F32)
-    mixed[half:] = got[...].astype(F32)
-    for h in range(heads):
-        cols = slice(h * HDIM, (h + 1) * HDIM)
-        part = mixed[:, h * steps : (h + 1) * steps, :].reshape(seqs * steps, lat_rank)
-        flat[:, cols] = dot(part.astype(BF16), vw_ref[:, cols], NN).astype(BF16)
-    _, _, y, core = here()
-    sign = 1 - 2 * core
-    step_of = [2 * v + (1 - core) for v in turned(y, -sign)]
-    step_of += [2 * v + core for v in turned(y, sign)]
-    count = seqs * steps
-    row = lax.broadcasted_iota(jnp.int32, (count, count), 0)
-    col = lax.broadcasted_iota(jnp.int32, (count, count), 1)
-    want_step = jnp.zeros((count, count), jnp.int32)
-    want_seq = jnp.zeros((count, count), jnp.int32)
-    for k in range(steps):
-        want_step = jnp.where(lax.div(row, seqs) == k, step_of[k], want_step)
-    for k in range(seqs):
-        want_seq = jnp.where(lax.div(col, steps) == k, order_ref[k], want_seq)
-    same = (want_step == lax.rem(col, steps)) & (want_seq == lax.rem(row, seqs))
-    pick = jnp.where(same, 1.0, 0.0).astype(BF16)
-    out_ref[...] = dot(pick, flat[...], NN).astype(BF16)
-
-
-def project_values(order, own, got, vw):
-    half, rows, lat_rank = own.shape
-    cols = vw.shape[1]
-    count = 2 * half * rows * HDIM // cols
-    return pl.pallas_call(
-        values_body,
-        in_specs=[SMEM] + [VMEM] * 3,
-        out_specs=VMEM,
-        out_shape=jax.ShapeDtypeStruct((count, cols), BF16),
-        scratch_shapes=[
-            pltpu.VMEM((2 * half, rows, lat_rank), F32),
-            pltpu.VMEM((count, cols), BF16),
-        ],
-        compiler_params=room(12),
-        name="project_values",
-    )(order, own, got, vw)
-
-
-def output_body(*refs, seqs):
-    tokens, weights = refs[:4], refs[4:8]
-    send_ref, keep_ref, v_buf, w_buf = refs[8:]
+    )(
+        order,
+        lengths,
+        q_own,
+        q_got,
+        r_own,
+        r_got,
+        nl,
+        nr,
+        vw_own,
+        vw_got,
+        in_hbm(lat),
+        in_hbm(rope),
+    )
+
+
+def output_body(*refs, rows):
+    tokens, own_w, got_w, outs = refs[:4], refs[4:8], refs[8:12], refs[12:16]
+    v_buf, w_buf = refs[16:]
     _, x, _, core = here()
     sign = 1 - 2 * core
-    v_buf[0] = tokens[0][...]
-    v_buf[lax.rem(SIDE - sign, SIDE)] = tokens[1][...]
-    v_buf[lax.rem(SIDE + sign, SIDE)] = tokens[2][...]
-    v_buf[2] = tokens[3][...]
-    depth = v_buf.shape[2]
-    part = weights[0].shape[0]
-    for k, offset in enumerate((0, SIDE - sign, SIDE + sign, 2)):
-        at = pl.multiple_of(lax.rem(x + offset, SIDE) * part, 64)
-        w_buf[pl.ds(at, part), :] = weights[k][...]
-    tokens_all = v_buf[...].reshape(-1, depth)
+    for place, ref in zip(turned(0, -sign), tokens):
+        v_buf[place] = ref[...]
+    part, depth = own_w[0].shape
+    for k, (weights, way) in enumerate(((own_w, -sign), (got_w, sign))):
+        for place, ref in zip(turned(x, way), weights):
+            at = pl.multiple_of(place * part, 64)
+            w_buf[pl.ds(at, part), k * depth : (k + 1) * depth] = ref[...]
+    tokens_all = v_buf[...].reshape(-1, v_buf.shape[2])
     width = 256
     for n in range(w_buf.shape[0] // width):
         cols = slice(n * width, (n + 1) * width)
-        res = dot(tokens_all, w_buf[cols, :], NT).reshape(SIDE, 2 * SIDE, seqs, width)
-        for b in range(SIDE):
+        res = dot(tokens_all, w_buf[cols, :], NT).reshape(SIDE, SIDE, rows, width)
+        for j in range(SIDE):
             for z in range(SIDE):
-                send_ref[b, z, :, cols] = res[z, b].astype(BF16)
-                keep_ref[b, z, :, cols] = res[z, SIDE + b].astype(BF16)
-
-
-def output_blocks(tokens, weights, seqs):
+                outs[j][z, :, cols] = res[z, j].astype(BF16)
+
+
+def output_blocks(tokens, own_w, got_w):
     count, depth = tokens[0].shape
-    cols = SIDE * weights[0].shape[0]
-    out = jax.ShapeDtypeStruct((SIDE, SIDE, seqs, cols), BF16)
-    return pl.pallas_call(
-        functools.partial(output_body, seqs=seqs),
-        in_specs=[VMEM] * 8,
-        out_specs=[VMEM] * 2,
-        out_shape=[out] * 2,
+    cols = SIDE * own_w[0].shape[0]
+    rows = count // SIDE
+    out = jax.ShapeDtypeStruct((SIDE, rows, cols), BF16)
+    return pl.pallas_call(
+        functools.partial(output_body, rows=rows),
+        in_specs=[VMEM] * 12,
+        out_specs=[VMEM] * 4,
+        out_shape=[out] * 4,
         scratch_shapes=[
             pltpu.VMEM((SIDE, count, depth), BF16),
             pltpu.VMEM((cols, depth), BF16),
         ],
-        compiler_params=room(16),
+        compiler_params=room(24),
         name="output_blocks",
-    )(*tokens, *weights)
-
-
-def add_blocks_body(keep, got, *outs):
-    for j in (3, 2, 1, 0):
-        for k in range(SIDE):
-            outs[j][k] = (keep[j, k].astype(F32) + got[j, k].astype(F32)).astype(BF16)
-
-
-def add_blocks(keep, got):
-    one = jax.ShapeDtypeStruct(got.shape[1:], BF16)
-    return pl.pallas_call(
-        add_blocks_body,
-        in_specs=[VMEM] * 2,
-        out_specs=[VMEM] * 4,
-        out_shape=[one] * 4,
-        compiler_params=room(8),
-        name="add_blocks",
-    )(keep, got)
+    )(*tokens, *own_w, *got_w)
 
 
 def total_body(a, b, c, *outs):
@@ -660,25 +627,47 @@
     )(*blocks)
 
 
-def settle_body(*refs):
-    out = refs[-1]
+def settle_body(order_ref, *refs):
+    blocks, out, buf = refs[:8], refs[8], refs[9]
+    steps, seqs, cols = out.shape
+    half = seqs // 2
+    each = steps // SIDE
+    count = steps * seqs
+    size = each * half
     _, _, y, core = here()
     sign = 1 - 2 * core
-    steps = [2 * v + core for v in turned(y, -sign)]
-    steps += [2 * v + (1 - core) for v in turned(y, sign)]
-    for step, ref in zip(steps, refs[:-1]):
-        out[step] = ref[...]
-
-
-def settle(blocks):
+    for k, ref in enumerate(blocks):
+        buf[k * size : (k + 1) * size, :] = ref[...].astype(F32)
+    row = lax.broadcasted_iota(jnp.int32, (count, count), 0)
+    col = lax.broadcasted_iota(jnp.int32, (count, count), 1)
+    step = jnp.zeros((count, count), jnp.int32)
+    for k, place in enumerate(turned(y, -sign) + turned(y, sign)):
+        step = jnp.where(lax.div(col, size) == k, each * place, step)
+    step += lax.rem(lax.div(col, half), each)
+    place = half * lax.div(col, SIDE * size) + lax.rem(col, half)
+    seq = jnp.zeros((count, count), jnp.int32)
+    for k in range(seqs):
+        seq = jnp.where(place == k, order_ref[k], seq)
+    same = (step == lax.div(row, seqs)) & (seq == lax.rem(row, seqs))
+    pick = jnp.where(same, 1.0, 0.0).astype(BF16)
+    width = 1024
+    for n in range(cols // width):
+        part = slice(n * width, (n + 1) * width)
+        res = dot(pick, buf[:, part].astype(BF16), NN)
+        out[:, :, part] = res.reshape(steps, seqs, width).astype(BF16)
+
+
+def settle(order, blocks):
+    rows, cols = blocks[0].shape
     return pl.pallas_call(
         settle_body,
-        in_specs=[VMEM] * 8,
+        in_specs=[SMEM] + [VMEM] * 8,
         out_specs=VMEM,
-        out_shape=jax.ShapeDtypeStruct((8,) + blocks[0].shape, BF16),
-        compiler_params=room(8),
+        out_shape=jax.ShapeDtypeStruct((rows, 8, cols), BF16),
+        scratch_shapes=[pltpu.VMEM((8 * rows, cols), F32)],
+        compiler_params=room(12),
         name="settle",
-    )(*blocks)
+    )(order, *blocks)
 
 
 def splits(seqs):
@@ -838,26 +827,32 @@
     units += more
 
     w_rows = SIDE * SIDE * params.shape[0]
+    by_seq, r_got, vw_got = lax.optimization_barrier((by_seq, r_got, other_core(value_weight)))
     q_own, q_send = queries(by_seq, units, w_rows, seq_local, q_rank)
-    mixed, mixed_send = attention(
+    w_one, q_send = lax.optimization_barrier((w_one, q_send))
+    w_three = forth(w_one, "x")
+    q_got, *early = lax.optimization_barrier((other_core(q_send), w_t, w_one, w_two))
+    got_w = [other_core(w) for w in early]
+    values = attention(
         order,
         lengths_in,
         q_own,
-        other_core(q_send),
+        q_got,
         r_own,
         r_got,
         nl,
         nr,
+        value_weight,
+        vw_got,
         latent_cache,
         rope_cache,
-        steps_n,
     )
-    w_one, mixed = lax.optimization_barrier((w_one, mixed))
-    out_weights = (w_t, w_one, w_two, forth(w_one, "x"))
-    values = project_values(order, mixed, other_core(mixed_send), value_weight)
-
-    send, keep = output_blocks(ring(values, "z"), out_weights, seq_local)
-    own, *sums = add_blocks(keep, other_core(send))
+
+    *got_w, w_three, values = lax.optimization_barrier((*got_w, w_three, values))
+    own_w = (w_t, w_one, w_two, w_three)
+    tokens = ring(values, "z")
+    got_w.append(other_core(w_three))
+    own, *sums = output_blocks(tokens, own_w, got_w)
     blocks = total_blocks((own,) + ring_sum(sums, "y"))
 
     arrived = [blocks[0]]
@@ -872,7 +867,7 @@
 
     column = list(ring(mine, "y"))
     column += [other_core(b) for b in column]
-    decoded = settle(column)
+    decoded = settle(order, column)
     return (new_params, new_one, new_two, decoded)
 
 

time: 139 us -> 139 us (level)
  waiting for transfers between devices: 38.3 us -> 30.1 us
  Pallas kernels: 26.4 us -> 32 us
    ppermute x30, waiting for transfers between devices: 31.6 us -> 25.8 us  [shift(): return lax.ppermute(v, ('fsdp', 'head'), moves(step))]
    pallas_call x1, Pallas kernels: 15.4 us -> 19.6 us  [attention(): pl.pallas_call(functools.partial(attention_body, steps=steps), in_specs=[...]
    ppermute x9 -> x12, starting transfers between devices: 24.9 us -> 28.8 us  [other_core(): return lax.ppermute(v, 'head', [(i, i ^ 1) for i in range(2 * SIDE)])]
    ppermute x30, starting transfers between devices: 46.7 us -> 44.1 us  [shift(): return lax.ppermute(v, ('fsdp', 'head'), moves(step))]
    ppermute x9 -> x12, waiting for transfers between devices: 4.55 us -> 1.88 us  [other_core(): return lax.ppermute(v, 'head', [(i, i ^ 1) for i in range(2 * SIDE)])]
    pallas_call x4 -> x2, Pallas kernels: 3.84 us -> 5.18 us  [the longest x1 3.32 us: output_blocks(): pl.pallas_call(functools.partial(output_body, rows=rows), in_specs=[VMEM]...]
  transfers between devices with their start and end apart: 42 -> 45, of which waited for: 24 -> 19; matrix products, arithmetic and copies ran while one was open for 0% -> 0% of each run, Pallas kernels for 3% -> 17%
where the time goes in v5:
time: 139 us
  starting transfers between devices  75.6 us (54%)
  Pallas kernels  32 us (23%)
  waiting for transfers between devices  30.1 us (22%)
    ppermute x30, starting transfers between devices, shift(): return lax.ppermute(v, ('fsdp', 'head'), moves(step))  44.1 us
    ppermute x12, starting transfers between devices, other_core(): return lax.ppermute(v, 'head', [(i, i ^ 1) for i in range(2 * SIDE)])  28.8 us
    ppermute x30, waiting for transfers between devices, shift(): return lax.ppermute(v, ('fsdp', 'head'), moves(step))  25.8 us
    pallas_call x1, Pallas kernels, attention(): pl.pallas_call(functools.partial(attention_body, steps=steps), in_specs=[...  19.6 us
    pallas_call x1, Pallas kernels, output_blocks(): pl.pallas_call(functools.partial(output_body, rows=rows), in_specs=[VMEM]...  3.32 us
  transfers between devices with their start and end apart: 45, of which 19 were waited for; matrix products, arithmetic and copies ran while one was open for 0% of the time, Pallas kernels for 17%

profile of v5, /device:TPU:1, one launch (start us, length us, event | category | flops | bytes accessed | tf_op | source)
XLA Modules:
  0.0 138.7 jit_solution(5735296743622499764)
XLA Ops:
  0.7 2.3 %pack_columns.1 = (bf16[4,128,1024]{2,1,0:T(8,128)(2,1)S(1)}, bf16[4,128,1024]{2,1,0:T(8,128)(2,1)S(1)}, f32[128,1024]{1,0:T(8,128)S(1)}, f32[128,1024]{1,0:T(8,128)S(1)}, f32[128,1024]{1,0:T(8,128)S(1)}) custom-call(bf16[128,8192]{1,0:T(8,128)(2,1)} %bitcast.6, f32[128,1024]{1,0:T(8,128)} %p.1, f32[128,1024]{1,0:T(8,128)} %one.1, f32[128,1024]{1,0:T(8,128)} %two.1), custom_call_target="tpu_custom_call" | custom-call | tf_op jit(solution)/shard_map/pack_columns/pallas_call | solution.py:153
  7.4 2.9 %collective-permute-start.1 = (bf16[128,512]{1,0:T(8,128)(2,1)S(1)}, bf16[128,512]{1,0:T(8,128)(2,1)S(1)}, u32[]{:S(2)}, u32[]{:S(2)}) collective-permute-start(bf16[128,512]{1,0:T(8,128)(2,1)S(1)} %get-tuple-element.59), channel_id=1, source_target_pairs={{0,2},{1,7},{2,4},{3,1},{4,6},{5,3},{6,0},{7,5},{8,10},{9,15},{10,... | collective-permute-start | bytes 393224 | tf_op jit(solution)/shard_map/ppermute | solution.py:52
  12.3 3.4 %collective-permute-start.2 = (bf16[128,512]{1,0:T(8,128)(2,1)S(1)}, bf16[128,512]{1,0:T(8,128)(2,1)S(1)}, u32[]{:S(2)}, u32[]{:S(2)}) collective-permute-start(bf16[128,512]{1,0:T(8,128)(2,1)S(1)} %add_two.3), channel_id=1, source_target_pairs={{0,2},{1,7},{2,4},{3,1},{4,6},{5,3},{6,0},{7,5},{8,10},{9,15},{10,... | collective-permute-start | bytes 393224 | tf_op jit(solution)/shard_map/ppermute | solution.py:52
  21.2 3.8 %collective-permute-start.8 = (bf16[128,512]{1,0:T(8,128)(2,1)S(1)}, bf16[128,512]{1,0:T(8,128)(2,1)S(1)}, u32[]{:S(2)}, u32[]{:S(2)}) collective-permute-start(bf16[128,512]{1,0:T(8,128)(2,1)S(1)} %adam_first.1.after.refs_0_), channel_id=1, source_target_pairs={{0,24},{1,97},{2,26},{3,99},{4,28},{5,101},{6,30},{7,103},{8,0},{9... | collective-permute-start | bytes 393224 | tf_op jit(solution)/shard_map/ppermute | solution.py:52
  27.8 2.6 %collective-permute-done.18.refs_2_ = bf16[128,512]{1,0:T(8,128)(2,1)S(1)} collective-permute-done((bf16[128,512]{1,0:T(8,128)(2,1)S(1)}, bf16[128,512]{1,0:T(8,128)(2,1)S(1)}, u32[]{:S(2)}, u32[]{:S(2)}) %collective-permute-start.18) | collective-permute-done | bytes 131104 | tf_op jit(solution)/shard_map/ppermute | solution.py:52
  32.3 4.0 %collective-permute-start.13 = (bf16[512,1024]{1,0:T(8,128)(2,1)S(1)}, bf16[512,1024]{1,0:T(8,128)(2,1)S(1)}, u32[]{:S(2)}, u32[]{:S(2)}) collective-permute-start(bf16[512,1024]{1,0:T(8,128)(2,1)S(1)} %copy-done.1), channel_id=1, source_target_pairs={{0,1},{1,0},{2,3},{3,2},{4,5},{5,4},{6,7},{7,6},{8,9},{9,8},{10,11... | collective-permute-start | bytes 3145736 | tf_op jit(solution)/shard_map/ppermute | solution.py:72
  37.9 2.6 %collective-permute-start.15 = (bf16[512,512]{1,0:T(8,128)(2,1)S(1)}, bf16[512,512]{1,0:T(8,128)(2,1)S(1)}, u32[]{:S(2)}, u32[]{:S(2)}) collective-permute-start(bf16[512,512]{1,0:T(8,128)(2,1)S(1)} %stack_rows.2.refs_0_), channel_id=1, source_target_pairs={{0,96},{1,25},{2,98},{3,27},{4,100},{5,29},{6,102},{7,31},{8,104},... | collective-permute-start | bytes 1572872 | tf_op jit(solution)/shard_map/ppermute | solution.py:52
  40.6 4.2 %collective-permute-done.21.refs_6_ = bf16[512,512]{1,0:T(8,128)(2,1)S(1)} collective-permute-done((bf16[512,512]{1,0:T(8,128)(2,1)S(1)}, bf16[512,512]{1,0:T(8,128)(2,1)S(1)}, u32[]{:S(2)}, u32[]{:S(2)}) %collective-permute-start.21) | collective-permute-done | bytes 524320 | tf_op jit(solution)/shard_map/ppermute | solution.py:52
  44.8 2.0 %collective-permute-start.22 = (bf16[512,512]{1,0:T(8,128)(2,1)S(1)}, bf16[512,512]{1,0:T(8,128)(2,1)S(1)}, u32[]{:S(2)}, u32[]{:S(2)}) collective-permute-start(bf16[512,512]{1,0:T(8,128)(2,1)S(1)} %collective-permute-done.21.refs_6_), channel_id=1, source_target_pairs={{0,96},{1,25},{2,98},{3,27},{4,100},{5,29},{6,102},{7,31},{8,104},... | collective-permute-start | bytes 1572872 | tf_op jit(solution)/shard_map/ppermute | solution.py:52
  48.8 5.3 %collective-permute-start.12 = (bf16[4,64,64]{2,1,0:T(8,128)(2,1)S(1)}, bf16[4,64,64]{2,1,0:T(8,128)(2,1)S(1)}, u32[]{:S(2)}, u32[]{:S(2)}) collective-permute-start(bf16[4,64,64]{2,1,0:T(8,128)(2,1)S(1)} %get-tuple-element.74), channel_id=1, source_target_pairs={{0,1},{1,0},{2,3},{3,2},{4,5},{5,4},{6,7},{7,6},{8,9},{9,8},{10,11... | collective-permute-start | bytes 98312 | tf_op jit(solution)/shard_map/ppermute | solution.py:72
  56.0 2.3 %collective-permute-done.16.refs_3_ = bf16[512,512]{1,0:T(8,128)(2,1)S(1)} collective-permute-done((bf16[512,512]{1,0:T(8,128)(2,1)S(1)}, bf16[512,512]{1,0:T(8,128)(2,1)S(1)}, u32[]{:S(2)}, u32[]{:S(2)}) %collective-permute-start.16) | collective-permute-done | bytes 524320 | tf_op jit(solution)/shard_map/ppermute | solution.py:52
  59.7 5.2 %collective-permute-start.23 = (bf16[4,64,512]{2,1,0:T(8,128)(2,1)S(1)}, bf16[4,64,512]{2,1,0:T(8,128)(2,1)S(1)}, u32[]{:S(2)}, u32[]{:S(2)}) collective-permute-start(bf16[4,64,512]{2,1,0:T(8,128)(2,1)S(1)} %get-tuple-element.79), channel_id=1, source_target_pairs={{0,1},{1,0},{2,3},{3,2},{4,5},{5,4},{6,7},{7,6},{8,9},{9,8},{10,11... | collective-permute-start | bytes 786440 | tf_op jit(solution)/shard_map/ppermute | solution.py:72
  64.9 2.8 %collective-permute-start.27 = (bf16[448,1024]{1,0:T(8,128)(2,1)S(1)}, bf16[448,1024]{1,0:T(8,128)(2,1)S(1)}, u32[]{:S(2)}, u32[]{:S(2)}) collective-permute-start(bf16[448,1024]{1,0:T(8,128)(2,1)S(1)} %collective-permute-done.10.refs_5_), channel_id=1, source_target_pairs={{0,8},{1,25},{2,10},{3,27},{4,12},{5,29},{6,14},{7,31},{8,16},{9,1... | collective-permute-start | bytes 2752520 | tf_op jit(solution)/shard_map/ppermute | solution.py:52
  68.4 19.6 %attention.1.refs_0_ = bf16[32,2048]{1,0:T(8,128)(2,1)S(1)} custom-call(s32[8]{0:T(128)S(1)} %get-tuple-element.71.order_ref, s32[8]{0:T(128)S(1)} %get-tuple-element.85.len_ref, bf16[4,64,512]{2,1,0:T(8,128)(2,1)S(1)} %get-tuple-element.86.q_own, bf16[4,64,512]{2,1,0:T(8,128)(2,1)S(1)} %collective-permute-done.23.q_got, ...), custom_call_target="tpu_custom_call" | custom-call | tf_op jit(solution)/shard_map/attention/pallas_call | solution.py:510
  90.0 3.5 %collective-permute-done.28.refs_1_ = bf16[32,2048]{1,0:T(8,128)(2,1)S(1)} collective-permute-done((bf16[32,2048]{1,0:T(8,128)(2,1)S(1)}, bf16[32,2048]{1,0:T(8,128)(2,1)S(1)}, u32[]{:S(2)}, u32[]{:S(2)}) %collective-permute-start.28) | collective-permute-done | bytes 131104 | tf_op jit(solution)/shard_map/ppermute | solution.py:52
  94.9 2.5 %collective-permute-done.30.refs_3_ = bf16[32,2048]{1,0:T(8,128)(2,1)S(1)} collective-permute-done((bf16[32,2048]{1,0:T(8,128)(2,1)S(1)}, bf16[32,2048]{1,0:T(8,128)(2,1)S(1)}, u32[]{:S(2)}, u32[]{:S(2)}) %collective-permute-start.30) | collective-permute-done | bytes 131104 | tf_op jit(solution)/shard_map/ppermute | solution.py:52
  97.3 3.3 %output_blocks.1 = (bf16[4,8,1792]{2,1,0:T(8,128)(2,1)S(1)}, bf16[4,8,1792]{2,1,0:T(8,128)(2,1)S(1)}, bf16[4,8,1792]{2,1,0:T(8,128)(2,1)S(1)}, bf16[4,8,1792]{2,1,0:T(8,128)(2,1)S(1)}) custom-call(bf16[32,2048]{1,0:T(8,128)(2,1)S(1)} %attention.1.refs_0_, bf16[32,2048]{1,0:T(8,128)(2,1)S(1)} %collective-permute-done.28.refs_1_, ...), custom_call_target="tpu_custom_call" | custom-call | tf_op jit(solution)/shard_map/output_blocks/pallas_call | solution.py:578
  100.7 2.6 %collective-permute-start.32 = (bf16[4,8,1792]{2,1,0:T(8,128)(2,1)S(1)}, bf16[4,8,1792]{2,1,0:T(8,128)(2,1)S(1)}, u32[]{:S(2)}, u32[]{:S(2)}) collective-permute-start(bf16[4,8,1792]{2,1,0:T(8,128)(2,1)S(1)} %get-tuple-element.100), channel_id=1, source_target_pairs={{0,2},{1,7},{2,4},{3,1},{4,6},{5,3},{6,0},{7,5},{8,10},{9,15},{10,... | collective-permute-start | bytes 344072 | tf_op jit(solution)/shard_map/ppermute | solution.py:52
  105.1 3.1 %collective-permute-start.33 = (bf16[4,8,1792]{2,1,0:T(8,128)(2,1)S(1)}, bf16[4,8,1792]{2,1,0:T(8,128)(2,1)S(1)}, u32[]{:S(2)}, u32[]{:S(2)}) collective-permute-start(bf16[4,8,1792]{2,1,0:T(8,128)(2,1)S(1)} %add_two.5), channel_id=1, source_target_pairs={{0,2},{1,7},{2,4},{3,1},{4,6},{5,3},{6,0},{7,5},{8,10},{9,15},{10,... | collective-permute-start | bytes 344072 | tf_op jit(solution)/shard_map/ppermute | solution.py:52
  108.3 2.6 %collective-permute-done.33.b = bf16[4,8,1792]{2,1,0:T(8,128)(2,1)S(1)} collective-permute-done((bf16[4,8,1792]{2,1,0:T(8,128)(2,1)S(1)}, bf16[4,8,1792]{2,1,0:T(8,128)(2,1)S(1)}, u32[]{:S(2)}, u32[]{:S(2)}) %collective-permute-start.33) | collective-permute-done | bytes 114720 | tf_op jit(solution)/shard_map/ppermute | solution.py:52
  116.1 3.2 %collective-permute-start.38 = (bf16[8,7168]{1,0:T(8,128)(2,1)S(1)}, bf16[8,7168]{1,0:T(8,128)(2,1)S(1)}, u32[]{:S(2)}, u32[]{:S(2)}) collective-permute-start(bf16[8,7168]{1,0:T(8,128)(2,1)S(1)} %join_columns.1.refs_0_), channel_id=1, source_target_pairs={{0,2},{1,7},{2,4},{3,1},{4,6},{5,3},{6,0},{7,5},{8,10},{9,15},{10,... | collective-permute-start | bytes 344072 | tf_op jit(solution)/shard_map/ppermute | solution.py:52
  121.1 3.1 %collective-permute-start.40 = (bf16[8,7168]{1,0:T(8,128)(2,1)S(1)}, bf16[8,7168]{1,0:T(8,128)(2,1)S(1)}, u32[]{:S(2)}, u32[]{:S(2)}) collective-permute-start(bf16[8,7168]{1,0:T(8,128)(2,1)S(1)} %collective-permute-done.38.refs_1_), channel_id=1, source_target_pairs={{0,2},{1,7},{2,4},{3,1},{4,6},{5,3},{6,0},{7,5},{8,10},{9,15},{10,... | collective-permute-start | bytes 344072 | tf_op jit(solution)/shard_map/ppermute | solution.py:52
  124.1 5.7 %collective-permute-start.41 = (bf16[8,7168]{1,0:T(8,128)(2,1)S(1)}, bf16[8,7168]{1,0:T(8,128)(2,1)S(1)}, u32[]{:S(2)}, u32[]{:S(2)}) collective-permute-start(bf16[8,7168]{1,0:T(8,128)(2,1)S(1)} %join_columns.1.refs_0_), channel_id=1, source_target_pairs={{0,1},{1,0},{2,3},{3,2},{4,5},{5,4},{6,7},{7,6},{8,9},{9,8},{10,11... | collective-permute-start | bytes 344072 | tf_op jit(solution)/shard_map/ppermute | solution.py:72
  130.4 5.5 %collective-permute-start.44 = (bf16[8,7168]{1,0:T(8,128)(2,1)S(1)}, bf16[8,7168]{1,0:T(8,128)(2,1)S(1)}, u32[]{:S(2)}, u32[]{:S(2)}) collective-permute-start(bf16[8,7168]{1,0:T(8,128)(2,1)S(1)} %collective-permute-done.40.refs_3_), channel_id=1, source_target_pairs={{0,1},{1,0},{2,3},{3,2},{4,5},{5,4},{6,7},{7,6},{8,9},{9,8},{10,11... | collective-permute-start | bytes 344072 | tf_op jit(solution)/shard_map/ppermute | solution.py:72
  (96 shorter events, 39.6 us)
Async XLA Ops:
  4.5 31.8 %collective-permute-start.11 = (bf16[448,1024]{1,0:T(8,128)(2,1)}, bf16[448,1024]{1,0:T(8,128)(2,1)S(1)}, u32[]{:S(2)}, u32[]{:S(2)}) collective-permute-start(bf16[448,1024]{1,0:T(8,128)(2,1)} %bitcast.2), channel_id=1, source_target_pairs={{0,24},{1,9},{2,26},{3,11},{4,28},{5,13},{6,30},{7,15},{8,0},{9,17... | collective-permute-start | bytes 2752520 | tf_op jit(solution)/shard_map/ppermute | solution.py:52
  5.8 30.5 %collective-permute-start.10 = (bf16[448,1024]{1,0:T(8,128)(2,1)}, bf16[448,1024]{1,0:T(8,128)(2,1)S(1)}, u32[]{:S(2)}, u32[]{:S(2)}) collective-permute-start(bf16[448,1024]{1,0:T(8,128)(2,1)} %bitcast.3), channel_id=1, source_target_pairs={{0,8},{1,25},{2,10},{3,27},{4,12},{5,29},{6,14},{7,31},{8,16},{9,1... | collective-permute-start | bytes 2752520 | tf_op jit(solution)/shard_map/ppermute | solution.py:52
  16.5 8.5 %collective-permute-start.5 = (bf16[128,512]{1,0:T(8,128)(2,1)S(1)}, bf16[128,512]{1,0:T(8,128)(2,1)S(1)}, u32[]{:S(2)}, u32[]{:S(2)}) collective-permute-start(bf16[128,512]{1,0:T(8,128)(2,1)S(1)} %add_two.4), channel_id=1, source_target_pairs={{0,2},{1,7},{2,4},{3,1},{4,6},{5,3},{6,0},{7,5},{8,10},{9,15},{10,... | collective-permute-start | bytes 393224 | tf_op jit(solution)/shard_map/ppermute | solution.py:52
  18.7 8.2 %collective-permute-start.7 = (bf16[128,512]{1,0:T(8,128)(2,1)S(1)}, bf16[128,512]{1,0:T(8,128)(2,1)S(1)}, u32[]{:S(2)}, u32[]{:S(2)}) collective-permute-start(bf16[128,512]{1,0:T(8,128)(2,1)S(1)} %adam_first.1.after.refs_0_), channel_id=1, source_target_pairs={{0,8},{1,33},{2,10},{3,35},{4,12},{5,37},{6,14},{7,39},{8,16},{9,4... | collective-permute-start | bytes 393224 | tf_op jit(solution)/shard_map/ppermute | solution.py:52
  21.2 6.6 %collective-permute-start.8 = (bf16[128,512]{1,0:T(8,128)(2,1)S(1)}, bf16[128,512]{1,0:T(8,128)(2,1)S(1)}, u32[]{:S(2)}, u32[]{:S(2)}) collective-permute-start(bf16[128,512]{1,0:T(8,128)(2,1)S(1)} %adam_first.1.after.refs_0_), channel_id=1, source_target_pairs={{0,24},{1,97},{2,26},{3,99},{4,28},{5,101},{6,30},{7,103},{8,0},{9... | collective-permute-start | bytes 393224 | tf_op jit(solution)/shard_map/ppermute | solution.py:52
  27.8 8.6 %collective-permute-start.17 = (bf16[128,512]{1,0:T(8,128)(2,1)S(1)}, bf16[128,512]{1,0:T(8,128)(2,1)S(1)}, u32[]{:S(2)}, u32[]{:S(2)}) collective-permute-start(bf16[128,512]{1,0:T(8,128)(2,1)S(1)} %get-tuple-element.77.refs_0_), channel_id=1, source_target_pairs={{0,8},{1,33},{2,10},{3,35},{4,12},{5,37},{6,14},{7,39},{8,16},{9,4... | collective-permute-start | bytes 393224 | tf_op jit(solution)/shard_map/ppermute | solution.py:52
  32.3 16.5 %collective-permute-start.13 = (bf16[512,1024]{1,0:T(8,128)(2,1)S(1)}, bf16[512,1024]{1,0:T(8,128)(2,1)S(1)}, u32[]{:S(2)}, u32[]{:S(2)}) collective-permute-start(bf16[512,1024]{1,0:T(8,128)(2,1)S(1)} %copy-done.1), channel_id=1, source_target_pairs={{0,1},{1,0},{2,3},{3,2},{4,5},{5,4},{6,7},{7,6},{8,9},{9,8},{10,11... | collective-permute-start | bytes 3145736 | tf_op jit(solution)/shard_map/ppermute | solution.py:72
  36.4 8.4 %collective-permute-start.21 = (bf16[512,512]{1,0:T(8,128)(2,1)S(1)}, bf16[512,512]{1,0:T(8,128)(2,1)S(1)}, u32[]{:S(2)}, u32[]{:S(2)}) collective-permute-start(bf16[512,512]{1,0:T(8,128)(2,1)S(1)} %stack_rows.3.refs_4_), channel_id=1, source_target_pairs={{0,96},{1,25},{2,98},{3,27},{4,100},{5,29},{6,102},{7,31},{8,104},... | collective-permute-start | bytes 1572872 | tf_op jit(solution)/shard_map/ppermute | solution.py:52
  37.6 9.5 %collective-permute-start.14 = (bf16[512,512]{1,0:T(8,128)(2,1)S(1)}, bf16[512,512]{1,0:T(8,128)(2,1)S(1)}, u32[]{:S(2)}, u32[]{:S(2)}) collective-permute-start(bf16[512,512]{1,0:T(8,128)(2,1)S(1)} %stack_rows.2.refs_0_), channel_id=1, source_target_pairs={{0,32},{1,9},{2,34},{3,11},{4,36},{5,13},{6,38},{7,15},{8,40},{9,1... | collective-permute-start | bytes 1572872 | tf_op jit(solution)/shard_map/ppermute | solution.py:52
  37.9 17.1 %collective-permute-start.20 = (bf16[512,512]{1,0:T(8,128)(2,1)S(1)}, bf16[512,512]{1,0:T(8,128)(2,1)S(1)}, u32[]{:S(2)}, u32[]{:S(2)}) collective-permute-start(bf16[512,512]{1,0:T(8,128)(2,1)S(1)} %stack_rows.3.refs_4_), channel_id=1, source_target_pairs={{0,32},{1,9},{2,34},{3,11},{4,36},{5,13},{6,38},{7,15},{8,40},{9,1... | collective-permute-start | bytes 1572872 | tf_op jit(solution)/shard_map/ppermute | solution.py:52
  37.9 17.0 %collective-permute-start.15 = (bf16[512,512]{1,0:T(8,128)(2,1)S(1)}, bf16[512,512]{1,0:T(8,128)(2,1)S(1)}, u32[]{:S(2)}, u32[]{:S(2)}) collective-permute-start(bf16[512,512]{1,0:T(8,128)(2,1)S(1)} %stack_rows.2.refs_0_), channel_id=1, source_target_pairs={{0,96},{1,25},{2,98},{3,27},{4,100},{5,29},{6,102},{7,31},{8,104},... | collective-permute-start | bytes 1572872 | tf_op jit(solution)/shard_map/ppermute | solution.py:52
  44.8 11.2 %collective-permute-start.22 = (bf16[512,512]{1,0:T(8,128)(2,1)S(1)}, bf16[512,512]{1,0:T(8,128)(2,1)S(1)}, u32[]{:S(2)}, u32[]{:S(2)}) collective-permute-start(bf16[512,512]{1,0:T(8,128)(2,1)S(1)} %collective-permute-done.21.refs_6_), channel_id=1, source_target_pairs={{0,96},{1,25},{2,98},{3,27},{4,100},{5,29},{6,102},{7,31},{8,104},... | collective-permute-start | bytes 1572872 | tf_op jit(solution)/shard_map/ppermute | solution.py:52
  47.1 11.2 %collective-permute-start.16 = (bf16[512,512]{1,0:T(8,128)(2,1)S(1)}, bf16[512,512]{1,0:T(8,128)(2,1)S(1)}, u32[]{:S(2)}, u32[]{:S(2)}) collective-permute-start(bf16[512,512]{1,0:T(8,128)(2,1)S(1)} %collective-permute-done.14.refs_1_), channel_id=1, source_target_pairs={{0,32},{1,9},{2,34},{3,11},{4,36},{5,13},{6,38},{7,15},{8,40},{9,1... | collective-permute-start | bytes 1572872 | tf_op jit(solution)/shard_map/ppermute | solution.py:52
  59.7 8.1 %collective-permute-start.23 = (bf16[4,64,512]{2,1,0:T(8,128)(2,1)S(1)}, bf16[4,64,512]{2,1,0:T(8,128)(2,1)S(1)}, u32[]{:S(2)}, u32[]{:S(2)}) collective-permute-start(bf16[4,64,512]{2,1,0:T(8,128)(2,1)S(1)} %get-tuple-element.79), channel_id=1, source_target_pairs={{0,1},{1,0},{2,3},{3,2},{4,5},{5,4},{6,7},{7,6},{8,9},{9,8},{10,11... | collective-permute-start | bytes 786440 | tf_op jit(solution)/shard_map/ppermute | solution.py:72
  64.9 23.1 %collective-permute-start.27 = (bf16[448,1024]{1,0:T(8,128)(2,1)S(1)}, bf16[448,1024]{1,0:T(8,128)(2,1)S(1)}, u32[]{:S(2)}, u32[]{:S(2)}) collective-permute-start(bf16[448,1024]{1,0:T(8,128)(2,1)S(1)} %collective-permute-done.10.refs_5_), channel_id=1, source_target_pairs={{0,8},{1,25},{2,10},{3,27},{4,12},{5,29},{6,14},{7,31},{8,16},{9,1... | collective-permute-start | bytes 2752520 | tf_op jit(solution)/shard_map/ppermute | solution.py:52
  67.8 20.3 %collective-permute-start.24 = (bf16[448,1024]{1,0:T(8,128)(2,1)S(1)}, bf16[448,1024]{1,0:T(8,128)(2,1)S(1)}, u32[]{:S(2)}, u32[]{:S(2)}) collective-permute-start(bf16[448,1024]{1,0:T(8,128)(2,1)S(1)} %bitcast.4), channel_id=1, source_target_pairs={{0,1},{1,0},{2,3},{3,2},{4,5},{5,4},{6,7},{7,6},{8,9},{9,8},{10,11... | collective-permute-start | bytes 2752520 | tf_op jit(solution)/shard_map/ppermute | solution.py:72
  67.8 20.3 %collective-permute-start.25 = (bf16[448,1024]{1,0:T(8,128)(2,1)S(1)}, bf16[448,1024]{1,0:T(8,128)(2,1)S(1)}, u32[]{:S(2)}, u32[]{:S(2)}) collective-permute-start(bf16[448,1024]{1,0:T(8,128)(2,1)S(1)} %collective-permute-done.10.refs_5_), channel_id=1, source_target_pairs={{0,1},{1,0},{2,3},{3,2},{4,5},{5,4},{6,7},{7,6},{8,9},{9,8},{10,11... | collective-permute-start | bytes 2752520 | tf_op jit(solution)/shard_map/ppermute | solution.py:72
  68.3 19.8 %collective-permute-start.26 = (bf16[448,1024]{1,0:T(8,128)(2,1)S(1)}, bf16[448,1024]{1,0:T(8,128)(2,1)S(1)}, u32[]{:S(2)}, u32[]{:S(2)}) collective-permute-start(bf16[448,1024]{1,0:T(8,128)(2,1)S(1)} %collective-permute-done.11.refs_6_), channel_id=1, source_target_pairs={{0,1},{1,0},{2,3},{3,2},{4,5},{5,4},{6,7},{7,6},{8,9},{9,8},{10,11... | collective-permute-start | bytes 2752520 | tf_op jit(solution)/shard_map/ppermute | solution.py:72
  88.1 9.3 %collective-permute-start.31 = (bf16[448,1024]{1,0:T(8,128)(2,1)S(1)}, bf16[448,1024]{1,0:T(8,128)(2,1)S(1)}, u32[]{:S(2)}, u32[]{:S(2)}) collective-permute-start(bf16[448,1024]{1,0:T(8,128)(2,1)S(1)} %collective-permute-done.27.refs_7_), channel_id=1, source_target_pairs={{0,1},{1,0},{2,3},{3,2},{4,5},{5,4},{6,7},{7,6},{8,9},{9,8},{10,11... | collective-permute-start | bytes 2752520 | tf_op jit(solution)/shard_map/ppermute | solution.py:72
  88.6 6.3 %collective-permute-start.29 = (bf16[32,2048]{1,0:T(8,128)(2,1)S(1)}, bf16[32,2048]{1,0:T(8,128)(2,1)S(1)}, u32[]{:S(2)}, u32[]{:S(2)}) collective-permute-start(bf16[32,2048]{1,0:T(8,128)(2,1)S(1)} %attention.1.refs_0_), channel_id=1, source_target_pairs={{0,96},{1,33},{2,98},{3,35},{4,100},{5,37},{6,102},{7,39},{8,104},... | collective-permute-start | bytes 393224 | tf_op jit(solution)/shard_map/ppermute | solution.py:52
  119.3 10.6 %collective-permute-start.39 = (bf16[8,7168]{1,0:T(8,128)(2,1)S(1)}, bf16[8,7168]{1,0:T(8,128)(2,1)S(1)}, u32[]{:S(2)}, u32[]{:S(2)}) collective-permute-start(bf16[8,7168]{1,0:T(8,128)(2,1)S(1)} %join_columns.1.refs_0_), channel_id=1, source_target_pairs={{0,6},{1,3},{2,0},{3,5},{4,2},{5,7},{6,4},{7,1},{8,14},{9,11},{10,... | collective-permute-start | bytes 344072 | tf_op jit(solution)/shard_map/ppermute | solution.py:52
  121.1 9.3 %collective-permute-start.40 = (bf16[8,7168]{1,0:T(8,128)(2,1)S(1)}, bf16[8,7168]{1,0:T(8,128)(2,1)S(1)}, u32[]{:S(2)}, u32[]{:S(2)}) collective-permute-start(bf16[8,7168]{1,0:T(8,128)(2,1)S(1)} %collective-permute-done.38.refs_1_), channel_id=1, source_target_pairs={{0,2},{1,7},{2,4},{3,1},{4,6},{5,3},{6,0},{7,5},{8,10},{9,15},{10,... | collective-permute-start | bytes 344072 | tf_op jit(solution)/shard_map/ppermute | solution.py:52
  124.1 11.7 %collective-permute-start.41 = (bf16[8,7168]{1,0:T(8,128)(2,1)S(1)}, bf16[8,7168]{1,0:T(8,128)(2,1)S(1)}, u32[]{:S(2)}, u32[]{:S(2)}) collective-permute-start(bf16[8,7168]{1,0:T(8,128)(2,1)S(1)} %join_columns.1.refs_0_), channel_id=1, source_target_pairs={{0,1},{1,0},{2,3},{3,2},{4,5},{5,4},{6,7},{7,6},{8,9},{9,8},{10,11... | collective-permute-start | bytes 344072 | tf_op jit(solution)/shard_map/ppermute | solution.py:72
  130.4 6.4 %collective-permute-start.44 = (bf16[8,7168]{1,0:T(8,128)(2,1)S(1)}, bf16[8,7168]{1,0:T(8,128)(2,1)S(1)}, u32[]{:S(2)}, u32[]{:S(2)}) collective-permute-start(bf16[8,7168]{1,0:T(8,128)(2,1)S(1)} %collective-permute-done.40.refs_3_), channel_id=1, source_target_pairs={{0,1},{1,0},{2,3},{3,2},{4,5},{5,4},{6,7},{7,6},{8,9},{9,8},{10,11... | collective-permute-start | bytes 344072 | tf_op jit(solution)/shard_map/ppermute | solution.py:72
  (28 other events, 434.5 us)

commit v6 on v5

--- a/solution.py
+++ b/solution.py
@@ -548,45 +548,57 @@
     )
 
 
-def output_body(*refs, rows):
-    tokens, own_w, got_w, outs = refs[:4], refs[4:8], refs[8:12], refs[12:16]
-    v_buf, w_buf = refs[16:]
+def join_weights_body(*refs):
+    own_w, got_w, out = refs[:4], refs[4:8], refs[8]
     _, x, _, core = here()
     sign = 1 - 2 * core
-    for place, ref in zip(turned(0, -sign), tokens):
-        v_buf[place] = ref[...]
     part, depth = own_w[0].shape
     for k, (weights, way) in enumerate(((own_w, -sign), (got_w, sign))):
         for place, ref in zip(turned(x, way), weights):
             at = pl.multiple_of(place * part, 64)
-            w_buf[pl.ds(at, part), k * depth : (k + 1) * depth] = ref[...]
+            out[pl.ds(at, part), k * depth : (k + 1) * depth] = ref[...]
+
+
+def join_weights(own_w, got_w):
+    part, depth = own_w[0].shape
+    return pl.pallas_call(
+        join_weights_body,
+        in_specs=[VMEM] * 8,
+        out_specs=VMEM,
+        out_shape=jax.ShapeDtypeStruct((SIDE * part, 2 * depth), BF16),
+        compiler_params=room(20),
+        name="join_weights",
+    )(*own_w, *got_w)
+
+
+def output_body(t0, t1, t2, t3, w_ref, *refs, rows):
+    outs, v_buf = refs[:4], refs[4]
+    sign = 1 - 2 * here()[3]
+    for place, ref in zip(turned(0, -sign), (t0, t1, t2, t3)):
+        v_buf[place] = ref[...]
     tokens_all = v_buf[...].reshape(-1, v_buf.shape[2])
     width = 256
-    for n in range(w_buf.shape[0] // width):
+    for n in range(w_ref.shape[0] // width):
         cols = slice(n * width, (n + 1) * width)
-        res = dot(tokens_all, w_buf[cols, :], NT).reshape(SIDE, SIDE, rows, width)
+        res = dot(tokens_all, w_ref[cols, :], NT).reshape(SIDE, SIDE, rows, width)
         for j in range(SIDE):
             for z in range(SIDE):
                 outs[j][z, :, cols] = res[z, j].astype(BF16)
 
 
-def output_blocks(tokens, own_w, got_w):
+def output_blocks(tokens, weights):
     count, depth = tokens[0].shape
-    cols = SIDE * own_w[0].shape[0]
     rows = count // SIDE
-    out = jax.ShapeDtypeStruct((SIDE, rows, cols), BF16)
+    out = jax.ShapeDtypeStruct((SIDE, rows, weights.shape[0]), BF16)
     return pl.pallas_call(
         functools.partial(output_body, rows=rows),
-        in_specs=[VMEM] * 12,
+        in_specs=[VMEM] * 5,
         out_specs=[VMEM] * 4,
         out_shape=[out] * 4,
-        scratch_shapes=[
-            pltpu.VMEM((SIDE, count, depth), BF16),
-            pltpu.VMEM((cols, depth), BF16),
-        ],
-        compiler_params=room(24),
+        scratch_shapes=[pltpu.VMEM((SIDE, count, depth), BF16)],
+        compiler_params=room(16),
         name="output_blocks",
-    )(*tokens, *own_w, *got_w)
+    )(*tokens, weights)
 
 
 def total_body(a, b, c, *outs):
@@ -852,7 +864,7 @@
     own_w = (w_t, w_one, w_two, w_three)
     tokens = ring(values, "z")
     got_w.append(other_core(w_three))
-    own, *sums = output_blocks(tokens, own_w, got_w)
+    own, *sums = output_blocks(tokens, join_weights(own_w, got_w))
     blocks = total_blocks((own,) + ring_sum(sums, "y"))
 
     arrived = [blocks[0]]

time: 139 us -> 140 us (level)
  waiting for transfers between devices: 30.1 us -> 34 us
  starting transfers between devices: 75.6 us -> 73.2 us
    ppermute x30, waiting for transfers between devices: 25.8 us -> 29.4 us  [shift(): return lax.ppermute(v, ('fsdp', 'head'), moves(step))]
    ppermute x12, starting transfers between devices: 28.8 us -> 26.4 us  [other_core(): return lax.ppermute(v, 'head', [(i, i ^ 1) for i in range(2 * SIDE)])]
    ppermute x30, starting transfers between devices: 44.1 us -> 42.6 us  [shift(): return lax.ppermute(v, ('fsdp', 'head'), moves(step))]
    ppermute x3, starting transfers between devices: 2.74 us -> 4.18 us  [body(): arrived.append(lax.ppermute(blocks[d], 'fsdp', perm))]
  transfers between devices with their start and end apart: 45 -> 45, of which waited for: 19 -> 22; matrix products, arithmetic and copies ran while one was open for 0% -> 0% of each run, Pallas kernels for 17% -> 17%
where the time goes in v6:
time: 140 us; the launch traced here: 139 us
  starting transfers between devices  73.2 us (52%)
  waiting for transfers between devices  34 us (24%)
  Pallas kernels  31 us (22%)
    ppermute x30, starting transfers between devices, shift(): return lax.ppermute(v, ('fsdp', 'head'), moves(step))  42.6 us
    ppermute x30, waiting for transfers between devices, shift(): return lax.ppermute(v, ('fsdp', 'head'), moves(step))  29.4 us
    ppermute x12, starting transfers between devices, other_core(): return lax.ppermute(v, 'head', [(i, i ^ 1) for i in range(2 * SIDE)])  26.4 us
    pallas_call x1, Pallas kernels, attention(): pl.pallas_call(functools.partial(attention_body, steps=steps), in_specs=[...  19 us
    ppermute x3, starting transfers between devices, body(): arrived.append(lax.ppermute(blocks[d], 'fsdp', perm))  4.18 us
  transfers between devices with their start and end apart: 45, of which 22 were waited for; matrix products, arithmetic and copies ran while one was open for 0% of the time, Pallas kernels for 17%

profile of v6, /device:TPU:1, one launch (start us, length us, event | category | flops | bytes accessed | tf_op | source)
XLA Modules:
  0.0 139.2 jit_solution(4952586135950316256)
XLA Ops:
  4.5 2.6 %collective-permute-start.10 = (bf16[448,1024]{1,0:T(8,128)(2,1)}, bf16[448,1024]{1,0:T(8,128)(2,1)S(1)}, u32[]{:S(2)}, u32[]{:S(2)}) collective-permute-start(bf16[448,1024]{1,0:T(8,128)(2,1)} %bitcast.2), channel_id=1, source_target_pairs={{0,8},{1,25},{2,10},{3,27},{4,12},{5,29},{6,14},{7,31},{8,16},{9,1... | collective-permute-start | bytes 2752520 | tf_op jit(solution)/shard_map/ppermute | solution.py:52
  7.3 2.8 %collective-permute-start.1 = (bf16[128,512]{1,0:T(8,128)(2,1)S(1)}, bf16[128,512]{1,0:T(8,128)(2,1)S(1)}, u32[]{:S(2)}, u32[]{:S(2)}) collective-permute-start(bf16[128,512]{1,0:T(8,128)(2,1)S(1)} %get-tuple-element.59), channel_id=1, source_target_pairs={{0,2},{1,7},{2,4},{3,1},{4,6},{5,3},{6,0},{7,5},{8,10},{9,15},{10,... | collective-permute-start | bytes 393224 | tf_op jit(solution)/shard_map/ppermute | solution.py:52
  12.1 3.4 %collective-permute-start.2 = (bf16[128,512]{1,0:T(8,128)(2,1)S(1)}, bf16[128,512]{1,0:T(8,128)(2,1)S(1)}, u32[]{:S(2)}, u32[]{:S(2)}) collective-permute-start(bf16[128,512]{1,0:T(8,128)(2,1)S(1)} %add_two.3), channel_id=1, source_target_pairs={{0,2},{1,7},{2,4},{3,1},{4,6},{5,3},{6,0},{7,5},{8,10},{9,15},{10,... | collective-permute-start | bytes 393224 | tf_op jit(solution)/shard_map/ppermute | solution.py:52
  18.5 3.0 %collective-permute-done.6.b2 = bf16[128,512]{1,0:T(8,128)(2,1)S(1)} collective-permute-done((bf16[128,512]{1,0:T(8,128)(2,1)S(1)}, bf16[128,512]{1,0:T(8,128)(2,1)S(1)}, u32[]{:S(2)}, u32[]{:S(2)}) %collective-permute-start.6) | collective-permute-done | bytes 131104 | tf_op jit(solution)/shard_map/ppermute | solution.py:52
  23.4 3.8 %collective-permute-start.18 = (bf16[128,512]{1,0:T(8,128)(2,1)S(1)}, bf16[128,512]{1,0:T(8,128)(2,1)S(1)}, u32[]{:S(2)}, u32[]{:S(2)}) collective-permute-start(bf16[128,512]{1,0:T(8,128)(2,1)S(1)} %get-tuple-element.77.refs_0_), channel_id=1, source_target_pairs={{0,24},{1,97},{2,26},{3,99},{4,28},{5,101},{6,30},{7,103},{8,0},{9... | collective-permute-start | bytes 393224 | tf_op jit(solution)/shard_map/ppermute | solution.py:52
  29.1 3.1 %collective-permute-start.19 = (bf16[128,512]{1,0:T(8,128)(2,1)S(1)}, bf16[128,512]{1,0:T(8,128)(2,1)S(1)}, u32[]{:S(2)}, u32[]{:S(2)}) collective-permute-start(bf16[128,512]{1,0:T(8,128)(2,1)S(1)} %collective-permute-done.18.refs_2_), channel_id=1, source_target_pairs={{0,24},{1,97},{2,26},{3,99},{4,28},{5,101},{6,30},{7,103},{8,0},{9... | collective-permute-start | bytes 393224 | tf_op jit(solution)/shard_map/ppermute | solution.py:52
  34.1 3.3 %collective-permute-start.13 = (bf16[512,1024]{1,0:T(8,128)(2,1)S(1)}, bf16[512,1024]{1,0:T(8,128)(2,1)S(1)}, u32[]{:S(2)}, u32[]{:S(2)}) collective-permute-start(bf16[512,1024]{1,0:T(8,128)(2,1)S(1)} %copy-done.1), channel_id=1, source_target_pairs={{0,1},{1,0},{2,3},{3,2},{4,5},{5,4},{6,7},{7,6},{8,9},{9,8},{10,11... | collective-permute-start | bytes 3145736 | tf_op jit(solution)/shard_map/ppermute | solution.py:72
  37.5 3.4 %collective-permute-start.21 = (bf16[512,512]{1,0:T(8,128)(2,1)S(1)}, bf16[512,512]{1,0:T(8,128)(2,1)S(1)}, u32[]{:S(2)}, u32[]{:S(2)}) collective-permute-start(bf16[512,512]{1,0:T(8,128)(2,1)S(1)} %stack_rows.3.refs_4_), channel_id=1, source_target_pairs={{0,96},{1,25},{2,98},{3,27},{4,100},{5,29},{6,102},{7,31},{8,104},... | collective-permute-start | bytes 1572872 | tf_op jit(solution)/shard_map/ppermute | solution.py:52
  41.1 2.7 %collective-permute-start.15 = (bf16[512,512]{1,0:T(8,128)(2,1)S(1)}, bf16[512,512]{1,0:T(8,128)(2,1)S(1)}, u32[]{:S(2)}, u32[]{:S(2)}) collective-permute-start(bf16[512,512]{1,0:T(8,128)(2,1)S(1)} %stack_rows.2.refs_0_), channel_id=1, source_target_pairs={{0,96},{1,25},{2,98},{3,27},{4,100},{5,29},{6,102},{7,31},{8,104},... | collective-permute-start | bytes 1572872 | tf_op jit(solution)/shard_map/ppermute | solution.py:52
  43.8 3.2 %collective-permute-done.21.refs_6_ = bf16[512,512]{1,0:T(8,128)(2,1)S(1)} collective-permute-done((bf16[512,512]{1,0:T(8,128)(2,1)S(1)}, bf16[512,512]{1,0:T(8,128)(2,1)S(1)}, u32[]{:S(2)}, u32[]{:S(2)}) %collective-permute-start.21) | collective-permute-done | bytes 524320 | tf_op jit(solution)/shard_map/ppermute | solution.py:52
  47.0 3.1 %collective-permute-start.22 = (bf16[512,512]{1,0:T(8,128)(2,1)S(1)}, bf16[512,512]{1,0:T(8,128)(2,1)S(1)}, u32[]{:S(2)}, u32[]{:S(2)}) collective-permute-start(bf16[512,512]{1,0:T(8,128)(2,1)S(1)} %collective-permute-done.21.refs_6_), channel_id=1, source_target_pairs={{0,96},{1,25},{2,98},{3,27},{4,100},{5,29},{6,102},{7,31},{8,104},... | collective-permute-start | bytes 1572872 | tf_op jit(solution)/shard_map/ppermute | solution.py:52
  52.3 3.9 %collective-permute-start.12 = (bf16[4,64,64]{2,1,0:T(8,128)(2,1)S(1)}, bf16[4,64,64]{2,1,0:T(8,128)(2,1)S(1)}, u32[]{:S(2)}, u32[]{:S(2)}) collective-permute-start(bf16[4,64,64]{2,1,0:T(8,128)(2,1)S(1)} %get-tuple-element.74), channel_id=1, source_target_pairs={{0,1},{1,0},{2,3},{3,2},{4,5},{5,4},{6,7},{7,6},{8,9},{9,8},{10,11... | collective-permute-start | bytes 98312 | tf_op jit(solution)/shard_map/ppermute | solution.py:72
  58.3 3.5 %collective-permute-done.16.refs_3_ = bf16[512,512]{1,0:T(8,128)(2,1)S(1)} collective-permute-done((bf16[512,512]{1,0:T(8,128)(2,1)S(1)}, bf16[512,512]{1,0:T(8,128)(2,1)S(1)}, u32[]{:S(2)}, u32[]{:S(2)}) %collective-permute-start.16) | collective-permute-done | bytes 524320 | tf_op jit(solution)/shard_map/ppermute | solution.py:52
  63.1 3.9 %collective-permute-start.23 = (bf16[4,64,512]{2,1,0:T(8,128)(2,1)S(1)}, bf16[4,64,512]{2,1,0:T(8,128)(2,1)S(1)}, u32[]{:S(2)}, u32[]{:S(2)}) collective-permute-start(bf16[4,64,512]{2,1,0:T(8,128)(2,1)S(1)} %get-tuple-element.79), channel_id=1, source_target_pairs={{0,1},{1,0},{2,3},{3,2},{4,5},{5,4},{6,7},{7,6},{8,9},{9,8},{10,11... | collective-permute-start | bytes 786440 | tf_op jit(solution)/shard_map/ppermute | solution.py:72
  67.1 2.3 %collective-permute-start.27 = (bf16[448,1024]{1,0:T(8,128)(2,1)S(1)}, bf16[448,1024]{1,0:T(8,128)(2,1)S(1)}, u32[]{:S(2)}, u32[]{:S(2)}) collective-permute-start(bf16[448,1024]{1,0:T(8,128)(2,1)S(1)} %collective-permute-done.10.refs_1_), channel_id=1, source_target_pairs={{0,8},{1,25},{2,10},{3,27},{4,12},{5,29},{6,14},{7,31},{8,16},{9,1... | collective-permute-start | bytes 2752520 | tf_op jit(solution)/shard_map/ppermute | solution.py:52
  70.0 19.0 %attention.1.t0 = bf16[32,2048]{1,0:T(8,128)(2,1)S(1)} custom-call(s32[8]{0:T(128)S(1)} %get-tuple-element.71.order_ref, s32[8]{0:T(128)S(1)} %get-tuple-element.85.len_ref, bf16[4,64,512]{2,1,0:T(8,128)(2,1)S(1)} %get-tuple-element.86.q_own, bf16[4,64,512]{2,1,0:T(8,128)(2,1)S(1)} %collective-permute-done.23.q_got, ...), custom_call_target="tpu_custom_call" | custom-call | tf_op jit(solution)/shard_map/attention/pallas_call | solution.py:510
  91.0 3.5 %collective-permute-done.28.t1 = bf16[32,2048]{1,0:T(8,128)(2,1)S(1)} collective-permute-done((bf16[32,2048]{1,0:T(8,128)(2,1)S(1)}, bf16[32,2048]{1,0:T(8,128)(2,1)S(1)}, u32[]{:S(2)}, u32[]{:S(2)}) %collective-permute-start.28) | collective-permute-done | bytes 131104 | tf_op jit(solution)/shard_map/ppermute | solution.py:52
  98.3 2.5 %output_blocks.1 = (bf16[4,8,1792]{2,1,0:T(8,128)(2,1)S(1)}, bf16[4,8,1792]{2,1,0:T(8,128)(2,1)S(1)}, bf16[4,8,1792]{2,1,0:T(8,128)(2,1)S(1)}, bf16[4,8,1792]{2,1,0:T(8,128)(2,1)S(1)}) custom-call(bf16[32,2048]{1,0:T(8,128)(2,1)S(1)} %attention.1.t0, bf16[32,2048]{1,0:T(8,128)(2,1)S(1)} %collective-permute-done.28.t1, ...), custom_call_target="tpu_custom_call" | custom-call | tf_op jit(solution)/shard_map/output_blocks/pallas_call | solution.py:593
  104.5 2.3 %collective-permute-start.33 = (bf16[4,8,1792]{2,1,0:T(8,128)(2,1)S(1)}, bf16[4,8,1792]{2,1,0:T(8,128)(2,1)S(1)}, u32[]{:S(2)}, u32[]{:S(2)}) collective-permute-start(bf16[4,8,1792]{2,1,0:T(8,128)(2,1)S(1)} %add_two.5), channel_id=1, source_target_pairs={{0,2},{1,7},{2,4},{3,1},{4,6},{5,3},{6,0},{7,5},{8,10},{9,15},{10,... | collective-permute-start | bytes 344072 | tf_op jit(solution)/shard_map/ppermute | solution.py:52
  108.8 4.0 %collective-permute-start.36 = (bf16[8,1792]{1,0:T(8,128)(2,1)S(1)}, bf16[8,1792]{1,0:T(8,128)(2,1)S(1)}, u32[]{:S(2)}, u32[]{:S(2)}) collective-permute-start(bf16[8,1792]{1,0:T(8,128)(2,1)S(1)} %get-tuple-element.104), channel_id=1, source_target_pairs={{0,64},{8,72},{16,80},{24,88},{32,96},{40,104},{48,112},{56,120},{... | collective-permute-start | bytes 86024 | tf_op jit(solution)/shard_map/ppermute | solution.py:877
  115.5 3.3 %collective-permute-start.38 = (bf16[8,7168]{1,0:T(8,128)(2,1)S(1)}, bf16[8,7168]{1,0:T(8,128)(2,1)S(1)}, u32[]{:S(2)}, u32[]{:S(2)}) collective-permute-start(bf16[8,7168]{1,0:T(8,128)(2,1)S(1)} %join_columns.1.refs_0_), channel_id=1, source_target_pairs={{0,2},{1,7},{2,4},{3,1},{4,6},{5,3},{6,0},{7,5},{8,10},{9,15},{10,... | collective-permute-start | bytes 344072 | tf_op jit(solution)/shard_map/ppermute | solution.py:52
  120.6 3.1 %collective-permute-start.40 = (bf16[8,7168]{1,0:T(8,128)(2,1)S(1)}, bf16[8,7168]{1,0:T(8,128)(2,1)S(1)}, u32[]{:S(2)}, u32[]{:S(2)}) collective-permute-start(bf16[8,7168]{1,0:T(8,128)(2,1)S(1)} %collective-permute-done.38.refs_1_), channel_id=1, source_target_pairs={{0,2},{1,7},{2,4},{3,1},{4,6},{5,3},{6,0},{7,5},{8,10},{9,15},{10,... | collective-permute-start | bytes 344072 | tf_op jit(solution)/shard_map/ppermute | solution.py:52
  123.7 6.7 %collective-permute-start.41 = (bf16[8,7168]{1,0:T(8,128)(2,1)S(1)}, bf16[8,7168]{1,0:T(8,128)(2,1)S(1)}, u32[]{:S(2)}, u32[]{:S(2)}) collective-permute-start(bf16[8,7168]{1,0:T(8,128)(2,1)S(1)} %join_columns.1.refs_0_), channel_id=1, source_target_pairs={{0,1},{1,0},{2,3},{3,2},{4,5},{5,4},{6,7},{7,6},{8,9},{9,8},{10,11... | collective-permute-start | bytes 344072 | tf_op jit(solution)/shard_map/ppermute | solution.py:72
  130.9 5.5 %collective-permute-start.44 = (bf16[8,7168]{1,0:T(8,128)(2,1)S(1)}, bf16[8,7168]{1,0:T(8,128)(2,1)S(1)}, u32[]{:S(2)}, u32[]{:S(2)}) collective-permute-start(bf16[8,7168]{1,0:T(8,128)(2,1)S(1)} %collective-permute-done.40.refs_3_), channel_id=1, source_target_pairs={{0,1},{1,0},{2,3},{3,2},{4,5},{5,4},{6,7},{7,6},{8,9},{9,8},{10,11... | collective-permute-start | bytes 344072 | tf_op jit(solution)/shard_map/ppermute | solution.py:72
  (97 shorter events, 40.4 us)
Async XLA Ops:
  4.5 36.5 %collective-permute-start.10 = (bf16[448,1024]{1,0:T(8,128)(2,1)}, bf16[448,1024]{1,0:T(8,128)(2,1)S(1)}, u32[]{:S(2)}, u32[]{:S(2)}) collective-permute-start(bf16[448,1024]{1,0:T(8,128)(2,1)} %bitcast.2), channel_id=1, source_target_pairs={{0,8},{1,25},{2,10},{3,27},{4,12},{5,29},{6,14},{7,31},{8,16},{9,1... | collective-permute-start | bytes 2752520 | tf_op jit(solution)/shard_map/ppermute | solution.py:52
  7.0 33.9 %collective-permute-start.11 = (bf16[448,1024]{1,0:T(8,128)(2,1)}, bf16[448,1024]{1,0:T(8,128)(2,1)S(1)}, u32[]{:S(2)}, u32[]{:S(2)}) collective-permute-start(bf16[448,1024]{1,0:T(8,128)(2,1)} %bitcast.3), channel_id=1, source_target_pairs={{0,24},{1,9},{2,26},{3,11},{4,28},{5,13},{6,30},{7,15},{8,0},{9,17... | collective-permute-start | bytes 2752520 | tf_op jit(solution)/shard_map/ppermute | solution.py:52
  10.5 6.4 %collective-permute-start.3 = (bf16[128,512]{1,0:T(8,128)(2,1)S(1)}, bf16[128,512]{1,0:T(8,128)(2,1)S(1)}, u32[]{:S(2)}, u32[]{:S(2)}) collective-permute-start(bf16[128,512]{1,0:T(8,128)(2,1)S(1)} %get-tuple-element.60), channel_id=1, source_target_pairs={{0,6},{1,3},{2,0},{3,5},{4,2},{5,7},{6,4},{7,1},{8,14},{9,11},{10,... | collective-permute-start | bytes 393224 | tf_op jit(solution)/shard_map/ppermute | solution.py:52
  12.1 6.2 %collective-permute-start.2 = (bf16[128,512]{1,0:T(8,128)(2,1)S(1)}, bf16[128,512]{1,0:T(8,128)(2,1)S(1)}, u32[]{:S(2)}, u32[]{:S(2)}) collective-permute-start(bf16[128,512]{1,0:T(8,128)(2,1)S(1)} %add_two.3), channel_id=1, source_target_pairs={{0,2},{1,7},{2,4},{3,1},{4,6},{5,3},{6,0},{7,5},{8,10},{9,15},{10,... | collective-permute-start | bytes 393224 | tf_op jit(solution)/shard_map/ppermute | solution.py:52
  27.1 6.7 %collective-permute-start.7 = (bf16[128,512]{1,0:T(8,128)(2,1)S(1)}, bf16[128,512]{1,0:T(8,128)(2,1)S(1)}, u32[]{:S(2)}, u32[]{:S(2)}) collective-permute-start(bf16[128,512]{1,0:T(8,128)(2,1)S(1)} %adam_first.1.after.refs_0_), channel_id=1, source_target_pairs={{0,8},{1,33},{2,10},{3,35},{4,12},{5,37},{6,14},{7,39},{8,16},{9,4... | collective-permute-start | bytes 393224 | tf_op jit(solution)/shard_map/ppermute | solution.py:52
  33.8 7.1 %collective-permute-start.9 = (bf16[128,512]{1,0:T(8,128)(2,1)S(1)}, bf16[128,512]{1,0:T(8,128)(2,1)S(1)}, u32[]{:S(2)}, u32[]{:S(2)}) collective-permute-start(bf16[128,512]{1,0:T(8,128)(2,1)S(1)} %collective-permute-done.7.refs_1_), channel_id=1, source_target_pairs={{0,8},{1,33},{2,10},{3,35},{4,12},{5,37},{6,14},{7,39},{8,16},{9,4... | collective-permute-start | bytes 393224 | tf_op jit(solution)/shard_map/ppermute | solution.py:52
  34.1 18.2 %collective-permute-start.13 = (bf16[512,1024]{1,0:T(8,128)(2,1)S(1)}, bf16[512,1024]{1,0:T(8,128)(2,1)S(1)}, u32[]{:S(2)}, u32[]{:S(2)}) collective-permute-start(bf16[512,1024]{1,0:T(8,128)(2,1)S(1)} %copy-done.1), channel_id=1, source_target_pairs={{0,1},{1,0},{2,3},{3,2},{4,5},{5,4},{6,7},{7,6},{8,9},{9,8},{10,11... | collective-permute-start | bytes 3145736 | tf_op jit(solution)/shard_map/ppermute | solution.py:72
  37.5 9.6 %collective-permute-start.21 = (bf16[512,512]{1,0:T(8,128)(2,1)S(1)}, bf16[512,512]{1,0:T(8,128)(2,1)S(1)}, u32[]{:S(2)}, u32[]{:S(2)}) collective-permute-start(bf16[512,512]{1,0:T(8,128)(2,1)S(1)} %stack_rows.3.refs_4_), channel_id=1, source_target_pairs={{0,96},{1,25},{2,98},{3,27},{4,100},{5,29},{6,102},{7,31},{8,104},... | collective-permute-start | bytes 1572872 | tf_op jit(solution)/shard_map/ppermute | solution.py:52
  41.0 9.6 %collective-permute-start.14 = (bf16[512,512]{1,0:T(8,128)(2,1)S(1)}, bf16[512,512]{1,0:T(8,128)(2,1)S(1)}, u32[]{:S(2)}, u32[]{:S(2)}) collective-permute-start(bf16[512,512]{1,0:T(8,128)(2,1)S(1)} %stack_rows.2.refs_0_), channel_id=1, source_target_pairs={{0,32},{1,9},{2,34},{3,11},{4,36},{5,13},{6,38},{7,15},{8,40},{9,1... | collective-permute-start | bytes 1572872 | tf_op jit(solution)/shard_map/ppermute | solution.py:52
  41.0 16.0 %collective-permute-start.20 = (bf16[512,512]{1,0:T(8,128)(2,1)S(1)}, bf16[512,512]{1,0:T(8,128)(2,1)S(1)}, u32[]{:S(2)}, u32[]{:S(2)}) collective-permute-start(bf16[512,512]{1,0:T(8,128)(2,1)S(1)} %stack_rows.3.refs_4_), channel_id=1, source_target_pairs={{0,32},{1,9},{2,34},{3,11},{4,36},{5,13},{6,38},{7,15},{8,40},{9,1... | collective-permute-start | bytes 1572872 | tf_op jit(solution)/shard_map/ppermute | solution.py:52
  41.1 16.0 %collective-permute-start.15 = (bf16[512,512]{1,0:T(8,128)(2,1)S(1)}, bf16[512,512]{1,0:T(8,128)(2,1)S(1)}, u32[]{:S(2)}, u32[]{:S(2)}) collective-permute-start(bf16[512,512]{1,0:T(8,128)(2,1)S(1)} %stack_rows.2.refs_0_), channel_id=1, source_target_pairs={{0,96},{1,25},{2,98},{3,27},{4,100},{5,29},{6,102},{7,31},{8,104},... | collective-permute-start | bytes 1572872 | tf_op jit(solution)/shard_map/ppermute | solution.py:52
  47.0 11.2 %collective-permute-start.22 = (bf16[512,512]{1,0:T(8,128)(2,1)S(1)}, bf16[512,512]{1,0:T(8,128)(2,1)S(1)}, u32[]{:S(2)}, u32[]{:S(2)}) collective-permute-start(bf16[512,512]{1,0:T(8,128)(2,1)S(1)} %collective-permute-done.21.refs_6_), channel_id=1, source_target_pairs={{0,96},{1,25},{2,98},{3,27},{4,100},{5,29},{6,102},{7,31},{8,104},... | collective-permute-start | bytes 1572872 | tf_op jit(solution)/shard_map/ppermute | solution.py:52
  50.6 11.2 %collective-permute-start.16 = (bf16[512,512]{1,0:T(8,128)(2,1)S(1)}, bf16[512,512]{1,0:T(8,128)(2,1)S(1)}, u32[]{:S(2)}, u32[]{:S(2)}) collective-permute-start(bf16[512,512]{1,0:T(8,128)(2,1)S(1)} %collective-permute-done.14.refs_1_), channel_id=1, source_target_pairs={{0,32},{1,9},{2,34},{3,11},{4,36},{5,13},{6,38},{7,15},{8,40},{9,1... | collective-permute-start | bytes 1572872 | tf_op jit(solution)/shard_map/ppermute | solution.py:52
  63.1 6.3 %collective-permute-start.23 = (bf16[4,64,512]{2,1,0:T(8,128)(2,1)S(1)}, bf16[4,64,512]{2,1,0:T(8,128)(2,1)S(1)}, u32[]{:S(2)}, u32[]{:S(2)}) collective-permute-start(bf16[4,64,512]{2,1,0:T(8,128)(2,1)S(1)} %get-tuple-element.79), channel_id=1, source_target_pairs={{0,1},{1,0},{2,3},{3,2},{4,5},{5,4},{6,7},{7,6},{8,9},{9,8},{10,11... | collective-permute-start | bytes 786440 | tf_op jit(solution)/shard_map/ppermute | solution.py:72
  67.1 21.9 %collective-permute-start.27 = (bf16[448,1024]{1,0:T(8,128)(2,1)S(1)}, bf16[448,1024]{1,0:T(8,128)(2,1)S(1)}, u32[]{:S(2)}, u32[]{:S(2)}) collective-permute-start(bf16[448,1024]{1,0:T(8,128)(2,1)S(1)} %collective-permute-done.10.refs_1_), channel_id=1, source_target_pairs={{0,8},{1,25},{2,10},{3,27},{4,12},{5,29},{6,14},{7,31},{8,16},{9,1... | collective-permute-start | bytes 2752520 | tf_op jit(solution)/shard_map/ppermute | solution.py:52
  69.4 19.6 %collective-permute-start.24 = (bf16[448,1024]{1,0:T(8,128)(2,1)S(1)}, bf16[448,1024]{1,0:T(8,128)(2,1)S(1)}, u32[]{:S(2)}, u32[]{:S(2)}) collective-permute-start(bf16[448,1024]{1,0:T(8,128)(2,1)S(1)} %bitcast.4), channel_id=1, source_target_pairs={{0,1},{1,0},{2,3},{3,2},{4,5},{5,4},{6,7},{7,6},{8,9},{9,8},{10,11... | collective-permute-start | bytes 2752520 | tf_op jit(solution)/shard_map/ppermute | solution.py:72
  69.4 19.6 %collective-permute-start.25 = (bf16[448,1024]{1,0:T(8,128)(2,1)S(1)}, bf16[448,1024]{1,0:T(8,128)(2,1)S(1)}, u32[]{:S(2)}, u32[]{:S(2)}) collective-permute-start(bf16[448,1024]{1,0:T(8,128)(2,1)S(1)} %collective-permute-done.10.refs_1_), channel_id=1, source_target_pairs={{0,1},{1,0},{2,3},{3,2},{4,5},{5,4},{6,7},{7,6},{8,9},{9,8},{10,11... | collective-permute-start | bytes 2752520 | tf_op jit(solution)/shard_map/ppermute | solution.py:72
  69.9 19.1 %collective-permute-start.26 = (bf16[448,1024]{1,0:T(8,128)(2,1)S(1)}, bf16[448,1024]{1,0:T(8,128)(2,1)S(1)}, u32[]{:S(2)}, u32[]{:S(2)}) collective-permute-start(bf16[448,1024]{1,0:T(8,128)(2,1)S(1)} %collective-permute-done.11.refs_2_), channel_id=1, source_target_pairs={{0,1},{1,0},{2,3},{3,2},{4,5},{5,4},{6,7},{7,6},{8,9},{9,8},{10,11... | collective-permute-start | bytes 2752520 | tf_op jit(solution)/shard_map/ppermute | solution.py:72
  89.0 6.2 %collective-permute-start.31 = (bf16[448,1024]{1,0:T(8,128)(2,1)S(1)}, bf16[448,1024]{1,0:T(8,128)(2,1)S(1)}, u32[]{:S(2)}, u32[]{:S(2)}) collective-permute-start(bf16[448,1024]{1,0:T(8,128)(2,1)S(1)} %collective-permute-done.27.refs_3_), channel_id=1, source_target_pairs={{0,1},{1,0},{2,3},{3,2},{4,5},{5,4},{6,7},{7,6},{8,9},{9,8},{10,11... | collective-permute-start | bytes 2752520 | tf_op jit(solution)/shard_map/ppermute | solution.py:72
  90.2 6.5 %collective-permute-start.29 = (bf16[32,2048]{1,0:T(8,128)(2,1)S(1)}, bf16[32,2048]{1,0:T(8,128)(2,1)S(1)}, u32[]{:S(2)}, u32[]{:S(2)}) collective-permute-start(bf16[32,2048]{1,0:T(8,128)(2,1)S(1)} %attention.1.t0), channel_id=1, source_target_pairs={{0,96},{1,33},{2,98},{3,35},{4,100},{5,37},{6,102},{7,39},{8,104},... | collective-permute-start | bytes 393224 | tf_op jit(solution)/shard_map/ppermute | solution.py:52
  118.8 11.6 %collective-permute-start.39 = (bf16[8,7168]{1,0:T(8,128)(2,1)S(1)}, bf16[8,7168]{1,0:T(8,128)(2,1)S(1)}, u32[]{:S(2)}, u32[]{:S(2)}) collective-permute-start(bf16[8,7168]{1,0:T(8,128)(2,1)S(1)} %join_columns.1.refs_0_), channel_id=1, source_target_pairs={{0,6},{1,3},{2,0},{3,5},{4,2},{5,7},{6,4},{7,1},{8,14},{9,11},{10,... | collective-permute-start | bytes 344072 | tf_op jit(solution)/shard_map/ppermute | solution.py:52
  120.6 10.3 %collective-permute-start.40 = (bf16[8,7168]{1,0:T(8,128)(2,1)S(1)}, bf16[8,7168]{1,0:T(8,128)(2,1)S(1)}, u32[]{:S(2)}, u32[]{:S(2)}) collective-permute-start(bf16[8,7168]{1,0:T(8,128)(2,1)S(1)} %collective-permute-done.38.refs_1_), channel_id=1, source_target_pairs={{0,2},{1,7},{2,4},{3,1},{4,6},{5,3},{6,0},{7,5},{8,10},{9,15},{10,... | collective-permute-start | bytes 344072 | tf_op jit(solution)/shard_map/ppermute | solution.py:52
  123.7 12.7 %collective-permute-start.41 = (bf16[8,7168]{1,0:T(8,128)(2,1)S(1)}, bf16[8,7168]{1,0:T(8,128)(2,1)S(1)}, u32[]{:S(2)}, u32[]{:S(2)}) collective-permute-start(bf16[8,7168]{1,0:T(8,128)(2,1)S(1)} %join_columns.1.refs_0_), channel_id=1, source_target_pairs={{0,1},{1,0},{2,3},{3,2},{4,5},{5,4},{6,7},{7,6},{8,9},{9,8},{10,11... | collective-permute-start | bytes 344072 | tf_op jit(solution)/shard_map/ppermute | solution.py:72
  130.9 6.4 %collective-permute-start.44 = (bf16[8,7168]{1,0:T(8,128)(2,1)S(1)}, bf16[8,7168]{1,0:T(8,128)(2,1)S(1)}, u32[]{:S(2)}, u32[]{:S(2)}) collective-permute-start(bf16[8,7168]{1,0:T(8,128)(2,1)S(1)} %collective-permute-done.40.refs_3_), channel_id=1, source_target_pairs={{0,1},{1,0},{2,3},{3,2},{4,5},{5,4},{6,7},{7,6},{8,9},{9,8},{10,11... | collective-permute-start | bytes 344072 | tf_op jit(solution)/shard_map/ppermute | solution.py:72
  (28 other events, 447.6 us)

commit v7 on v6

--- a/solution.py
+++ b/solution.py
@@ -640,7 +640,7 @@
 
 
 def settle_body(order_ref, *refs):
-    blocks, out, buf = refs[:8], refs[8], refs[9]
+    blocks, out = refs[:8], refs[8]
     steps, seqs, cols = out.shape
     half = seqs // 2
     each = steps // SIDE
@@ -648,8 +648,6 @@
     size = each * half
     _, _, y, core = here()
     sign = 1 - 2 * core
-    for k, ref in enumerate(blocks):
-        buf[k * size : (k + 1) * size, :] = ref[...].astype(F32)
     row = lax.broadcasted_iota(jnp.int32, (count, count), 0)
     col = lax.broadcasted_iota(jnp.int32, (count, count), 1)
     step = jnp.zeros((count, count), jnp.int32)
@@ -665,7 +663,8 @@
     width = 1024
     for n in range(cols // width):
         part = slice(n * width, (n + 1) * width)
-        res = dot(pick, buf[:, part].astype(BF16), NN)
+        rows = jnp.concatenate([ref[:, part].astype(F32) for ref in blocks], axis=0)
+        res = dot(pick, rows.astype(BF16), NN)
         out[:, :, part] = res.reshape(steps, seqs, width).astype(BF16)
 
 
@@ -676,7 +675,6 @@
         in_specs=[SMEM] + [VMEM] * 8,
         out_specs=VMEM,
         out_shape=jax.ShapeDtypeStruct((rows, 8, cols), BF16),
-        scratch_shapes=[pltpu.VMEM((8 * rows, cols), F32)],
         compiler_params=room(12),
         name="settle",
     )(order, *blocks)

time: 140 us -> 137 us (0.979)
  transfers between devices with their start and end apart: 45 -> 45, of which waited for: 22 -> 22; matrix products, arithmetic and copies ran while one was open for 0% -> 0% of each run, Pallas kernels for 17% -> 16%
where the time goes in v7:
time: 137 us
  starting transfers between devices  72.1 us (53%)
  waiting for transfers between devices  34.7 us (25%)
  Pallas kernels  29.6 us (22%)
    ppermute x30, starting transfers between devices, shift(): return lax.ppermute(v, ('fsdp', 'head'), moves(step))  42.1 us
    ppermute x30, waiting for transfers between devices, shift(): return lax.ppermute(v, ('fsdp', 'head'), moves(step))  30.1 us
    ppermute x12, starting transfers between devices, other_core(): return lax.ppermute(v, 'head', [(i, i ^ 1) for i in range(2 * SIDE)])  26.3 us
    pallas_call x1, Pallas kernels, attention(): pl.pallas_call(functools.partial(attention_body, steps=steps), in_specs=[...  17.6 us
    ppermute x3, starting transfers between devices, body(): arrived.append(lax.ppermute(blocks[d], 'fsdp', perm))  3.7 us
  transfers between devices with their start and end apart: 45, of which 22 were waited for; matrix products, arithmetic and copies ran while one was open for 0% of the time, Pallas kernels for 16%

profile of v7, /device:TPU:1, one launch (start us, length us, event | category | flops | bytes accessed | tf_op | source)
XLA Modules:
  0.0 137.4 jit_solution(4952586135950316256)
XLA Ops:
  4.5 2.6 %collective-permute-start.10 = (bf16[448,1024]{1,0:T(8,128)(2,1)}, bf16[448,1024]{1,0:T(8,128)(2,1)S(1)}, u32[]{:S(2)}, u32[]{:S(2)}) collective-permute-start(bf16[448,1024]{1,0:T(8,128)(2,1)} %bitcast.2), channel_id=1, source_target_pairs={{0,8},{1,25},{2,10},{3,27},{4,12},{5,29},{6,14},{7,31},{8,16},{9,1... | collective-permute-start | bytes 2752520 | tf_op jit(solution)/shard_map/ppermute | solution.py:52
  7.3 2.8 %collective-permute-start.1 = (bf16[128,512]{1,0:T(8,128)(2,1)S(1)}, bf16[128,512]{1,0:T(8,128)(2,1)S(1)}, u32[]{:S(2)}, u32[]{:S(2)}) collective-permute-start(bf16[128,512]{1,0:T(8,128)(2,1)S(1)} %get-tuple-element.59), channel_id=1, source_target_pairs={{0,2},{1,7},{2,4},{3,1},{4,6},{5,3},{6,0},{7,5},{8,10},{9,15},{10,... | collective-permute-start | bytes 393224 | tf_op jit(solution)/shard_map/ppermute | solution.py:52
  12.1 3.4 %collective-permute-start.2 = (bf16[128,512]{1,0:T(8,128)(2,1)S(1)}, bf16[128,512]{1,0:T(8,128)(2,1)S(1)}, u32[]{:S(2)}, u32[]{:S(2)}) collective-permute-start(bf16[128,512]{1,0:T(8,128)(2,1)S(1)} %add_two.3), channel_id=1, source_target_pairs={{0,2},{1,7},{2,4},{3,1},{4,6},{5,3},{6,0},{7,5},{8,10},{9,15},{10,... | collective-permute-start | bytes 393224 | tf_op jit(solution)/shard_map/ppermute | solution.py:52
  18.5 3.0 %collective-permute-done.6.b2 = bf16[128,512]{1,0:T(8,128)(2,1)S(1)} collective-permute-done((bf16[128,512]{1,0:T(8,128)(2,1)S(1)}, bf16[128,512]{1,0:T(8,128)(2,1)S(1)}, u32[]{:S(2)}, u32[]{:S(2)}) %collective-permute-start.6) | collective-permute-done | bytes 131104 | tf_op jit(solution)/shard_map/ppermute | solution.py:52
  23.4 3.8 %collective-permute-start.18 = (bf16[128,512]{1,0:T(8,128)(2,1)S(1)}, bf16[128,512]{1,0:T(8,128)(2,1)S(1)}, u32[]{:S(2)}, u32[]{:S(2)}) collective-permute-start(bf16[128,512]{1,0:T(8,128)(2,1)S(1)} %get-tuple-element.77.refs_0_), channel_id=1, source_target_pairs={{0,24},{1,97},{2,26},{3,99},{4,28},{5,101},{6,30},{7,103},{8,0},{9... | collective-permute-start | bytes 393224 | tf_op jit(solution)/shard_map/ppermute | solution.py:52
  29.1 3.1 %collective-permute-start.19 = (bf16[128,512]{1,0:T(8,128)(2,1)S(1)}, bf16[128,512]{1,0:T(8,128)(2,1)S(1)}, u32[]{:S(2)}, u32[]{:S(2)}) collective-permute-start(bf16[128,512]{1,0:T(8,128)(2,1)S(1)} %collective-permute-done.18.refs_2_), channel_id=1, source_target_pairs={{0,24},{1,97},{2,26},{3,99},{4,28},{5,101},{6,30},{7,103},{8,0},{9... | collective-permute-start | bytes 393224 | tf_op jit(solution)/shard_map/ppermute | solution.py:52
  34.1 3.3 %collective-permute-start.13 = (bf16[512,1024]{1,0:T(8,128)(2,1)S(1)}, bf16[512,1024]{1,0:T(8,128)(2,1)S(1)}, u32[]{:S(2)}, u32[]{:S(2)}) collective-permute-start(bf16[512,1024]{1,0:T(8,128)(2,1)S(1)} %copy-done.1), channel_id=1, source_target_pairs={{0,1},{1,0},{2,3},{3,2},{4,5},{5,4},{6,7},{7,6},{8,9},{9,8},{10,11... | collective-permute-start | bytes 3145736 | tf_op jit(solution)/shard_map/ppermute | solution.py:72
  37.5 3.4 %collective-permute-start.21 = (bf16[512,512]{1,0:T(8,128)(2,1)S(1)}, bf16[512,512]{1,0:T(8,128)(2,1)S(1)}, u32[]{:S(2)}, u32[]{:S(2)}) collective-permute-start(bf16[512,512]{1,0:T(8,128)(2,1)S(1)} %stack_rows.3.refs_4_), channel_id=1, source_target_pairs={{0,96},{1,25},{2,98},{3,27},{4,100},{5,29},{6,102},{7,31},{8,104},... | collective-permute-start | bytes 1572872 | tf_op jit(solution)/shard_map/ppermute | solution.py:52
  41.1 2.7 %collective-permute-start.15 = (bf16[512,512]{1,0:T(8,128)(2,1)S(1)}, bf16[512,512]{1,0:T(8,128)(2,1)S(1)}, u32[]{:S(2)}, u32[]{:S(2)}) collective-permute-start(bf16[512,512]{1,0:T(8,128)(2,1)S(1)} %stack_rows.2.refs_0_), channel_id=1, source_target_pairs={{0,96},{1,25},{2,98},{3,27},{4,100},{5,29},{6,102},{7,31},{8,104},... | collective-permute-start | bytes 1572872 | tf_op jit(solution)/shard_map/ppermute | solution.py:52
  43.8 3.2 %collective-permute-done.21.refs_6_ = bf16[512,512]{1,0:T(8,128)(2,1)S(1)} collective-permute-done((bf16[512,512]{1,0:T(8,128)(2,1)S(1)}, bf16[512,512]{1,0:T(8,128)(2,1)S(1)}, u32[]{:S(2)}, u32[]{:S(2)}) %collective-permute-start.21) | collective-permute-done | bytes 524320 | tf_op jit(solution)/shard_map/ppermute | solution.py:52
  47.0 3.1 %collective-permute-start.22 = (bf16[512,512]{1,0:T(8,128)(2,1)S(1)}, bf16[512,512]{1,0:T(8,128)(2,1)S(1)}, u32[]{:S(2)}, u32[]{:S(2)}) collective-permute-start(bf16[512,512]{1,0:T(8,128)(2,1)S(1)} %collective-permute-done.21.refs_6_), channel_id=1, source_target_pairs={{0,96},{1,25},{2,98},{3,27},{4,100},{5,29},{6,102},{7,31},{8,104},... | collective-permute-start | bytes 1572872 | tf_op jit(solution)/shard_map/ppermute | solution.py:52
  52.3 3.9 %collective-permute-start.12 = (bf16[4,64,64]{2,1,0:T(8,128)(2,1)S(1)}, bf16[4,64,64]{2,1,0:T(8,128)(2,1)S(1)}, u32[]{:S(2)}, u32[]{:S(2)}) collective-permute-start(bf16[4,64,64]{2,1,0:T(8,128)(2,1)S(1)} %get-tuple-element.74), channel_id=1, source_target_pairs={{0,1},{1,0},{2,3},{3,2},{4,5},{5,4},{6,7},{7,6},{8,9},{9,8},{10,11... | collective-permute-start | bytes 98312 | tf_op jit(solution)/shard_map/ppermute | solution.py:72
  58.3 3.5 %collective-permute-done.16.refs_3_ = bf16[512,512]{1,0:T(8,128)(2,1)S(1)} collective-permute-done((bf16[512,512]{1,0:T(8,128)(2,1)S(1)}, bf16[512,512]{1,0:T(8,128)(2,1)S(1)}, u32[]{:S(2)}, u32[]{:S(2)}) %collective-permute-start.16) | collective-permute-done | bytes 524320 | tf_op jit(solution)/shard_map/ppermute | solution.py:52
  63.1 3.9 %collective-permute-start.23 = (bf16[4,64,512]{2,1,0:T(8,128)(2,1)S(1)}, bf16[4,64,512]{2,1,0:T(8,128)(2,1)S(1)}, u32[]{:S(2)}, u32[]{:S(2)}) collective-permute-start(bf16[4,64,512]{2,1,0:T(8,128)(2,1)S(1)} %get-tuple-element.79), channel_id=1, source_target_pairs={{0,1},{1,0},{2,3},{3,2},{4,5},{5,4},{6,7},{7,6},{8,9},{9,8},{10,11... | collective-permute-start | bytes 786440 | tf_op jit(solution)/shard_map/ppermute | solution.py:72
  67.1 2.3 %collective-permute-start.27 = (bf16[448,1024]{1,0:T(8,128)(2,1)S(1)}, bf16[448,1024]{1,0:T(8,128)(2,1)S(1)}, u32[]{:S(2)}, u32[]{:S(2)}) collective-permute-start(bf16[448,1024]{1,0:T(8,128)(2,1)S(1)} %collective-permute-done.10.refs_1_), channel_id=1, source_target_pairs={{0,8},{1,25},{2,10},{3,27},{4,12},{5,29},{6,14},{7,31},{8,16},{9,1... | collective-permute-start | bytes 2752520 | tf_op jit(solution)/shard_map/ppermute | solution.py:52
  70.0 17.6 %attention.1.t0 = bf16[32,2048]{1,0:T(8,128)(2,1)S(1)} custom-call(s32[8]{0:T(128)S(1)} %get-tuple-element.71.order_ref, s32[8]{0:T(128)S(1)} %get-tuple-element.85.len_ref, bf16[4,64,512]{2,1,0:T(8,128)(2,1)S(1)} %get-tuple-element.86.q_own, bf16[4,64,512]{2,1,0:T(8,128)(2,1)S(1)} %collective-permute-done.23.q_got, ...), custom_call_target="tpu_custom_call" | custom-call | tf_op jit(solution)/shard_map/attention/pallas_call | solution.py:510
  89.6 3.5 %collective-permute-done.28.t1 = bf16[32,2048]{1,0:T(8,128)(2,1)S(1)} collective-permute-done((bf16[32,2048]{1,0:T(8,128)(2,1)S(1)}, bf16[32,2048]{1,0:T(8,128)(2,1)S(1)}, u32[]{:S(2)}, u32[]{:S(2)}) %collective-permute-start.28) | collective-permute-done | bytes 131104 | tf_op jit(solution)/shard_map/ppermute | solution.py:52
  94.4 2.5 %collective-permute-done.30.t3 = bf16[32,2048]{1,0:T(8,128)(2,1)S(1)} collective-permute-done((bf16[32,2048]{1,0:T(8,128)(2,1)S(1)}, bf16[32,2048]{1,0:T(8,128)(2,1)S(1)}, u32[]{:S(2)}, u32[]{:S(2)}) %collective-permute-start.30) | collective-permute-done | bytes 131104 | tf_op jit(solution)/shard_map/ppermute | solution.py:52
  96.9 2.5 %output_blocks.1 = (bf16[4,8,1792]{2,1,0:T(8,128)(2,1)S(1)}, bf16[4,8,1792]{2,1,0:T(8,128)(2,1)S(1)}, bf16[4,8,1792]{2,1,0:T(8,128)(2,1)S(1)}, bf16[4,8,1792]{2,1,0:T(8,128)(2,1)S(1)}) custom-call(bf16[32,2048]{1,0:T(8,128)(2,1)S(1)} %attention.1.t0, bf16[32,2048]{1,0:T(8,128)(2,1)S(1)} %collective-permute-done.28.t1, ...), custom_call_target="tpu_custom_call" | custom-call | tf_op jit(solution)/shard_map/output_blocks/pallas_call | solution.py:593
  107.8 3.1 %collective-permute-start.36 = (bf16[8,1792]{1,0:T(8,128)(2,1)S(1)}, bf16[8,1792]{1,0:T(8,128)(2,1)S(1)}, u32[]{:S(2)}, u32[]{:S(2)}) collective-permute-start(bf16[8,1792]{1,0:T(8,128)(2,1)S(1)} %get-tuple-element.104), channel_id=1, source_target_pairs={{0,64},{8,72},{16,80},{24,88},{32,96},{40,104},{48,112},{56,120},{... | collective-permute-start | bytes 86024 | tf_op jit(solution)/shard_map/ppermute | solution.py:875
  113.7 3.5 %collective-permute-start.38 = (bf16[8,7168]{1,0:T(8,128)(2,1)S(1)}, bf16[8,7168]{1,0:T(8,128)(2,1)S(1)}, u32[]{:S(2)}, u32[]{:S(2)}) collective-permute-start(bf16[8,7168]{1,0:T(8,128)(2,1)S(1)} %join_columns.1.refs_0_), channel_id=1, source_target_pairs={{0,2},{1,7},{2,4},{3,1},{4,6},{5,3},{6,0},{7,5},{8,10},{9,15},{10,... | collective-permute-start | bytes 344072 | tf_op jit(solution)/shard_map/ppermute | solution.py:52
  119.0 3.1 %collective-permute-start.40 = (bf16[8,7168]{1,0:T(8,128)(2,1)S(1)}, bf16[8,7168]{1,0:T(8,128)(2,1)S(1)}, u32[]{:S(2)}, u32[]{:S(2)}) collective-permute-start(bf16[8,7168]{1,0:T(8,128)(2,1)S(1)} %collective-permute-done.38.refs_1_), channel_id=1, source_target_pairs={{0,2},{1,7},{2,4},{3,1},{4,6},{5,3},{6,0},{7,5},{8,10},{9,15},{10,... | collective-permute-start | bytes 344072 | tf_op jit(solution)/shard_map/ppermute | solution.py:52
  122.0 6.6 %collective-permute-start.41 = (bf16[8,7168]{1,0:T(8,128)(2,1)S(1)}, bf16[8,7168]{1,0:T(8,128)(2,1)S(1)}, u32[]{:S(2)}, u32[]{:S(2)}) collective-permute-start(bf16[8,7168]{1,0:T(8,128)(2,1)S(1)} %join_columns.1.refs_0_), channel_id=1, source_target_pairs={{0,1},{1,0},{2,3},{3,2},{4,5},{5,4},{6,7},{7,6},{8,9},{9,8},{10,11... | collective-permute-start | bytes 344072 | tf_op jit(solution)/shard_map/ppermute | solution.py:72
  129.1 5.5 %collective-permute-start.44 = (bf16[8,7168]{1,0:T(8,128)(2,1)S(1)}, bf16[8,7168]{1,0:T(8,128)(2,1)S(1)}, u32[]{:S(2)}, u32[]{:S(2)}) collective-permute-start(bf16[8,7168]{1,0:T(8,128)(2,1)S(1)} %collective-permute-done.40.refs_3_), channel_id=1, source_target_pairs={{0,1},{1,0},{2,3},{3,2},{4,5},{5,4},{6,7},{7,6},{8,9},{9,8},{10,11... | collective-permute-start | bytes 344072 | tf_op jit(solution)/shard_map/ppermute | solution.py:72
  (97 shorter events, 40.6 us)
Async XLA Ops:
  4.5 36.5 %collective-permute-start.10 = (bf16[448,1024]{1,0:T(8,128)(2,1)}, bf16[448,1024]{1,0:T(8,128)(2,1)S(1)}, u32[]{:S(2)}, u32[]{:S(2)}) collective-permute-start(bf16[448,1024]{1,0:T(8,128)(2,1)} %bitcast.2), channel_id=1, source_target_pairs={{0,8},{1,25},{2,10},{3,27},{4,12},{5,29},{6,14},{7,31},{8,16},{9,1... | collective-permute-start | bytes 2752520 | tf_op jit(solution)/shard_map/ppermute | solution.py:52
  7.0 33.9 %collective-permute-start.11 = (bf16[448,1024]{1,0:T(8,128)(2,1)}, bf16[448,1024]{1,0:T(8,128)(2,1)S(1)}, u32[]{:S(2)}, u32[]{:S(2)}) collective-permute-start(bf16[448,1024]{1,0:T(8,128)(2,1)} %bitcast.3), channel_id=1, source_target_pairs={{0,24},{1,9},{2,26},{3,11},{4,28},{5,13},{6,30},{7,15},{8,0},{9,17... | collective-permute-start | bytes 2752520 | tf_op jit(solution)/shard_map/ppermute | solution.py:52
  10.5 6.4 %collective-permute-start.3 = (bf16[128,512]{1,0:T(8,128)(2,1)S(1)}, bf16[128,512]{1,0:T(8,128)(2,1)S(1)}, u32[]{:S(2)}, u32[]{:S(2)}) collective-permute-start(bf16[128,512]{1,0:T(8,128)(2,1)S(1)} %get-tuple-element.60), channel_id=1, source_target_pairs={{0,6},{1,3},{2,0},{3,5},{4,2},{5,7},{6,4},{7,1},{8,14},{9,11},{10,... | collective-permute-start | bytes 393224 | tf_op jit(solution)/shard_map/ppermute | solution.py:52
  12.1 6.2 %collective-permute-start.2 = (bf16[128,512]{1,0:T(8,128)(2,1)S(1)}, bf16[128,512]{1,0:T(8,128)(2,1)S(1)}, u32[]{:S(2)}, u32[]{:S(2)}) collective-permute-start(bf16[128,512]{1,0:T(8,128)(2,1)S(1)} %add_two.3), channel_id=1, source_target_pairs={{0,2},{1,7},{2,4},{3,1},{4,6},{5,3},{6,0},{7,5},{8,10},{9,15},{10,... | collective-permute-start | bytes 393224 | tf_op jit(solution)/shard_map/ppermute | solution.py:52
  15.5 6.1 %collective-permute-start.6 = (bf16[128,512]{1,0:T(8,128)(2,1)S(1)}, bf16[128,512]{1,0:T(8,128)(2,1)S(1)}, u32[]{:S(2)}, u32[]{:S(2)}) collective-permute-start(bf16[128,512]{1,0:T(8,128)(2,1)S(1)} %get-tuple-element.63), channel_id=1, source_target_pairs={{0,6},{1,3},{2,0},{3,5},{4,2},{5,7},{6,4},{7,1},{8,14},{9,11},{10,... | collective-permute-start | bytes 393224 | tf_op jit(solution)/shard_map/ppermute | solution.py:52
  27.1 6.7 %collective-permute-start.7 = (bf16[128,512]{1,0:T(8,128)(2,1)S(1)}, bf16[128,512]{1,0:T(8,128)(2,1)S(1)}, u32[]{:S(2)}, u32[]{:S(2)}) collective-permute-start(bf16[128,512]{1,0:T(8,128)(2,1)S(1)} %adam_first.1.after.refs_0_), channel_id=1, source_target_pairs={{0,8},{1,33},{2,10},{3,35},{4,12},{5,37},{6,14},{7,39},{8,16},{9,4... | collective-permute-start | bytes 393224 | tf_op jit(solution)/shard_map/ppermute | solution.py:52
  33.8 7.1 %collective-permute-start.9 = (bf16[128,512]{1,0:T(8,128)(2,1)S(1)}, bf16[128,512]{1,0:T(8,128)(2,1)S(1)}, u32[]{:S(2)}, u32[]{:S(2)}) collective-permute-start(bf16[128,512]{1,0:T(8,128)(2,1)S(1)} %collective-permute-done.7.refs_1_), channel_id=1, source_target_pairs={{0,8},{1,33},{2,10},{3,35},{4,12},{5,37},{6,14},{7,39},{8,16},{9,4... | collective-permute-start | bytes 393224 | tf_op jit(solution)/shard_map/ppermute | solution.py:52
  34.1 18.2 %collective-permute-start.13 = (bf16[512,1024]{1,0:T(8,128)(2,1)S(1)}, bf16[512,1024]{1,0:T(8,128)(2,1)S(1)}, u32[]{:S(2)}, u32[]{:S(2)}) collective-permute-start(bf16[512,1024]{1,0:T(8,128)(2,1)S(1)} %copy-done.1), channel_id=1, source_target_pairs={{0,1},{1,0},{2,3},{3,2},{4,5},{5,4},{6,7},{7,6},{8,9},{9,8},{10,11... | collective-permute-start | bytes 3145736 | tf_op jit(solution)/shard_map/ppermute | solution.py:72
  37.5 9.6 %collective-permute-start.21 = (bf16[512,512]{1,0:T(8,128)(2,1)S(1)}, bf16[512,512]{1,0:T(8,128)(2,1)S(1)}, u32[]{:S(2)}, u32[]{:S(2)}) collective-permute-start(bf16[512,512]{1,0:T(8,128)(2,1)S(1)} %stack_rows.3.refs_4_), channel_id=1, source_target_pairs={{0,96},{1,25},{2,98},{3,27},{4,100},{5,29},{6,102},{7,31},{8,104},... | collective-permute-start | bytes 1572872 | tf_op jit(solution)/shard_map/ppermute | solution.py:52
  41.0 9.6 %collective-permute-start.14 = (bf16[512,512]{1,0:T(8,128)(2,1)S(1)}, bf16[512,512]{1,0:T(8,128)(2,1)S(1)}, u32[]{:S(2)}, u32[]{:S(2)}) collective-permute-start(bf16[512,512]{1,0:T(8,128)(2,1)S(1)} %stack_rows.2.refs_0_), channel_id=1, source_target_pairs={{0,32},{1,9},{2,34},{3,11},{4,36},{5,13},{6,38},{7,15},{8,40},{9,1... | collective-permute-start | bytes 1572872 | tf_op jit(solution)/shard_map/ppermute | solution.py:52
  41.0 16.0 %collective-permute-start.20 = (bf16[512,512]{1,0:T(8,128)(2,1)S(1)}, bf16[512,512]{1,0:T(8,128)(2,1)S(1)}, u32[]{:S(2)}, u32[]{:S(2)}) collective-permute-start(bf16[512,512]{1,0:T(8,128)(2,1)S(1)} %stack_rows.3.refs_4_), channel_id=1, source_target_pairs={{0,32},{1,9},{2,34},{3,11},{4,36},{5,13},{6,38},{7,15},{8,40},{9,1... | collective-permute-start | bytes 1572872 | tf_op jit(solution)/shard_map/ppermute | solution.py:52
  41.1 16.0 %collective-permute-start.15 = (bf16[512,512]{1,0:T(8,128)(2,1)S(1)}, bf16[512,512]{1,0:T(8,128)(2,1)S(1)}, u32[]{:S(2)}, u32[]{:S(2)}) collective-permute-start(bf16[512,512]{1,0:T(8,128)(2,1)S(1)} %stack_rows.2.refs_0_), channel_id=1, source_target_pairs={{0,96},{1,25},{2,98},{3,27},{4,100},{5,29},{6,102},{7,31},{8,104},... | collective-permute-start | bytes 1572872 | tf_op jit(solution)/shard_map/ppermute | solution.py:52
  47.0 11.2 %collective-permute-start.22 = (bf16[512,512]{1,0:T(8,128)(2,1)S(1)}, bf16[512,512]{1,0:T(8,128)(2,1)S(1)}, u32[]{:S(2)}, u32[]{:S(2)}) collective-permute-start(bf16[512,512]{1,0:T(8,128)(2,1)S(1)} %collective-permute-done.21.refs_6_), channel_id=1, source_target_pairs={{0,96},{1,25},{2,98},{3,27},{4,100},{5,29},{6,102},{7,31},{8,104},... | collective-permute-start | bytes 1572872 | tf_op jit(solution)/shard_map/ppermute | solution.py:52
  50.6 11.2 %collective-permute-start.16 = (bf16[512,512]{1,0:T(8,128)(2,1)S(1)}, bf16[512,512]{1,0:T(8,128)(2,1)S(1)}, u32[]{:S(2)}, u32[]{:S(2)}) collective-permute-start(bf16[512,512]{1,0:T(8,128)(2,1)S(1)} %collective-permute-done.14.refs_1_), channel_id=1, source_target_pairs={{0,32},{1,9},{2,34},{3,11},{4,36},{5,13},{6,38},{7,15},{8,40},{9,1... | collective-permute-start | bytes 1572872 | tf_op jit(solution)/shard_map/ppermute | solution.py:52
  63.1 6.3 %collective-permute-start.23 = (bf16[4,64,512]{2,1,0:T(8,128)(2,1)S(1)}, bf16[4,64,512]{2,1,0:T(8,128)(2,1)S(1)}, u32[]{:S(2)}, u32[]{:S(2)}) collective-permute-start(bf16[4,64,512]{2,1,0:T(8,128)(2,1)S(1)} %get-tuple-element.79), channel_id=1, source_target_pairs={{0,1},{1,0},{2,3},{3,2},{4,5},{5,4},{6,7},{7,6},{8,9},{9,8},{10,11... | collective-permute-start | bytes 786440 | tf_op jit(solution)/shard_map/ppermute | solution.py:72
  67.1 20.5 %collective-permute-start.27 = (bf16[448,1024]{1,0:T(8,128)(2,1)S(1)}, bf16[448,1024]{1,0:T(8,128)(2,1)S(1)}, u32[]{:S(2)}, u32[]{:S(2)}) collective-permute-start(bf16[448,1024]{1,0:T(8,128)(2,1)S(1)} %collective-permute-done.10.refs_1_), channel_id=1, source_target_pairs={{0,8},{1,25},{2,10},{3,27},{4,12},{5,29},{6,14},{7,31},{8,16},{9,1... | collective-permute-start | bytes 2752520 | tf_op jit(solution)/shard_map/ppermute | solution.py:52
  69.4 18.2 %collective-permute-start.24 = (bf16[448,1024]{1,0:T(8,128)(2,1)S(1)}, bf16[448,1024]{1,0:T(8,128)(2,1)S(1)}, u32[]{:S(2)}, u32[]{:S(2)}) collective-permute-start(bf16[448,1024]{1,0:T(8,128)(2,1)S(1)} %bitcast.4), channel_id=1, source_target_pairs={{0,1},{1,0},{2,3},{3,2},{4,5},{5,4},{6,7},{7,6},{8,9},{9,8},{10,11... | collective-permute-start | bytes 2752520 | tf_op jit(solution)/shard_map/ppermute | solution.py:72
  69.4 18.2 %collective-permute-start.25 = (bf16[448,1024]{1,0:T(8,128)(2,1)S(1)}, bf16[448,1024]{1,0:T(8,128)(2,1)S(1)}, u32[]{:S(2)}, u32[]{:S(2)}) collective-permute-start(bf16[448,1024]{1,0:T(8,128)(2,1)S(1)} %collective-permute-done.10.refs_1_), channel_id=1, source_target_pairs={{0,1},{1,0},{2,3},{3,2},{4,5},{5,4},{6,7},{7,6},{8,9},{9,8},{10,11... | collective-permute-start | bytes 2752520 | tf_op jit(solution)/shard_map/ppermute | solution.py:72
  69.9 17.7 %collective-permute-start.26 = (bf16[448,1024]{1,0:T(8,128)(2,1)S(1)}, bf16[448,1024]{1,0:T(8,128)(2,1)S(1)}, u32[]{:S(2)}, u32[]{:S(2)}) collective-permute-start(bf16[448,1024]{1,0:T(8,128)(2,1)S(1)} %collective-permute-done.11.refs_2_), channel_id=1, source_target_pairs={{0,1},{1,0},{2,3},{3,2},{4,5},{5,4},{6,7},{7,6},{8,9},{9,8},{10,11... | collective-permute-start | bytes 2752520 | tf_op jit(solution)/shard_map/ppermute | solution.py:72
  88.1 6.3 %collective-permute-start.29 = (bf16[32,2048]{1,0:T(8,128)(2,1)S(1)}, bf16[32,2048]{1,0:T(8,128)(2,1)S(1)}, u32[]{:S(2)}, u32[]{:S(2)}) collective-permute-start(bf16[32,2048]{1,0:T(8,128)(2,1)S(1)} %attention.1.t0), channel_id=1, source_target_pairs={{0,96},{1,33},{2,98},{3,35},{4,100},{5,37},{6,102},{7,39},{8,104},... | collective-permute-start | bytes 393224 | tf_op jit(solution)/shard_map/ppermute | solution.py:52
  117.2 11.4 %collective-permute-start.39 = (bf16[8,7168]{1,0:T(8,128)(2,1)S(1)}, bf16[8,7168]{1,0:T(8,128)(2,1)S(1)}, u32[]{:S(2)}, u32[]{:S(2)}) collective-permute-start(bf16[8,7168]{1,0:T(8,128)(2,1)S(1)} %join_columns.1.refs_0_), channel_id=1, source_target_pairs={{0,6},{1,3},{2,0},{3,5},{4,2},{5,7},{6,4},{7,1},{8,14},{9,11},{10,... | collective-permute-start | bytes 344072 | tf_op jit(solution)/shard_map/ppermute | solution.py:52
  119.0 10.1 %collective-permute-start.40 = (bf16[8,7168]{1,0:T(8,128)(2,1)S(1)}, bf16[8,7168]{1,0:T(8,128)(2,1)S(1)}, u32[]{:S(2)}, u32[]{:S(2)}) collective-permute-start(bf16[8,7168]{1,0:T(8,128)(2,1)S(1)} %collective-permute-done.38.refs_1_), channel_id=1, source_target_pairs={{0,2},{1,7},{2,4},{3,1},{4,6},{5,3},{6,0},{7,5},{8,10},{9,15},{10,... | collective-permute-start | bytes 344072 | tf_op jit(solution)/shard_map/ppermute | solution.py:52
  122.0 12.6 %collective-permute-start.41 = (bf16[8,7168]{1,0:T(8,128)(2,1)S(1)}, bf16[8,7168]{1,0:T(8,128)(2,1)S(1)}, u32[]{:S(2)}, u32[]{:S(2)}) collective-permute-start(bf16[8,7168]{1,0:T(8,128)(2,1)S(1)} %join_columns.1.refs_0_), channel_id=1, source_target_pairs={{0,1},{1,0},{2,3},{3,2},{4,5},{5,4},{6,7},{7,6},{8,9},{9,8},{10,11... | collective-permute-start | bytes 344072 | tf_op jit(solution)/shard_map/ppermute | solution.py:72
  129.1 6.4 %collective-permute-start.44 = (bf16[8,7168]{1,0:T(8,128)(2,1)S(1)}, bf16[8,7168]{1,0:T(8,128)(2,1)S(1)}, u32[]{:S(2)}, u32[]{:S(2)}) collective-permute-start(bf16[8,7168]{1,0:T(8,128)(2,1)S(1)} %collective-permute-done.40.refs_3_), channel_id=1, source_target_pairs={{0,1},{1,0},{2,3},{3,2},{4,5},{5,4},{6,7},{7,6},{8,9},{9,8},{10,11... | collective-permute-start | bytes 344072 | tf_op jit(solution)/shard_map/ppermute | solution.py:72
  (28 other events, 446.2 us)
